TPU v7x, 512 devices: a whole 4x4x16 slice. The times are simulated.
512 devices in a mesh: rel: 32 (over z, core), ent: 16 (over x, y).
Axes of the slice: x: 4, y: 4, z: 16, core: 2. Of those that a mesh axis runs over, the one named last changes fastest.
Arguments:
- anchors: bfloat16 [262144, 400], P(('rel', 'ent')), may hold values from -6 to 6
- rel_ids: int32 [262144, 1], P(('rel', 'ent')), may hold values from 0 to 511; in each aligned block of 512 rows (0 to 511, 512 to 1023, ...) at most 2 rows name the same one
- query_of: int32 [512, 512], P(('rel', 'ent')), may hold values from 0 to 255, never falling along the last dimension, each value on 1 to 3 neighbouring positions
- answer: int32 [131072], P(('rel', 'ent')), may hold values from 0 to 1023
- cand_ids: int32 [32, 1024], P('rel', 'ent'), may hold values from 0 to 4095, as said below
- ent_table: bfloat16 [4096, 400], P('ent'), may hold values from -6 to 6
- w_in: bfloat16 [512, 400, 1600], P(('rel', 'ent')), may hold values from -0.3125 to 0.3125
- w_out: bfloat16 [512, 1600, 400], P(('rel', 'ent')), may hold values from -0.15625 to 0.15625
- att_weight: bfloat16 [400, 400], replicated, may hold values from -0.3125 to 0.3125
Outputs:
- query_loss: float32 [131072], P(('rel', 'ent'))
- cand_grad: float32 [32, 1024, 400], P('rel', 'ent')
- w_in_grad: bfloat16 [512, 400, 1600], P(('rel', 'ent'))
Inputs may be any that keep to these rules, and one draw needn't show every extreme that they name: `rel_ids`: among the branches of one device no relation occurs more than 2 times. `query_of`: A query's branches stand next to each other on its device; every query has 1 to 3 branches. `cand_ids`: for every group, ids b * 64 to (b + 1) * 64 - 1 of its list lie in table rows b * 256 to (b + 1) * 256 - 1.
All inputs are finite; a program needn't handle non-finite values.
Results may differ from a plain program's by a relative error of at most 0.017.
Values may be sent and summed in bfloat16 or wider, within the bound.
No kernel may reach another device: no remote copies, remote signals or barrier semaphores. Data moves between devices by JAX's collectives and lax.ppermute only.
A program may use at most 64 MiB of HBM per device.

v0:
```python
import jax
import jax.numpy as jnp
from jax import lax
from jax.experimental import pallas as pl
from jax.experimental.pallas import tpu as pltpu
from jax.sharding import PartitionSpec as P

GELU_C = 0.7978845608
GELU_K = 0.044715
ATT_GAIN = 3.0
BOTH = ("rel", "ent")
F32 = jnp.float32
BF16 = jnp.bfloat16
VMEM_LIMIT = 56 * 1024 * 1024


def iota(shape, dim):
    return lax.broadcasted_iota(jnp.int32, shape, dim)


def mm(lhs, rhs, lhs_dim=1, rhs_dim=0):
    return lax.dot_general(
        lhs, rhs, (((lhs_dim,), (rhs_dim,)), ((), ())), preferred_element_type=F32
    )


def split(value):
    high = value.astype(BF16)
    return high, (value - high.astype(F32)).astype(BF16)


def call(kernel, outs, flops, moved, **more):
    return pl.pallas_call(
        kernel,
        out_shape=[jax.ShapeDtypeStruct(shape, dtype) for shape, dtype in outs],
        compiler_params=pltpu.CompilerParams(vmem_limit_bytes=VMEM_LIMIT),
        cost_estimate=pl.CostEstimate(flops=flops, bytes_accessed=moved, transcendentals=0),
        **more,
    )


def pack_kernel(rel_row, rel_col, anchors_t, packed, place):
    count = rel_row.shape[1]
    row = rel_row[...]
    same = (rel_col[...] == row) & (iota((count, count), 0) < iota((count, count), 1))
    rank = jnp.sum(jnp.where(same, 1.0, 0.0), axis=0, keepdims=True).astype(jnp.int32)
    slot = row * 2 + rank
    rows = packed.shape[0]
    step = 256
    for start in range(0, rows, step):
        hot = jnp.where(iota((step, count), 0) + start == slot, 1.0, 0.0).astype(BF16)
        place[start : start + step, :] = hot
        packed[start : start + step, :] = mm(hot, anchors_t[...], 1, 1).astype(BF16)


def maps_kernel(rel_row, rel_col, query_row, query_col, place_t, same_query, first, expand):
    count = rel_row.shape[1]
    queries = first.shape[0]
    col = rel_col[...]
    same = (col == rel_row[...]) & (iota((count, count), 1) < iota((count, count), 0))
    rank = jnp.sum(jnp.where(same, 1.0, 0.0), axis=1, keepdims=True).astype(jnp.int32)
    slot = col * 2 + rank
    place_t[...] = jnp.where(iota(place_t.shape, 1) == slot, 1.0, 0.0).astype(BF16)
    q_row = query_row[...]
    q_col = query_col[...]
    together = q_row == q_col
    same_query[...] = jnp.where(together, 1.0, 0.0).astype(BF16)
    earlier = together & (iota((count, count), 0) < iota((count, count), 1))
    before = jnp.sum(jnp.where(earlier, 1.0, 0.0), axis=0, keepdims=True)
    leading = jnp.where(before == 0.0, q_row, -1)
    first[...] = jnp.where(iota((queries, count), 0) == leading, 1.0, 0.0).astype(BF16)
    expand[...] = jnp.where(iota((count, queries), 1) == q_col, 1.0, 0.0).astype(BF16)


def gelu(pre):
    tangent = jnp.tanh(GELU_C * (pre + GELU_K * pre * pre * pre))
    return 0.5 * pre * (1.0 + tangent)


def gelu_slope(pre):
    square = pre * pre
    tangent = jnp.tanh(GELU_C * (pre + GELU_K * pre * square))
    return 0.5 * (1.0 + tangent) + 0.5 * pre * (1.0 - tangent * tangent) * GELU_C * (
        1.0 + 3.0 * GELU_K * square
    )


def forward_kernel(inputs, w_in, w_out_t, moved):
    rows = inputs[...]
    hidden = gelu(mm(rows, w_in[...])).astype(BF16)
    moved[...] = (rows.astype(F32) + mm(hidden, w_out_t[...], 1, 1)).astype(BF16)


def slope_kernel(inputs, w_in, slope):
    slope[...] = gelu_slope(mm(inputs[...], w_in[...])).astype(BF16)


def middle_kernel(
    returned,
    place_t,
    place,
    same_query,
    first,
    expand,
    att_weight,
    cands,
    answer,
    outgoing,
    coef_t,
    query_b,
    loss,
):
    width = returned.shape[1]
    scale = width ** (-0.5)
    projected = mm(place_t[...], returned[...])
    att_tanh = jnp.tanh(mm(projected.astype(BF16), att_weight[...]))
    att_exp = jnp.exp(ATT_GAIN * att_tanh)
    exp_hi, exp_lo = split(att_exp)
    both_hi, both_lo = split(att_exp * projected)
    group = same_query[...]
    inverse = 1.0 / (mm(group, exp_hi) + mm(group, exp_lo))
    query_each = (mm(group, both_hi) + mm(group, both_lo)) * inverse
    share = att_exp * inverse
    queries = mm(first[...], query_each.astype(BF16)).astype(BF16)
    query_b[...] = queries
    candidates = cands[:, :width]
    scores = mm(candidates, queries, 1, 1) * scale
    is_answer = iota(scores.shape, 0) == answer[...]
    signed = jnp.where(is_answer, -scores, scores)
    weight = jnp.where(is_answer, 1.0, 1.0 / (scores.shape[0] - 1))
    small = jnp.exp(-jnp.abs(signed))
    softplus = jnp.maximum(signed, 0.0) + jnp.log1p(small)
    loss[...] = jnp.sum(softplus * weight, axis=0, keepdims=True)
    sigmoid = jnp.where(signed >= 0.0, 1.0, small) / (1.0 + small) * weight
    coefficient = jnp.where(is_answer, -sigmoid, sigmoid).astype(BF16)
    coef_t[...] = coefficient
    grad_hi, grad_lo = split(mm(coefficient, candidates, 0, 0) * scale)
    spread = expand[...]
    grad_each = (mm(spread, grad_hi) + mm(spread, grad_lo)) * share
    pre_grad = grad_each * (projected - query_each) * ATT_GAIN * (1.0 - att_tanh * att_tanh)
    proj_grad = grad_each + mm(pre_grad.astype(BF16), att_weight[...], 1, 1)
    outgoing[...] = mm(place[...], proj_grad.astype(BF16)).astype(BF16)


def backward_kernel(incoming, inputs, slope, w_out_t, w_in_grad):
    hidden = w_in_grad.shape[1]
    grads = incoming[...]
    rows = inputs[...]
    step = 512
    for start in range(0, hidden, step):
        stop = min(start + step, hidden)
        part = mm(grads, w_out_t[:, start:stop])
        part = (part * slope[:, start:stop].astype(F32)).astype(BF16)
        w_in_grad[:, start:stop] = mm(rows, part, 0, 0).astype(BF16)


def shards(anchors, rel_ids, query_of, answer, cand_ids, ent_table, w_in, w_out, att_weight):
    owners = lax.axis_size("rel") * lax.axis_size("ent")
    branches, width = anchors.shape
    queries = answer.shape[0]
    slots = 2 * owners
    hidden = w_in.shape[2]
    weight_in = w_in[0]
    weight_out_t = w_out[0].T

    def exchange(rows):
        pairs = rows.reshape(owners, 2, width)
        pairs = lax.all_to_all(pairs, BOTH, split_axis=0, concat_axis=0, tiled=True)
        return pairs.reshape(slots, width)

    rel_row = rel_ids.reshape(1, branches)
    query_col = query_of.reshape(branches, 1)
    packed, place = call(
        pack_kernel,
        [((slots, width), BF16), ((slots, branches), BF16)],
        2 * slots * branches * width,
        4 * slots * branches,
    )(rel_row, rel_ids, anchors.T)
    inputs = exchange(packed)

    local_ids = cand_ids[0] - lax.axis_index("ent") * ent_table.shape[0]
    chosen = (local_ids[:, None] == iota((local_ids.shape[0], ent_table.shape[0]), 1)).astype(BF16)
    picked = jnp.dot(chosen, ent_table, preferred_element_type=F32).astype(BF16)
    picked = jnp.pad(picked, ((0, 0), (0, 512 - width)))
    cands = lax.all_gather(picked, "ent", axis=0, tiled=True)
    negatives = cands.shape[0]

    place_t, same_query, first, expand = call(
        maps_kernel,
        [
            ((branches, slots), BF16),
            ((branches, branches), BF16),
            ((queries, branches), BF16),
            ((branches, queries), BF16),
        ],
        10 * branches * slots,
        4 * branches * slots,
    )(rel_row, rel_ids, query_of, query_col)

    block = 256
    whole = lambda shape: pl.BlockSpec(shape, lambda i: (0, 0))
    rows_of = lambda cols: pl.BlockSpec((block, cols), lambda i: (i, 0))
    (moved,) = call(
        forward_kernel,
        [((slots, width), BF16)],
        4 * slots * width * hidden,
        4 * slots * width + 4 * width * hidden,
        grid=(slots // block,),
        in_specs=[rows_of(width), whole((width, hidden)), whole((width, hidden))],
        out_specs=[rows_of(width)],
    )(inputs, weight_in, weight_out_t)
    returned = exchange(moved)

    (slope,) = call(
        slope_kernel,
        [((slots, hidden), BF16)],
        2 * slots * width * hidden,
        2 * slots * hidden,
        grid=(slots // block,),
        in_specs=[rows_of(width), whole((width, hidden))],
        out_specs=[rows_of(hidden)],
    )(inputs, weight_in)

    outgoing, coef_t, query_b, loss = call(
        middle_kernel,
        [
            ((slots, width), BF16),
            ((negatives, queries), BF16),
            ((queries, width), BF16),
            ((1, queries), F32),
        ],
        4 * branches * slots * width,
        8 * slots * width,
    )(
        returned,
        place_t,
        place,
        same_query,
        first,
        expand,
        att_weight,
        cands,
        answer.reshape(1, queries),
    )
    incoming = exchange(outgoing)

    cand_part = jnp.dot(coef_t, query_b, preferred_element_type=F32) * width ** (-0.5)
    cand_grad = lax.psum_scatter(
        cand_part.astype(BF16), "ent", scatter_dimension=0, tiled=True
    ).astype(F32)

    (w_in_grad,) = call(
        backward_kernel,
        [((width, hidden), BF16)],
        4 * slots * width * hidden,
        4 * slots * hidden,
    )(incoming, inputs, slope, weight_out_t)
    return (loss.reshape(queries), cand_grad[None], w_in_grad[None])


def solution(mesh):
    placed = (
        P(BOTH, None),
        P(BOTH, None),
        P(BOTH, None),
        P(BOTH),
        P("rel", "ent"),
        P("ent", None),
        P(BOTH, None, None),
        P(BOTH, None, None),
        P(),
    )
    return jax.shard_map(
        shards,
        mesh=mesh,
        in_specs=placed,
        out_specs=(P(BOTH), P("rel", "ent", None), P(BOTH, None, None)),
        check_vma=False,
    )
```

profile of v0, /device:TPU:1, one launch (start us, length us, event | category | flops | bytes accessed | tf_op | source)
XLA Modules:
  0.0 324.2 jit_solution(16667995846948520578)
XLA Ops:
  7.2 0.0 copy-start
  7.2 1.6 copy.14.rel_col
  8.8 3.0 shard_map.112
  11.8 1.5 reshape.44
  13.3 81.9 %all_to_all.15 = bf16[512,2,400]{2,1,0:T(2,128)(2,1)S(1)} all-to-all(bf16[512,2,400]{2,1,0:T(2,128)(2,1)S(1)} %reshape.44), channel_id=1, replica_groups=mesh['rel'=32,'ent'=16] {'rel','ent'}, dimensions={0} | all-to-all | bytes 1638400 | tf_op jit(solution)/shard_map/all_to_all | solution.py:168
  95.2 1.7 reshape.45.inputs
  96.9 7.3 %shard_map.113 = bf16[1024,400]{1,0:T(8,128)(2,1)} custom-call(bf16[1024,400]{1,0:T(8,128)(2,1)} %reshape.45.inputs, bf16[400,1600]{1,0:T(8,128)(2,1)} %bitcast.18, bf16[400,1600]{1,0:T(8,128)(2,1)} %bitcast.24), custom_call_target="tpu_custom_call" | custom-call | flops 2621440000 | bytes 4198400 | tf_op jit(solution)/shard_map/pallas_call | solution.py:203
  104.2 0.0 copy-start.4
  104.2 0.0 copy-start.3
  104.2 2.3 reshape.46
  106.5 9.5 %all-to-all-start.1 = ((bf16[512,2,400]{2,1,0:T(2,128)(2,1)}), bf16[512,2,400]{2,1,0:T(2,128)(2,1)S(1)}, u32[]{:S(2)}, u32[]{:S(2)}) async-start(bf16[512,2,400]{2,1,0:T(2,128)(2,1)} %reshape.46), calls=%async_computation.1 | async-start | bytes 2097152 | tf_op jit(solution)/shard_map/all_to_all | solution.py:168
  116.1 0.2 all-gather.2.cloned.1.call-start
  116.3 0.0 copy-done.4
  116.3 0.0 copy-done
  116.4 0.2 convolution_convert_fusion
  116.6 0.6 pad.4
  117.2 0.0 all-gather.2.cloned.1.call-update
  117.2 0.0 copy-done.3
  117.2 0.9 copy.16.query_col
  118.1 2.9 shard_map.114
  121.0 53.0 %all-to-all-done.1 = bf16[512,2,400]{2,1,0:T(2,128)(2,1)S(1)} async-done(((bf16[512,2,400]{2,1,0:T(2,128)(2,1)}), bf16[512,2,400]{2,1,0:T(2,128)(2,1)S(1)}, u32[]{:S(2)}, u32[]{:S(2)}) %all-to-all-start.1) | async-done | bytes 819232 | tf_op jit(solution)/shard_map/all_to_all | solution.py:168
  174.0 1.7 reshape.47.returned
  175.7 4.3 %all-gather.2.cloned.1.call-done.cands = bf16[1024,512]{1,0:T(8,128)(2,1)} async-done(((bf16[64,512]{1,0:T(8,128)(2,1)}), bf16[1024,512]{1,0:T(8,128)(2,1)}) %all-gather.2.cloned.1.call-update) | async-done | bytes 1048592 | tf_op jit(solution)/shard_map/all_gather | solution.py:185
  179.9 9.3 %shard_map.115 = (bf16[1024,400]{1,0:T(8,128)(2,1)}, bf16[1024,256]{1,0:T(8,128)(2,1)}, bf16[256,400]{1,0:T(8,128)(2,1)}, f32[1,256]{1,0:T(1,128)}) custom-call(bf16[1024,400]{1,0:T(8,128)(2,1)} %reshape.47.returned, bf16[512,1024]{1,0:T(8,128)(2,1)} %get-tuple-element.14.place_t, bf16[1024,512]{1,0:T(8,128)(2,1)} %get-tuple-element.15.place, ...), custom_call_target="tpu_custom_call" | custom-call | flops 838860800 | bytes 3276800 | tf_op jit(solution)/shard_map/pallas_call | solution.py:224
  189.2 0.0 copy-start.1
  189.2 0.0 copy-start.2
  189.3 2.4 reshape.51
  191.6 19.8 %all-to-all-start.2 = ((bf16[512,2,400]{2,1,0:T(2,128)(2,1)}), bf16[512,2,400]{2,1,0:T(2,128)(2,1)S(1)}, u32[]{:S(2)}, u32[]{:S(2)}) async-start(bf16[512,2,400]{2,1,0:T(2,128)(2,1)} %reshape.51), calls=%async_computation.3 | async-start | bytes 2097152 | tf_op jit(solution)/shard_map/all_to_all | solution.py:168
  211.4 0.3 reduce-scatter.2.cloned.1.call-start
  211.7 0.0 copy-done.1
  211.7 0.0 copy-done.2
  211.7 1.4 multiply_convert_fusion
  213.1 0.0 reduce-scatter.2.cloned.1.call-update
  213.2 7.5 %shard_map.116.slope = bf16[1024,1600]{1,0:T(8,128)(2,1)} custom-call(bf16[1024,400]{1,0:T(8,128)(2,1)} %reshape.45.inputs, bf16[400,1600]{1,0:T(8,128)(2,1)} %bitcast.19), custom_call_target="tpu_custom_call" | custom-call | flops 1310720000 | bytes 3276800 | tf_op jit(solution)/shard_map/pallas_call | solution.py:214
  220.7 85.6 %reduce-scatter.2.cloned.1.call-done = bf16[64,400]{1,0:T(8,128)(2,1)} async-done(((bf16[1024,400]{1,0:T(8,128)(2,1)}), bf16[64,400]{1,0:T(8,128)(2,1)}) %reduce-scatter.2.cloned.1.call-update) | async-done | bytes 51216 | tf_op jit(solution)/shard_map/reduce_scatter | solution.py:248
  306.2 1.5 bitcast_convert_fusion
  307.7 0.0 all-to-all-done.2
  307.7 1.7 reshape.52.incoming
  309.4 7.9 %shard_map.117 = bf16[400,1600]{1,0:T(8,128)(2,1)} custom-call(bf16[1024,400]{1,0:T(8,128)(2,1)} %reshape.52.incoming, bf16[1024,400]{1,0:T(8,128)(2,1)} %reshape.45.inputs, bf16[1024,1600]{1,0:T(8,128)(2,1)} %shard_map.116.slope, bf16[400,1600]{1,0:T(8,128)(2,1)} %bitcast.25), custom_call_target="tpu_custom_call" | custom-call | flops 2621440000 | bytes 6553600 | tf_op jit(solution)/shard_map/pallas_call | solution.py:252
  (1 shorter events, 0.0 us)
Async XLA Ops:
  7.2 109.2 %copy-start = (bf16[256,400]{0,1:T(8,128)(2,1)S(1)}, bf16[256,400]{0,1:T(8,128)(2,1)}, u32[]{:S(2)}) copy-start(bf16[256,400]{0,1:T(8,128)(2,1)} %param.14) | copy-start | bytes 614404
  104.2 12.1 %copy-start.4 = (s32[1,64]{1,0:T(1,128)S(1)}, s32[1,64]{1,0:T(1,128)}, u32[]{:S(2)}) copy-start(s32[1,64]{1,0:T(1,128)} %param.13) | copy-start | bytes 772
  104.2 13.0 %copy-start.3 = (s32[1,512]{1,0:T(1,128)S(1)}, s32[1,512]{1,0:T(1,128)}, u32[]{:S(2)}) copy-start(s32[1,512]{1,0:T(1,128)} %query_row.1) | copy-start | bytes 6148
  106.5 67.5 %all-to-all-start.1 = ((bf16[512,2,400]{2,1,0:T(2,128)(2,1)}), bf16[512,2,400]{2,1,0:T(2,128)(2,1)S(1)}, u32[]{:S(2)}, u32[]{:S(2)}) async-start(bf16[512,2,400]{2,1,0:T(2,128)(2,1)} %reshape.46), calls=%async_computation.1 | async-start | bytes 2097152 | tf_op jit(solution)/shard_map/all_to_all | solution.py:168
  116.1 63.8 %all-gather.2.cloned.1.call-start = ((), (), s32[]{:S(2)}) async-start(), calls=%async_computation.4 | async-start | bytes 1114112 | tf_op jit(solution)/shard_map/all_gather | solution.py:185
  189.2 22.5 %copy-start.1 = (bf16[1024,256]{1,0:T(8,128)(2,1)S(1)}, bf16[1024,256]{1,0:T(8,128)(2,1)}, u32[]{:S(2)}) copy-start(bf16[1024,256]{1,0:T(8,128)(2,1)} %get-tuple-element.20) | copy-start | bytes 1572868
  189.2 22.5 %copy-start.2 = (bf16[256,400]{1,0:T(8,128)(2,1)S(1)}, bf16[256,400]{1,0:T(8,128)(2,1)}, u32[]{:S(2)}) copy-start(bf16[256,400]{1,0:T(8,128)(2,1)} %get-tuple-element.21) | copy-start | bytes 614404
  191.6 116.1 %all-to-all-start.2 = ((bf16[512,2,400]{2,1,0:T(2,128)(2,1)}), bf16[512,2,400]{2,1,0:T(2,128)(2,1)S(1)}, u32[]{:S(2)}, u32[]{:S(2)}) async-start(bf16[512,2,400]{2,1,0:T(2,128)(2,1)} %reshape.51), calls=%async_computation.3 | async-start | bytes 2097152 | tf_op jit(solution)/shard_map/all_to_all | solution.py:168
  211.4 94.8 %reduce-scatter.2.cloned.1.call-start = ((), (), s32[]{:S(2)}) async-start(), calls=%async_computation.5 | async-start | bytes 1114112 | tf_op jit(solution)/shard_map/reduce_scatter | solution.py:248
Sparse Core Ops, SparseCore 0:
  120.5 59.3 all-gather.1
  216.9 89.2 reduce-scatter.1
where the time goes:
time: 325 us; the launch traced here: 324 us
  waiting for transfers between devices  143 us (44%)
  blocking collectives  81.9 us (25%)
  Pallas kernels  38 us (12%)
  starting transfers between devices  29.8 us (9%)
  local copies, waits for them, and re-layouts  14.3 us (4%)
  between operations  14.1 us (4%)
    reduce_scatter x1, waiting for transfers between devices, shards(): lax.psum_scatter(cand_part.astype(BF16), 'ent', scatter_dimension=0, tile...  85.6 us
    all_to_all x1, blocking collectives, exchange(): pairs = lax.all_to_all(pairs, BOTH, split_axis=0, concat_axis=0, tiled=True)  81.9 us
    all_to_all x2, waiting for transfers between devices, exchange(): pairs = lax.all_to_all(pairs, BOTH, split_axis=0, concat_axis=0, tiled=True)  53 us
    all_to_all x2, starting transfers between devices, exchange(): pairs = lax.all_to_all(pairs, BOTH, split_axis=0, concat_axis=0, tiled=True)  29.3 us
    pallas_call x1, Pallas kernels, shards(): call(middle_kernel, [((slots, width), BF16), ((negatives, queries), BF16)...  9.32 us
    pallas_call x1, Pallas kernels, shards(): call(backward_kernel, [((width, hidden), BF16)], 4 * slots * width * hidd...  7.91 us
    pallas_call x1, Pallas kernels, shards(): call(slope_kernel, [((slots, hidden), BF16)], 2 * slots * width * hidden,...  7.5 us
    pallas_call x1, Pallas kernels, shards(): call(forward_kernel, [((slots, width), BF16)], 4 * slots * width * hidden...  7.34 us
  transfers between devices with their start and end apart: 4, of which 3 were waited for; matrix products, arithmetic and copies ran while one was open for 2% of the time, Pallas kernels for 3%

commit v1 on v0

--- a/solution.py
+++ b/solution.py
@@ -11,7 +11,7 @@
 BOTH = ("rel", "ent")
 F32 = jnp.float32
 BF16 = jnp.bfloat16
-VMEM_LIMIT = 56 * 1024 * 1024
+MIB = 1024 * 1024
 
 
 def iota(shape, dim):
@@ -29,11 +29,11 @@
     return high, (value - high.astype(F32)).astype(BF16)
 
 
-def call(kernel, outs, flops, moved, **more):
+def call(kernel, outs, flops, moved, limit=16, **more):
     return pl.pallas_call(
         kernel,
         out_shape=[jax.ShapeDtypeStruct(shape, dtype) for shape, dtype in outs],
-        compiler_params=pltpu.CompilerParams(vmem_limit_bytes=VMEM_LIMIT),
+        compiler_params=pltpu.CompilerParams(vmem_limit_bytes=limit * MIB),
         cost_estimate=pl.CostEstimate(flops=flops, bytes_accessed=moved, transcendentals=0),
         **more,
     )
@@ -87,12 +87,19 @@
 
 def forward_kernel(inputs, w_in, w_out_t, moved):
     rows = inputs[...]
-    hidden = gelu(mm(rows, w_in[...])).astype(BF16)
-    moved[...] = (rows.astype(F32) + mm(hidden, w_out_t[...], 1, 1)).astype(BF16)
-
-
-def slope_kernel(inputs, w_in, slope):
-    slope[...] = gelu_slope(mm(inputs[...], w_in[...])).astype(BF16)
+    total = rows.astype(F32)
+    hidden = w_in.shape[1]
+    for start in range(0, hidden, 512):
+        stop = min(start + 512, hidden)
+        active = gelu(mm(rows, w_in[:, start:stop])).astype(BF16)
+        total = total + mm(active, w_out_t[:, start:stop], 1, 1)
+    moved[...] = total.astype(BF16)
+
+
+def slope_kernel(inputs, w_in, slope, inputs_t):
+    rows = inputs[...]
+    slope[...] = gelu_slope(mm(rows, w_in[...])).astype(BF16)
+    inputs_t[...] = rows.T
 
 
 def middle_kernel(
@@ -142,16 +149,33 @@
     outgoing[...] = mm(place[...], proj_grad.astype(BF16)).astype(BF16)
 
 
-def backward_kernel(incoming, inputs, slope, w_out_t, w_in_grad):
+def backward_kernel(incoming, inputs_t, slope, w_out_t, w_in_grad):
     hidden = w_in_grad.shape[1]
     grads = incoming[...]
-    rows = inputs[...]
+    columns = inputs_t[...]
     step = 512
     for start in range(0, hidden, step):
         stop = min(start + step, hidden)
         part = mm(grads, w_out_t[:, start:stop])
         part = (part * slope[:, start:stop].astype(F32)).astype(BF16)
-        w_in_grad[:, start:stop] = mm(rows, part, 0, 0).astype(BF16)
+        w_in_grad[:, start:stop] = mm(columns, part).astype(BF16)
+
+
+def scatter_sum(part, axis):
+    count = lax.axis_size(axis)
+    me = lax.axis_index(axis)
+    gap = count // 2
+    while gap:
+        half = part.shape[0] // 2
+        low, high = part[:half], part[half:]
+        upper = (me & gap) != 0
+        sent = jnp.where(upper, low, high)
+        kept = jnp.where(upper, high, low)
+        pairs = [(i, i ^ gap) for i in range(count)]
+        got = lax.ppermute(sent.astype(BF16), axis, pairs)
+        part = kept + got.astype(F32)
+        gap //= 2
+    return part
 
 
 def shards(anchors, rel_ids, query_of, answer, cand_ids, ent_table, w_in, w_out, att_weight):
@@ -184,6 +208,7 @@
     picked = jnp.pad(picked, ((0, 0), (0, 512 - width)))
     cands = lax.all_gather(picked, "ent", axis=0, tiled=True)
     negatives = cands.shape[0]
+    inputs, cands = lax.optimization_barrier((inputs, cands))
 
     place_t, same_query, first, expand = call(
         maps_kernel,
@@ -211,14 +236,14 @@
     )(inputs, weight_in, weight_out_t)
     returned = exchange(moved)
 
-    (slope,) = call(
+    slope, inputs_t = call(
         slope_kernel,
-        [((slots, hidden), BF16)],
+        [((slots, hidden), BF16), ((width, slots), BF16)],
         2 * slots * width * hidden,
         2 * slots * hidden,
         grid=(slots // block,),
         in_specs=[rows_of(width), whole((width, hidden))],
-        out_specs=[rows_of(hidden)],
+        out_specs=[rows_of(hidden), pl.BlockSpec((width, block), lambda i: (0, i))],
     )(inputs, weight_in)
 
     outgoing, coef_t, query_b, loss = call(
@@ -245,16 +270,14 @@
     incoming = exchange(outgoing)
 
     cand_part = jnp.dot(coef_t, query_b, preferred_element_type=F32) * width ** (-0.5)
-    cand_grad = lax.psum_scatter(
-        cand_part.astype(BF16), "ent", scatter_dimension=0, tiled=True
-    ).astype(F32)
+    cand_grad = scatter_sum(cand_part, "ent")
 
     (w_in_grad,) = call(
         backward_kernel,
         [((width, hidden), BF16)],
         4 * slots * width * hidden,
         4 * slots * hidden,
-    )(incoming, inputs, slope, weight_out_t)
+    )(incoming, inputs_t, slope, weight_out_t)
     return (loss.reshape(queries), cand_grad[None], w_in_grad[None])
 
 

time: 325 us -> 292 us (0.90)
  blocking collectives: 81.9 us -> 0 us
  starting transfers between devices: 29.8 us -> 76.7 us
  local copies, waits for them, and re-layouts: 14.3 us -> 32.6 us
  Pallas kernels: 38 us -> 24.6 us
  waiting for transfers between devices: 143 us -> 137 us
    reduce_scatter x1 -> x0, waiting for transfers between devices: 85.6 us -> none  [shards(): lax.psum_scatter(cand_part.astype(BF16), 'ent', scatter_dimension=0, tile...]
    all_to_all x1 -> x0, blocking collectives: 81.9 us -> none  [exchange(): pairs = lax.all_to_all(pairs, BOTH, split_axis=0, concat_axis=0, tiled=True)]
    all_to_all x2 -> x3, waiting for transfers between devices: 53 us -> 113 us  [exchange(): pairs = lax.all_to_all(pairs, BOTH, split_axis=0, concat_axis=0, tiled=True)]
    all_to_all x2 -> x3, starting transfers between devices: 29.3 us -> 58.4 us  [exchange(): pairs = lax.all_to_all(pairs, BOTH, split_axis=0, concat_axis=0, tiled=True)]
    unnamed x11 -> x60, local copies, waits for them, and re-layouts: 1.62 us -> 23.3 us
    ppermute x0 -> x4, waiting for transfers between devices: none -> 18.7 us  [scatter_sum(): got = lax.ppermute(sent.astype(BF16), axis, pairs)]
    ppermute x0 -> x4, starting transfers between devices: none -> 18.3 us  [scatter_sum(): got = lax.ppermute(sent.astype(BF16), axis, pairs)]
  transfers between devices with their start and end apart: 4 -> 8, of which waited for: 3 -> 7; matrix products, arithmetic and copies ran while one was open for 2% -> 3% of each run, Pallas kernels for 3% -> 2%
where the time goes in v1:
time: 292 us; the launch traced here: 291 us
  waiting for transfers between devices  137 us (47%)
  starting transfers between devices  76.7 us (26%)
  local copies, waits for them, and re-layouts  32.6 us (11%)
  Pallas kernels  24.6 us (8%)
  between operations  14.4 us (5%)
  other arithmetic  3.44 us (1%)
    all_to_all x3, waiting for transfers between devices, exchange(): pairs = lax.all_to_all(pairs, BOTH, split_axis=0, concat_axis=0, tiled=True)  113 us
    all_to_all x3, starting transfers between devices, exchange(): pairs = lax.all_to_all(pairs, BOTH, split_axis=0, concat_axis=0, tiled=True)  58.4 us
    unnamed x60, local copies, waits for them, and re-layouts  23.3 us
    ppermute x4, waiting for transfers between devices, scatter_sum(): got = lax.ppermute(sent.astype(BF16), axis, pairs)  18.7 us
    ppermute x4, starting transfers between devices, scatter_sum(): got = lax.ppermute(sent.astype(BF16), axis, pairs)  18.3 us
    pallas_call x1, Pallas kernels, shards(): call(forward_kernel, [((slots, width), BF16)], 4 * slots * width * hidden...  6.54 us
    pallas_call x1, Pallas kernels, shards(): call(middle_kernel, [((slots, width), BF16), ((negatives, queries), BF16)...  6.21 us
  transfers between devices with their start and end apart: 8, of which 7 were waited for; matrix products, arithmetic and copies ran while one was open for 3% of the time, Pallas kernels for 2%

profile of v1, /device:TPU:1, one launch (start us, length us, event | category | flops | bytes accessed | tf_op | source)
XLA Modules:
  0.0 290.6 jit_solution(6390378075906347647)
XLA Ops:
  7.2 0.9 copy.15.rel_col
  8.7 1.0 copy-done.25
  9.7 1.0 shard_map.112
  10.7 1.3 reshape.44
  12.0 24.3 %all-to-all-start = ((bf16[512,2,400]{2,1,0:T(2,128)(2,1)}), bf16[512,2,400]{2,1,0:T(2,128)(2,1)S(1)}, u32[]{:S(2)}, u32[]{:S(2)}) async-start(bf16[512,2,400]{2,1,0:T(2,128)(2,1)} %reshape.44), calls=%async_computation | async-start | bytes 2097152 | tf_op jit(solution)/shard_map/all_to_all | solution.py:192
  37.3 56.8 %all-to-all-done = bf16[512,2,400]{2,1,0:T(2,128)(2,1)S(1)} async-done(((bf16[512,2,400]{2,1,0:T(2,128)(2,1)}), bf16[512,2,400]{2,1,0:T(2,128)(2,1)S(1)}, u32[]{:S(2)}, u32[]{:S(2)}) %all-to-all-start) | async-done | bytes 819232 | tf_op jit(solution)/shard_map/all_to_all | solution.py:192
  94.1 0.9 reshape.45.inputs
  95.0 5.0 %all-gather.2.cloned.1.call-done.cands = bf16[1024,512]{1,0:T(8,128)(2,1)} async-done(((bf16[64,512]{1,0:T(8,128)(2,1)}), bf16[1024,512]{1,0:T(8,128)(2,1)}) %all-gather.2.cloned.1.call-update) | async-done | bytes 1048592 | tf_op jit(solution)/shard_map/all_gather | solution.py:209
  100.0 1.3 copy-done.21
  101.4 1.3 copy-done.23
  102.7 6.5 %shard_map.113 = bf16[1024,400]{1,0:T(8,128)(2,1)S(1)} custom-call(bf16[1024,400]{1,0:T(8,128)(2,1)S(1)} %reshape.45.inputs, bf16[400,1600]{1,0:T(8,128)(2,1)S(1)} %bitcast.21, bf16[400,1600]{1,0:T(8,128)(2,1)S(1)} %bitcast.23), custom_call_target="tpu_custom_call" | custom-call | flops 2621440000 | bytes 4198400 | tf_op jit(solution)/shard_map/pallas_call | solution.py:228
  109.3 1.3 reshape.46
  110.5 21.9 %all-to-all-start.1 = ((bf16[512,2,400]{2,1,0:T(2,128)(2,1)}), bf16[512,2,400]{2,1,0:T(2,128)(2,1)}, u32[]{:S(2)}, u32[]{:S(2)}) async-start(bf16[512,2,400]{2,1,0:T(2,128)(2,1)} %reshape.46), calls=%async_computation.1 | async-start | bytes 2097152 | tf_op jit(solution)/shard_map/all_to_all | solution.py:192
  132.6 0.7 shard_map.114
  133.3 1.0 copy-done.4
  134.3 0.8 copy-done.8
  136.5 51.7 %all-to-all-done.1 = bf16[512,2,400]{2,1,0:T(2,128)(2,1)} async-done(((bf16[512,2,400]{2,1,0:T(2,128)(2,1)}), bf16[512,2,400]{2,1,0:T(2,128)(2,1)}, u32[]{:S(2)}, u32[]{:S(2)}) %all-to-all-start.1) | async-done | bytes 819232 | tf_op jit(solution)/shard_map/all_to_all | solution.py:192
  188.2 1.9 reshape.47.returned
  190.1 1.2 copy-done.2
  191.4 1.2 copy-done.3
  192.6 1.2 copy-done.5
  193.8 1.0 copy-done.9
  194.8 1.0 copy-done.10
  195.8 0.9 copy-done.14
  196.8 0.9 copy-done.16
  197.7 6.2 %shard_map.115 = (bf16[1024,400]{1,0:T(8,128)(2,1)S(1)}, bf16[1024,256]{1,0:T(8,128)(2,1)S(1)}, bf16[256,400]{1,0:T(8,128)(2,1)S(1)}, f32[1,256]{1,0:T(1,128)}) custom-call(bf16[1024,400]{1,0:T(8,128)(2,1)S(1)} %reshape.47.returned, bf16[512,1024]{1,0:T(8,128)(2,1)S(1)} %copy-done.5, bf16[1024,512]{1,0:T(8,128)(2,1)S(1)} %copy-done.2, ...), custom_call_target="tpu_custom_call" | custom-call | flops 838860800 | bytes 3276800 | tf_op jit(solution)/shard_map/pallas_call | solution.py:249
  204.0 0.8 copy-done.6
  204.7 0.7 copy-done.11
  205.5 1.3 reshape.51
  206.7 12.2 %all-to-all-start.2 = ((bf16[512,2,400]{2,1,0:T(2,128)(2,1)}), bf16[512,2,400]{2,1,0:T(2,128)(2,1)}, u32[]{:S(2)}, u32[]{:S(2)}) async-start(bf16[512,2,400]{2,1,0:T(2,128)(2,1)} %reshape.51), calls=%async_computation.2 | async-start | bytes 2097152 | tf_op jit(solution)/shard_map/all_to_all | solution.py:192
  218.9 1.6 convolution_multiply_fusion
  220.6 1.5 select_convert_fusion
  222.0 4.8 %collective-permute-start = (bf16[512,400]{0,1:T(8,128)(2,1)S(1)}, bf16[512,400]{0,1:T(8,128)(2,1)S(1)}, u32[]{:S(2)}, u32[]{:S(2)}) collective-permute-start(bf16[512,400]{0,1:T(8,128)(2,1)S(1)} %select_convert_fusion), channel_id=1, source_target_pairs={{0,8},{1,9},{2,10},{3,11},{4,12},{5,13},{6,14},{7,15},{8,0},{9,1},... | collective-permute-start | bytes 1228808 | tf_op jit(solution)/shard_map/ppermute | solution.py:175
  226.9 10.1 %collective-permute-done = bf16[512,400]{0,1:T(8,128)(2,1)S(1)} collective-permute-done((bf16[512,400]{0,1:T(8,128)(2,1)S(1)}, bf16[512,400]{0,1:T(8,128)(2,1)S(1)}, u32[]{:S(2)}, u32[]{:S(2)}) %collective-permute-start) | collective-permute-done | bytes 409632 | tf_op jit(solution)/shard_map/ppermute | solution.py:175
  237.0 1.6 convert_add_fusion
  238.6 5.3 %collective-permute-start.1 = (bf16[256,400]{0,1:T(8,128)(2,1)S(1)}, bf16[256,400]{0,1:T(8,128)(2,1)S(1)}, u32[]{:S(2)}, u32[]{:S(2)}) collective-permute-start(bf16[256,400]{0,1:T(8,128)(2,1)S(1)} %select_convert_fusion.1), channel_id=1, source_target_pairs={{0,4},{1,5},{2,6},{3,7},{4,0},{5,1},{6,2},{7,3},{8,12},{9,13},{10,... | collective-permute-start | bytes 614408 | tf_op jit(solution)/shard_map/ppermute | solution.py:175
  244.0 5.5 %collective-permute-done.1 = bf16[256,400]{0,1:T(8,128)(2,1)S(1)} collective-permute-done((bf16[256,400]{0,1:T(8,128)(2,1)S(1)}, bf16[256,400]{0,1:T(8,128)(2,1)S(1)}, u32[]{:S(2)}, u32[]{:S(2)}) %collective-permute-start.1) | collective-permute-done | bytes 204832 | tf_op jit(solution)/shard_map/ppermute | solution.py:175
  249.6 4.9 %collective-permute-start.2 = (bf16[128,400]{0,1:T(8,128)(2,1)S(1)}, bf16[128,400]{0,1:T(8,128)(2,1)S(1)}, u32[]{:S(2)}, u32[]{:S(2)}) collective-permute-start(bf16[128,400]{0,1:T(8,128)(2,1)S(1)} %select_convert_fusion.3), channel_id=1, source_target_pairs={{0,2},{1,3},{2,0},{3,1},{4,6},{5,7},{6,4},{7,5},{8,10},{9,11},{10,... | collective-permute-start | bytes 307208 | tf_op jit(solution)/shard_map/ppermute | solution.py:175
  254.4 3.1 %collective-permute-done.2 = bf16[128,400]{0,1:T(8,128)(2,1)S(1)} collective-permute-done((bf16[128,400]{0,1:T(8,128)(2,1)S(1)}, bf16[128,400]{0,1:T(8,128)(2,1)S(1)}, u32[]{:S(2)}, u32[]{:S(2)}) %collective-permute-start.2) | collective-permute-done | bytes 102432 | tf_op jit(solution)/shard_map/ppermute | solution.py:175
  257.7 3.2 %collective-permute-start.3 = (bf16[64,400]{0,1:T(8,128)(2,1)S(1)}, bf16[64,400]{0,1:T(8,128)(2,1)S(1)}, u32[]{:S(2)}, u32[]{:S(2)}) collective-permute-start(bf16[64,400]{0,1:T(8,128)(2,1)S(1)} %select_convert_fusion.2), channel_id=1, source_target_pairs={{0,1},{1,0},{2,3},{3,2},{4,5},{5,4},{6,7},{7,6},{8,9},{9,8},{10,11... | collective-permute-start | bytes 153608 | tf_op jit(solution)/shard_map/ppermute | solution.py:175
  260.9 1.3 copy-done.22
  262.2 5.2 %shard_map.116 = (bf16[1024,1600]{1,0:T(8,128)(2,1)S(1)}, bf16[400,1024]{1,0:T(8,128)(2,1)S(1)}) custom-call(bf16[1024,400]{1,0:T(8,128)(2,1)S(1)} %reshape.45.inputs, bf16[400,1600]{1,0:T(8,128)(2,1)S(1)} %bitcast.22), custom_call_target="tpu_custom_call" | custom-call | flops 1310720000 | bytes 3276800 | tf_op jit(solution)/shard_map/pallas_call | solution.py:239
  267.4 1.7 copy-done.26
  269.2 0.8 copy.18
  270.0 4.8 %all-to-all-done.2 = bf16[512,2,400]{2,1,0:T(2,128)(2,1)} async-done(((bf16[512,2,400]{2,1,0:T(2,128)(2,1)}), bf16[512,2,400]{2,1,0:T(2,128)(2,1)}, u32[]{:S(2)}, u32[]{:S(2)}) %all-to-all-start.2) | async-done | bytes 819232 | tf_op jit(solution)/shard_map/all_to_all | solution.py:192
  274.9 1.9 reshape.52.incoming
  276.8 2.0 copy-done.27
  278.8 5.0 %shard_map.117 = bf16[400,1600]{1,0:T(8,128)(2,1)} custom-call(bf16[1024,400]{1,0:T(8,128)(2,1)S(1)} %reshape.52.incoming, bf16[400,1024]{1,0:T(8,128)(2,1)S(1)} %get-tuple-element.29.inputs_t, bf16[1024,1600]{1,0:T(8,128)(2,1)S(1)} %copy-done.27, bf16[400,1600]{1,0:T(8,128)(2,1)S(1)} %bitcast.24), custom_call_target="tpu_custom_call" | custom-call | flops 2621440000 | bytes 6553600 | tf_op jit(solution)/shard_map/pallas_call | solution.py:275
  (54 shorter events, 3.6 us)
Async XLA Ops:
  7.2 29.3 %copy-start = (bf16[256,400]{0,1:T(8,128)(2,1)S(1)}, bf16[256,400]{0,1:T(8,128)(2,1)}, u32[]{:S(2)}) copy-start(bf16[256,400]{0,1:T(8,128)(2,1)} %param.14) | copy-start | bytes 614404
  8.0 0.7 copy-start.17
  8.7 1.0 copy-start.25
  10.7 1.3 copy-start.1
  10.7 25.7 %copy-start.28 = (s32[1,64]{1,0:T(1,128)S(1)}, s32[1,64]{1,0:T(1,128)}, u32[]{:S(2)}) copy-start(s32[1,64]{1,0:T(1,128)} %param.13) | copy-start | bytes 772
  12.0 82.1 %all-to-all-start = ((bf16[512,2,400]{2,1,0:T(2,128)(2,1)}), bf16[512,2,400]{2,1,0:T(2,128)(2,1)S(1)}, u32[]{:S(2)}, u32[]{:S(2)}) async-start(bf16[512,2,400]{2,1,0:T(2,128)(2,1)} %reshape.44), calls=%async_computation | async-start | bytes 2097152 | tf_op jit(solution)/shard_map/all_to_all | solution.py:192
  36.4 63.7 %all-gather.2.cloned.1.call-start = ((), (), s32[]{:S(2)}) async-start(), calls=%async_computation.3 | async-start | bytes 1114112 | tf_op jit(solution)/shard_map/all_gather | solution.py:209
  100.0 1.3 copy-start.21
  101.4 1.3 copy-start.23
  109.2 23.2 %copy-start.19 = (s32[1,512]{1,0:T(1,128)S(1)}, s32[1,512]{1,0:T(1,128)}, u32[]{:S(2)}) copy-start(s32[1,512]{1,0:T(1,128)} %query_row.1) | copy-start | bytes 6148
  110.5 22.1 %copy-start.18 = (s32[512,1]{0,1:T(1,128)S(1)}, s32[512,1]{0,1:T(1,128)}, u32[]{:S(2)}) copy-start(s32[512,1]{0,1:T(1,128)} %param.10) | copy-start | bytes 6148
  110.5 77.7 %all-to-all-start.1 = ((bf16[512,2,400]{2,1,0:T(2,128)(2,1)}), bf16[512,2,400]{2,1,0:T(2,128)(2,1)}, u32[]{:S(2)}, u32[]{:S(2)}) async-start(bf16[512,2,400]{2,1,0:T(2,128)(2,1)} %reshape.46), calls=%async_computation.1 | async-start | bytes 2097152 | tf_op jit(solution)/shard_map/all_to_all | solution.py:192
  132.4 57.7 %copy-start.20 = (s32[256]{0:T(256)S(1)}, s32[256]{0:T(256)}, u32[]{:S(2)}) copy-start(s32[256]{0:T(256)} %param.12) | copy-start | bytes 3076
  133.3 1.0 copy-start.4
  134.3 0.8 copy-start.8
  135.1 0.7 copy-start.13
  135.8 0.7 copy-start.15
  190.1 1.2 copy-start.2
  191.4 1.2 copy-start.3
  192.6 1.2 copy-start.5
  193.8 1.0 copy-start.9
  194.8 1.0 copy-start.10
  195.8 0.9 copy-start.14
  196.8 0.9 copy-start.16
  204.0 0.8 copy-start.6
  204.7 0.7 copy-start.11
  205.5 13.5 %copy-start.7 = (bf16[1024,256]{1,0:T(8,128)(2,1)S(1)}, bf16[1024,256]{1,0:T(8,128)(2,1)}, u32[]{:S(2)}) copy-start(bf16[1024,256]{1,0:T(8,128)(2,1)} %copy-done.6) | copy-start | bytes 1572868
  205.5 13.5 %copy-start.12 = (bf16[256,400]{1,0:T(8,128)(2,1)S(1)}, bf16[256,400]{1,0:T(8,128)(2,1)}, u32[]{:S(2)}) copy-start(bf16[256,400]{1,0:T(8,128)(2,1)} %copy-done.11) | copy-start | bytes 614404
  206.7 68.1 %all-to-all-start.2 = ((bf16[512,2,400]{2,1,0:T(2,128)(2,1)}), bf16[512,2,400]{2,1,0:T(2,128)(2,1)}, u32[]{:S(2)}, u32[]{:S(2)}) async-start(bf16[512,2,400]{2,1,0:T(2,128)(2,1)} %reshape.51), calls=%async_computation.2 | async-start | bytes 2097152 | tf_op jit(solution)/shard_map/all_to_all | solution.py:192
  222.0 14.9 %collective-permute-start = (bf16[512,400]{0,1:T(8,128)(2,1)S(1)}, bf16[512,400]{0,1:T(8,128)(2,1)S(1)}, u32[]{:S(2)}, u32[]{:S(2)}) collective-permute-start(bf16[512,400]{0,1:T(8,128)(2,1)S(1)} %select_convert_fusion), channel_id=1, source_target_pairs={{0,8},{1,9},{2,10},{3,11},{4,12},{5,13},{6,14},{7,15},{8,0},{9,1},... | collective-permute-start | bytes 1228808 | tf_op jit(solution)/shard_map/ppermute | solution.py:175
  238.6 10.8 %collective-permute-start.1 = (bf16[256,400]{0,1:T(8,128)(2,1)S(1)}, bf16[256,400]{0,1:T(8,128)(2,1)S(1)}, u32[]{:S(2)}, u32[]{:S(2)}) collective-permute-start(bf16[256,400]{0,1:T(8,128)(2,1)S(1)} %select_convert_fusion.1), channel_id=1, source_target_pairs={{0,4},{1,5},{2,6},{3,7},{4,0},{5,1},{6,2},{7,3},{8,12},{9,13},{10,... | collective-permute-start | bytes 614408 | tf_op jit(solution)/shard_map/ppermute | solution.py:175
  249.6 8.0 %collective-permute-start.2 = (bf16[128,400]{0,1:T(8,128)(2,1)S(1)}, bf16[128,400]{0,1:T(8,128)(2,1)S(1)}, u32[]{:S(2)}, u32[]{:S(2)}) collective-permute-start(bf16[128,400]{0,1:T(8,128)(2,1)S(1)} %select_convert_fusion.3), channel_id=1, source_target_pairs={{0,2},{1,3},{2,0},{3,1},{4,6},{5,7},{6,4},{7,5},{8,10},{9,11},{10,... | collective-permute-start | bytes 307208 | tf_op jit(solution)/shard_map/ppermute | solution.py:175
  257.7 11.5 %collective-permute-start.3 = (bf16[64,400]{0,1:T(8,128)(2,1)S(1)}, bf16[64,400]{0,1:T(8,128)(2,1)S(1)}, u32[]{:S(2)}, u32[]{:S(2)}) collective-permute-start(bf16[64,400]{0,1:T(8,128)(2,1)S(1)} %select_convert_fusion.2), channel_id=1, source_target_pairs={{0,1},{1,0},{2,3},{3,2},{4,5},{5,4},{6,7},{7,6},{8,9},{9,8},{10,11... | collective-permute-start | bytes 153608 | tf_op jit(solution)/shard_map/ppermute | solution.py:175
  260.9 1.3 copy-start.22
  267.4 1.7 copy-start.26
  269.1 7.7 %copy-start.24 = (bf16[1,1600,400]{1,2,0:T(8,128)(2,1)S(1)}, bf16[1,1600,400]{1,2,0:T(8,128)(2,1)}, u32[]{:S(2)}) copy-start(bf16[1,1600,400]{1,2,0:T(8,128)(2,1)} %param.16) | copy-start | bytes 3840004
  276.8 2.0 copy-start.27
Sparse Core Ops, SparseCore 0:
  40.8 59.2 all-gather.1

commit v2 on v1

--- a/solution.py
+++ b/solution.py
@@ -29,7 +29,7 @@
     return high, (value - high.astype(F32)).astype(BF16)
 
 
-def call(kernel, outs, flops, moved, limit=16, **more):
+def call(kernel, outs, flops, moved, limit=56, **more):
     return pl.pallas_call(
         kernel,
         out_shape=[jax.ShapeDtypeStruct(shape, dtype) for shape, dtype in outs],

time: 292 us -> 290 us (level)
  local copies, waits for them, and re-layouts: 32.6 us -> 16.9 us
  Pallas kernels: 24.6 us -> 39.6 us
  waiting for transfers between devices: 137 us -> 143 us
    unnamed x60 -> x12, local copies, waits for them, and re-layouts: 23.3 us -> 2.39 us
    all_to_all x3, waiting for transfers between devices: 113 us -> 120 us  [exchange(): pairs = lax.all_to_all(pairs, BOTH, split_axis=0, concat_axis=0, tiled=True)]
    reshape x3, local copies, waits for them, and re-layouts: 3.81 us -> 7 us  [exchange(): pairs = rows.reshape(owners, 2, width)]
    pallas_call x1, Pallas kernels: 6.21 us -> 9.28 us  [shards(): call(middle_kernel, [((slots, width), BF16), ((negatives, queries), BF16)...]
  transfers between devices with their start and end apart: 8 -> 8, of which waited for: 7 -> 7; matrix products, arithmetic and copies ran while one was open for 3% -> 2% of each run, Pallas kernels for 2% -> 4%
where the time goes in v2:
time: 290 us
  waiting for transfers between devices  143 us (49%)
  starting transfers between devices  75.3 us (26%)
  Pallas kernels  39.6 us (14%)
  local copies, waits for them, and re-layouts  16.9 us (6%)
  between operations  14.2 us (5%)
    all_to_all x3, waiting for transfers between devices, exchange(): pairs = lax.all_to_all(pairs, BOTH, split_axis=0, concat_axis=0, tiled=True)  120 us
    all_to_all x3, starting transfers between devices, exchange(): pairs = lax.all_to_all(pairs, BOTH, split_axis=0, concat_axis=0, tiled=True)  56.3 us
    ppermute x4, starting transfers between devices, scatter_sum(): got = lax.ppermute(sent.astype(BF16), axis, pairs)  19 us
    ppermute x4, waiting for transfers between devices, scatter_sum(): got = lax.ppermute(sent.astype(BF16), axis, pairs)  17.9 us
    pallas_call x1, Pallas kernels, shards(): call(middle_kernel, [((slots, width), BF16), ((negatives, queries), BF16)...  9.28 us
    pallas_call x1, Pallas kernels, shards(): call(forward_kernel, [((slots, width), BF16)], 4 * slots * width * hidden...  9.01 us
    pallas_call x1, Pallas kernels, shards(): call(backward_kernel, [((width, hidden), BF16)], 4 * slots * width * hidd...  7.85 us
    pallas_call x1, Pallas kernels, shards(): call(slope_kernel, [((slots, hidden), BF16), ((width, slots), BF16)], 2 *...  7.56 us
  transfers between devices with their start and end apart: 8, of which 7 were waited for; matrix products, arithmetic and copies ran while one was open for 2% of the time, Pallas kernels for 4%

profile of v2, /device:TPU:1, one launch (start us, length us, event | category | flops | bytes accessed | tf_op | source)
XLA Modules:
  0.0 289.8 jit_solution(17721644369870050029)
XLA Ops:
  7.2 0.0 copy-start
  7.2 1.6 copy.15.rel_col
  8.8 3.0 %shard_map.112 = (bf16[1024,400]{1,0:T(8,128)(2,1)}, bf16[1024,512]{1,0:T(8,128)(2,1)}) custom-call(s32[1,512]{1,0:T(1,128)} %bitcast.17, s32[512,1]{1,0:T(8,128)} %copy.15.rel_col, bf16[400,512]{1,0:T(8,128)(2,1)} %bitcast.25), custom_call_target="tpu_custom_call" | custom-call | flops 419430400 | bytes 2097152 | tf_op jit(solution)/shard_map/pallas_call | solution.py:197
  11.8 0.0 copy-start.4
  11.8 2.3 reshape.44
  14.1 24.3 %all-to-all-start = ((bf16[512,2,400]{2,1,0:T(2,128)(2,1)}), bf16[512,2,400]{2,1,0:T(2,128)(2,1)S(1)}, u32[]{:S(2)}, u32[]{:S(2)}) async-start(bf16[512,2,400]{2,1,0:T(2,128)(2,1)} %reshape.44), calls=%async_computation | async-start | bytes 2097152 | tf_op jit(solution)/shard_map/all_to_all | solution.py:192
  38.4 0.0 all-gather.2.cloned.1.call-start
  38.5 0.0 copy-done.4
  38.5 0.0 copy-done
  38.5 0.2 convolution_convert_fusion
  38.7 0.6 pad.4
  39.4 0.0 all-gather.2.cloned.1.call-update
  39.4 56.8 %all-to-all-done = bf16[512,2,400]{2,1,0:T(2,128)(2,1)S(1)} async-done(((bf16[512,2,400]{2,1,0:T(2,128)(2,1)}), bf16[512,2,400]{2,1,0:T(2,128)(2,1)S(1)}, u32[]{:S(2)}, u32[]{:S(2)}) %all-to-all-start) | async-done | bytes 819232 | tf_op jit(solution)/shard_map/all_to_all | solution.py:192
  96.2 1.7 reshape.45.inputs
  97.9 4.3 %all-gather.2.cloned.1.call-done.cands = bf16[1024,512]{1,0:T(8,128)(2,1)} async-done(((bf16[64,512]{1,0:T(8,128)(2,1)}), bf16[1024,512]{1,0:T(8,128)(2,1)}) %all-gather.2.cloned.1.call-update) | async-done | bytes 1048592 | tf_op jit(solution)/shard_map/all_gather | solution.py:209
  102.1 9.0 %shard_map.113 = bf16[1024,400]{1,0:T(8,128)(2,1)} custom-call(bf16[1024,400]{1,0:T(8,128)(2,1)} %reshape.45.inputs, bf16[400,1600]{1,0:T(8,128)(2,1)} %bitcast.21, bf16[400,1600]{1,0:T(8,128)(2,1)} %bitcast.23), custom_call_target="tpu_custom_call" | custom-call | flops 2621440000 | bytes 4198400 | tf_op jit(solution)/shard_map/pallas_call | solution.py:228
  111.1 0.0 copy-start.3
  111.1 2.3 reshape.46
  113.4 19.8 %all-to-all-start.1 = ((bf16[512,2,400]{2,1,0:T(2,128)(2,1)}), bf16[512,2,400]{2,1,0:T(2,128)(2,1)S(1)}, u32[]{:S(2)}, u32[]{:S(2)}) async-start(bf16[512,2,400]{2,1,0:T(2,128)(2,1)} %reshape.46), calls=%async_computation.1 | async-start | bytes 2097152 | tf_op jit(solution)/shard_map/all_to_all | solution.py:192
  133.2 0.0 copy-done.3
  133.2 0.8 copy.17.query_col
  134.1 2.8 shard_map.114
  136.9 54.1 %all-to-all-done.1 = bf16[512,2,400]{2,1,0:T(2,128)(2,1)S(1)} async-done(((bf16[512,2,400]{2,1,0:T(2,128)(2,1)}), bf16[512,2,400]{2,1,0:T(2,128)(2,1)S(1)}, u32[]{:S(2)}, u32[]{:S(2)}) %all-to-all-start.1) | async-done | bytes 819232 | tf_op jit(solution)/shard_map/all_to_all | solution.py:192
  191.0 1.6 reshape.47.returned
  192.6 9.3 %shard_map.115 = (bf16[1024,400]{1,0:T(8,128)(2,1)}, bf16[1024,256]{1,0:T(8,128)(2,1)}, bf16[256,400]{1,0:T(8,128)(2,1)}, f32[1,256]{1,0:T(1,128)}) custom-call(bf16[1024,400]{1,0:T(8,128)(2,1)} %reshape.47.returned, bf16[512,1024]{1,0:T(8,128)(2,1)} %get-tuple-element.19.place_t, bf16[1024,512]{1,0:T(8,128)(2,1)} %get-tuple-element.20.place, ...), custom_call_target="tpu_custom_call" | custom-call | flops 838860800 | bytes 3276800 | tf_op jit(solution)/shard_map/pallas_call | solution.py:249
  201.9 2.4 reshape.51
  204.3 12.2 %all-to-all-start.2 = ((bf16[512,2,400]{2,1,0:T(2,128)(2,1)}), bf16[512,2,400]{2,1,0:T(2,128)(2,1)}, u32[]{:S(2)}, u32[]{:S(2)}) async-start(bf16[512,2,400]{2,1,0:T(2,128)(2,1)} %reshape.51), calls=%async_computation.2 | async-start | bytes 2097152 | tf_op jit(solution)/shard_map/all_to_all | solution.py:192
  216.5 0.0 copy-done.1
  216.5 0.0 copy-done.2
  216.5 0.4 convolution_multiply_fusion
  217.0 0.1 select_convert_fusion
  217.0 4.8 %collective-permute-start = (bf16[512,400]{0,1:T(8,128)(2,1)S(1)}, bf16[512,400]{0,1:T(8,128)(2,1)S(1)}, u32[]{:S(2)}, u32[]{:S(2)}) collective-permute-start(bf16[512,400]{0,1:T(8,128)(2,1)S(1)} %select_convert_fusion), channel_id=1, source_target_pairs={{0,8},{1,9},{2,10},{3,11},{4,12},{5,13},{6,14},{7,15},{8,0},{9,1},... | collective-permute-start | bytes 1228808 | tf_op jit(solution)/shard_map/ppermute | solution.py:175
  221.9 9.7 %collective-permute-done = bf16[512,400]{0,1:T(8,128)(2,1)S(1)} collective-permute-done((bf16[512,400]{0,1:T(8,128)(2,1)S(1)}, bf16[512,400]{0,1:T(8,128)(2,1)S(1)}, u32[]{:S(2)}, u32[]{:S(2)}) %collective-permute-start) | collective-permute-done | bytes 409632 | tf_op jit(solution)/shard_map/ppermute | solution.py:175
  231.6 0.2 convert_add_fusion
  231.8 5.6 %collective-permute-start.1 = (bf16[256,400]{0,1:T(8,128)(2,1)S(1)}, bf16[256,400]{0,1:T(8,128)(2,1)S(1)}, u32[]{:S(2)}, u32[]{:S(2)}) collective-permute-start(bf16[256,400]{0,1:T(8,128)(2,1)S(1)} %select_convert_fusion.1), channel_id=1, source_target_pairs={{0,4},{1,5},{2,6},{3,7},{4,0},{5,1},{6,2},{7,3},{8,12},{9,13},{10,... | collective-permute-start | bytes 614408 | tf_op jit(solution)/shard_map/ppermute | solution.py:175
  237.5 5.4 %collective-permute-done.1 = bf16[256,400]{0,1:T(8,128)(2,1)S(1)} collective-permute-done((bf16[256,400]{0,1:T(8,128)(2,1)S(1)}, bf16[256,400]{0,1:T(8,128)(2,1)S(1)}, u32[]{:S(2)}, u32[]{:S(2)}) %collective-permute-start.1) | collective-permute-done | bytes 204832 | tf_op jit(solution)/shard_map/ppermute | solution.py:175
  242.9 0.1 convert_add_fusion.1
  243.0 4.8 %collective-permute-start.2 = (bf16[128,400]{0,1:T(8,128)(2,1)S(1)}, bf16[128,400]{0,1:T(8,128)(2,1)S(1)}, u32[]{:S(2)}, u32[]{:S(2)}) collective-permute-start(bf16[128,400]{0,1:T(8,128)(2,1)S(1)} %select_convert_fusion.3), channel_id=1, source_target_pairs={{0,2},{1,3},{2,0},{3,1},{4,6},{5,7},{6,4},{7,5},{8,10},{9,11},{10,... | collective-permute-start | bytes 307208 | tf_op jit(solution)/shard_map/ppermute | solution.py:175
  247.8 2.8 collective-permute-done.2
  250.6 0.1 select_convert_fusion.2
  250.8 3.7 %collective-permute-start.3 = (bf16[64,400]{0,1:T(8,128)(2,1)S(1)}, bf16[64,400]{0,1:T(8,128)(2,1)S(1)}, u32[]{:S(2)}, u32[]{:S(2)}) collective-permute-start(bf16[64,400]{0,1:T(8,128)(2,1)S(1)} %select_convert_fusion.2), channel_id=1, source_target_pairs={{0,1},{1,0},{2,3},{3,2},{4,5},{5,4},{6,7},{7,6},{8,9},{9,8},{10,11... | collective-permute-start | bytes 153608 | tf_op jit(solution)/shard_map/ppermute | solution.py:175
  254.5 7.6 %shard_map.116 = (bf16[1024,1600]{1,0:T(8,128)(2,1)}, bf16[400,1024]{1,0:T(8,128)(2,1)}) custom-call(bf16[1024,400]{1,0:T(8,128)(2,1)} %reshape.45.inputs, bf16[400,1600]{1,0:T(8,128)(2,1)} %bitcast.22), custom_call_target="tpu_custom_call" | custom-call | flops 1310720000 | bytes 3276800 | tf_op jit(solution)/shard_map/pallas_call | solution.py:239
  262.0 0.0 collective-permute-done.3
  262.0 0.1 add_bitcast_fusion
  262.2 0.8 copy.18
  262.9 9.5 %all-to-all-done.2 = bf16[512,2,400]{2,1,0:T(2,128)(2,1)} async-done(((bf16[512,2,400]{2,1,0:T(2,128)(2,1)}), bf16[512,2,400]{2,1,0:T(2,128)(2,1)}, u32[]{:S(2)}, u32[]{:S(2)}) %all-to-all-start.2) | async-done | bytes 819232 | tf_op jit(solution)/shard_map/all_to_all | solution.py:192
  272.4 2.7 reshape.52.incoming
  275.1 7.8 %shard_map.117 = bf16[400,1600]{1,0:T(8,128)(2,1)} custom-call(bf16[1024,400]{1,0:T(8,128)(2,1)} %reshape.52.incoming, bf16[400,1024]{1,0:T(8,128)(2,1)} %get-tuple-element.29.inputs_t, bf16[1024,1600]{1,0:T(8,128)(2,1)} %get-tuple-element.30.slope, bf16[400,1600]{1,0:T(8,128)(2,1)} %bitcast.24), custom_call_target="tpu_custom_call" | custom-call | flops 2621440000 | bytes 6553600 | tf_op jit(solution)/shard_map/pallas_call | solution.py:275
  (6 shorter events, 0.1 us)
Async XLA Ops:
  7.2 31.4 %copy-start = (bf16[256,400]{0,1:T(8,128)(2,1)S(1)}, bf16[256,400]{0,1:T(8,128)(2,1)}, u32[]{:S(2)}) copy-start(bf16[256,400]{0,1:T(8,128)(2,1)} %param.14) | copy-start | bytes 614404
  11.8 26.7 %copy-start.4 = (s32[1,64]{1,0:T(1,128)S(1)}, s32[1,64]{1,0:T(1,128)}, u32[]{:S(2)}) copy-start(s32[1,64]{1,0:T(1,128)} %param.13) | copy-start | bytes 772
  14.1 82.1 %all-to-all-start = ((bf16[512,2,400]{2,1,0:T(2,128)(2,1)}), bf16[512,2,400]{2,1,0:T(2,128)(2,1)S(1)}, u32[]{:S(2)}, u32[]{:S(2)}) async-start(bf16[512,2,400]{2,1,0:T(2,128)(2,1)} %reshape.44), calls=%async_computation | async-start | bytes 2097152 | tf_op jit(solution)/shard_map/all_to_all | solution.py:192
  38.4 63.7 %all-gather.2.cloned.1.call-start = ((), (), s32[]{:S(2)}) async-start(), calls=%async_computation.3 | async-start | bytes 1114112 | tf_op jit(solution)/shard_map/all_gather | solution.py:209
  111.1 22.1 %copy-start.3 = (s32[1,512]{1,0:T(1,128)S(1)}, s32[1,512]{1,0:T(1,128)}, u32[]{:S(2)}) copy-start(s32[1,512]{1,0:T(1,128)} %query_row.1) | copy-start | bytes 6148
  113.4 77.6 %all-to-all-start.1 = ((bf16[512,2,400]{2,1,0:T(2,128)(2,1)}), bf16[512,2,400]{2,1,0:T(2,128)(2,1)S(1)}, u32[]{:S(2)}, u32[]{:S(2)}) async-start(bf16[512,2,400]{2,1,0:T(2,128)(2,1)} %reshape.46), calls=%async_computation.1 | async-start | bytes 2097152 | tf_op jit(solution)/shard_map/all_to_all | solution.py:192
  201.9 14.6 %copy-start.1 = (bf16[1024,256]{1,0:T(8,128)(2,1)S(1)}, bf16[1024,256]{1,0:T(8,128)(2,1)}, u32[]{:S(2)}) copy-start(bf16[1024,256]{1,0:T(8,128)(2,1)} %get-tuple-element.26) | copy-start | bytes 1572868
  201.9 14.6 %copy-start.2 = (bf16[256,400]{1,0:T(8,128)(2,1)S(1)}, bf16[256,400]{1,0:T(8,128)(2,1)}, u32[]{:S(2)}) copy-start(bf16[256,400]{1,0:T(8,128)(2,1)} %get-tuple-element.27) | copy-start | bytes 614404
  204.3 68.1 %all-to-all-start.2 = ((bf16[512,2,400]{2,1,0:T(2,128)(2,1)}), bf16[512,2,400]{2,1,0:T(2,128)(2,1)}, u32[]{:S(2)}, u32[]{:S(2)}) async-start(bf16[512,2,400]{2,1,0:T(2,128)(2,1)} %reshape.51), calls=%async_computation.2 | async-start | bytes 2097152 | tf_op jit(solution)/shard_map/all_to_all | solution.py:192
  217.0 14.6 %collective-permute-start = (bf16[512,400]{0,1:T(8,128)(2,1)S(1)}, bf16[512,400]{0,1:T(8,128)(2,1)S(1)}, u32[]{:S(2)}, u32[]{:S(2)}) collective-permute-start(bf16[512,400]{0,1:T(8,128)(2,1)S(1)} %select_convert_fusion), channel_id=1, source_target_pairs={{0,8},{1,9},{2,10},{3,11},{4,12},{5,13},{6,14},{7,15},{8,0},{9,1},... | collective-permute-start | bytes 1228808 | tf_op jit(solution)/shard_map/ppermute | solution.py:175
  231.8 11.0 %collective-permute-start.1 = (bf16[256,400]{0,1:T(8,128)(2,1)S(1)}, bf16[256,400]{0,1:T(8,128)(2,1)S(1)}, u32[]{:S(2)}, u32[]{:S(2)}) collective-permute-start(bf16[256,400]{0,1:T(8,128)(2,1)S(1)} %select_convert_fusion.1), channel_id=1, source_target_pairs={{0,4},{1,5},{2,6},{3,7},{4,0},{5,1},{6,2},{7,3},{8,12},{9,13},{10,... | collective-permute-start | bytes 614408 | tf_op jit(solution)/shard_map/ppermute | solution.py:175
  243.0 7.6 %collective-permute-start.2 = (bf16[128,400]{0,1:T(8,128)(2,1)S(1)}, bf16[128,400]{0,1:T(8,128)(2,1)S(1)}, u32[]{:S(2)}, u32[]{:S(2)}) collective-permute-start(bf16[128,400]{0,1:T(8,128)(2,1)S(1)} %select_convert_fusion.3), channel_id=1, source_target_pairs={{0,2},{1,3},{2,0},{3,1},{4,6},{5,7},{6,4},{7,5},{8,10},{9,11},{10,... | collective-permute-start | bytes 307208 | tf_op jit(solution)/shard_map/ppermute | solution.py:175
  250.8 11.3 %collective-permute-start.3 = (bf16[64,400]{0,1:T(8,128)(2,1)S(1)}, bf16[64,400]{0,1:T(8,128)(2,1)S(1)}, u32[]{:S(2)}, u32[]{:S(2)}) collective-permute-start(bf16[64,400]{0,1:T(8,128)(2,1)S(1)} %select_convert_fusion.2), channel_id=1, source_target_pairs={{0,1},{1,0},{2,3},{3,2},{4,5},{5,4},{6,7},{7,6},{8,9},{9,8},{10,11... | collective-permute-start | bytes 153608 | tf_op jit(solution)/shard_map/ppermute | solution.py:175
Sparse Core Ops, SparseCore 0:
  42.9 59.2 all-gather.1

commit v3 on v2

--- a/solution.py
+++ b/solution.py
@@ -37,6 +37,26 @@
         cost_estimate=pl.CostEstimate(flops=flops, bytes_accessed=moved, transcendentals=0),
         **more,
     )
+
+
+def fetch(sources, targets, sems):
+    copies = [
+        pltpu.make_async_copy(source, target, sems.at[number])
+        for number, (source, target) in enumerate(zip(sources, targets))
+    ]
+    for copy in copies:
+        copy.start()
+    return copies
+
+
+FAR = pl.BlockSpec(memory_space=pltpu.HBM)
+NEAR = pl.BlockSpec(memory_space=pltpu.VMEM)
+
+
+def room(arrays):
+    return [pltpu.VMEM(a.shape, a.dtype) for a in arrays] + [
+        pltpu.SemaphoreType.DMA((len(arrays),))
+    ]
 
 
 def pack_kernel(rel_row, rel_col, anchors_t, packed, place):
@@ -87,13 +107,8 @@
 
 def forward_kernel(inputs, w_in, w_out_t, moved):
     rows = inputs[...]
-    total = rows.astype(F32)
-    hidden = w_in.shape[1]
-    for start in range(0, hidden, 512):
-        stop = min(start + 512, hidden)
-        active = gelu(mm(rows, w_in[:, start:stop])).astype(BF16)
-        total = total + mm(active, w_out_t[:, start:stop], 1, 1)
-    moved[...] = total.astype(BF16)
+    hidden = gelu(mm(rows, w_in[...])).astype(BF16)
+    moved[...] = (rows.astype(F32) + mm(hidden, w_out_t[...], 1, 1)).astype(BF16)
 
 
 def slope_kernel(inputs, w_in, slope, inputs_t):
@@ -104,33 +119,51 @@
 
 def middle_kernel(
     returned,
-    place_t,
-    place,
-    same_query,
-    first,
-    expand,
-    att_weight,
-    cands,
     answer,
+    far_place_t,
+    far_weight,
+    far_same,
+    far_first,
+    far_cands,
+    far_expand,
+    far_place,
     outgoing,
     coef_t,
     query_b,
     loss,
+    place_t,
+    att_weight,
+    same_query,
+    first,
+    cands,
+    expand,
+    place,
+    sems,
 ):
+    copies = fetch(
+        (far_place_t, far_weight, far_same, far_first, far_cands, far_expand, far_place),
+        (place_t, att_weight, same_query, first, cands, expand, place),
+        sems,
+    )
     width = returned.shape[1]
     scale = width ** (-0.5)
+    copies[0].wait()
     projected = mm(place_t[...], returned[...])
+    copies[1].wait()
     att_tanh = jnp.tanh(mm(projected.astype(BF16), att_weight[...]))
     att_exp = jnp.exp(ATT_GAIN * att_tanh)
     exp_hi, exp_lo = split(att_exp)
     both_hi, both_lo = split(att_exp * projected)
+    copies[2].wait()
     group = same_query[...]
     inverse = 1.0 / (mm(group, exp_hi) + mm(group, exp_lo))
     query_each = (mm(group, both_hi) + mm(group, both_lo)) * inverse
     share = att_exp * inverse
+    copies[3].wait()
     queries = mm(first[...], query_each.astype(BF16)).astype(BF16)
     query_b[...] = queries
-    candidates = cands[:, :width]
+    copies[4].wait()
+    candidates = cands[...]
     scores = mm(candidates, queries, 1, 1) * scale
     is_answer = iota(scores.shape, 0) == answer[...]
     signed = jnp.where(is_answer, -scores, scores)
@@ -142,23 +175,18 @@
     coefficient = jnp.where(is_answer, -sigmoid, sigmoid).astype(BF16)
     coef_t[...] = coefficient
     grad_hi, grad_lo = split(mm(coefficient, candidates, 0, 0) * scale)
+    copies[5].wait()
     spread = expand[...]
     grad_each = (mm(spread, grad_hi) + mm(spread, grad_lo)) * share
     pre_grad = grad_each * (projected - query_each) * ATT_GAIN * (1.0 - att_tanh * att_tanh)
     proj_grad = grad_each + mm(pre_grad.astype(BF16), att_weight[...], 1, 1)
+    copies[6].wait()
     outgoing[...] = mm(place[...], proj_grad.astype(BF16)).astype(BF16)
 
 
-def backward_kernel(incoming, inputs_t, slope, w_out_t, w_in_grad):
-    hidden = w_in_grad.shape[1]
-    grads = incoming[...]
-    columns = inputs_t[...]
-    step = 512
-    for start in range(0, hidden, step):
-        stop = min(start + step, hidden)
-        part = mm(grads, w_out_t[:, start:stop])
-        part = (part * slope[:, start:stop].astype(F32)).astype(BF16)
-        w_in_grad[:, start:stop] = mm(columns, part).astype(BF16)
+def backward_kernel(incoming, w_out_t, slope, inputs_t, w_in_grad):
+    part = (mm(incoming[...], w_out_t[...]) * slope[...].astype(F32)).astype(BF16)
+    w_in_grad[...] = mm(inputs_t[...], part).astype(BF16)
 
 
 def scatter_sum(part, axis):
@@ -199,13 +227,13 @@
         [((slots, width), BF16), ((slots, branches), BF16)],
         2 * slots * branches * width,
         4 * slots * branches,
+        limit=16,
     )(rel_row, rel_ids, anchors.T)
     inputs = exchange(packed)
 
     local_ids = cand_ids[0] - lax.axis_index("ent") * ent_table.shape[0]
     chosen = (local_ids[:, None] == iota((local_ids.shape[0], ent_table.shape[0]), 1)).astype(BF16)
     picked = jnp.dot(chosen, ent_table, preferred_element_type=F32).astype(BF16)
-    picked = jnp.pad(picked, ((0, 0), (0, 512 - width)))
     cands = lax.all_gather(picked, "ent", axis=0, tiled=True)
     negatives = cands.shape[0]
     inputs, cands = lax.optimization_barrier((inputs, cands))
@@ -223,6 +251,8 @@
     )(rel_row, rel_ids, query_of, query_col)
 
     block = 256
+    half = slots // 2
+    columns = 896
     whole = lambda shape: pl.BlockSpec(shape, lambda i: (0, 0))
     rows_of = lambda cols: pl.BlockSpec((block, cols), lambda i: (i, 0))
     (moved,) = call(
@@ -230,9 +260,13 @@
         [((slots, width), BF16)],
         4 * slots * width * hidden,
         4 * slots * width + 4 * width * hidden,
-        grid=(slots // block,),
-        in_specs=[rows_of(width), whole((width, hidden)), whole((width, hidden))],
-        out_specs=[rows_of(width)],
+        grid=(slots // half,),
+        in_specs=[
+            pl.BlockSpec((half, width), lambda i: (i, 0)),
+            whole((width, hidden)),
+            whole((width, hidden)),
+        ],
+        out_specs=[pl.BlockSpec((half, width), lambda i: (i, 0))],
     )(inputs, weight_in, weight_out_t)
     returned = exchange(moved)
 
@@ -246,6 +280,7 @@
         out_specs=[rows_of(hidden), pl.BlockSpec((width, block), lambda i: (0, i))],
     )(inputs, weight_in)
 
+    far = (place_t, att_weight, same_query, first, cands, expand, place)
     outgoing, coef_t, query_b, loss = call(
         middle_kernel,
         [
@@ -256,17 +291,10 @@
         ],
         4 * branches * slots * width,
         8 * slots * width,
-    )(
-        returned,
-        place_t,
-        place,
-        same_query,
-        first,
-        expand,
-        att_weight,
-        cands,
-        answer.reshape(1, queries),
-    )
+        in_specs=[NEAR, NEAR] + [FAR] * len(far),
+        out_specs=[NEAR] * 4,
+        scratch_shapes=room(far),
+    )(returned, answer.reshape(1, queries), *far)
     incoming = exchange(outgoing)
 
     cand_part = jnp.dot(coef_t, query_b, preferred_element_type=F32) * width ** (-0.5)
@@ -277,7 +305,15 @@
         [((width, hidden), BF16)],
         4 * slots * width * hidden,
         4 * slots * hidden,
-    )(incoming, inputs_t, slope, weight_out_t)
+        grid=(pl.cdiv(hidden, columns),),
+        in_specs=[
+            whole((slots, width)),
+            pl.BlockSpec((width, columns), lambda i: (0, i)),
+            pl.BlockSpec((slots, columns), lambda i: (0, i)),
+            whole((width, slots)),
+        ],
+        out_specs=[pl.BlockSpec((width, columns), lambda i: (0, i))],
+    )(incoming, weight_out_t, slope, inputs_t)
     return (loss.reshape(queries), cand_grad[None], w_in_grad[None])
 
 

time: 290 us -> 260 us (0.90)
  waiting for transfers between devices: 143 us -> 116 us
  blocking collectives: 0 us -> 23.6 us
  between operations: 14.2 us -> 0.9 us
  starting transfers between devices: 75.3 us -> 65 us
  Pallas kernels: 39.6 us -> 35.6 us
    all_gather x0 -> x1, blocking collectives: none -> 23.6 us  [shards(): cands = lax.all_gather(picked, 'ent', axis=0, tiled=True)]
    all_to_all x3, waiting for transfers between devices: 120 us -> 97.6 us  [exchange(): pairs = lax.all_to_all(pairs, BOTH, split_axis=0, concat_axis=0, tiled=True)]
    all_to_all x3, starting transfers between devices: 56.3 us -> 46 us  [exchange(): pairs = lax.all_to_all(pairs, BOTH, split_axis=0, concat_axis=0, tiled=True)]
    all_gather x1 -> x0, waiting for transfers between devices: 4.26 us -> none  [shards(): cands = lax.all_gather(picked, 'ent', axis=0, tiled=True)]
  transfers between devices with their start and end apart: 8 -> 7, of which waited for: 7 -> 6; matrix products, arithmetic and copies ran while one was open for 2% -> 1% of each run, Pallas kernels for 4% -> 4%
where the time goes in v3:
time: 260 us; the launch traced here: 259 us
  waiting for transfers between devices  116 us (45%)
  starting transfers between devices  65 us (25%)
  Pallas kernels  35.6 us (14%)
  blocking collectives  23.6 us (9%)
  local copies, waits for them, and re-layouts  17.1 us (7%)
    all_to_all x3, waiting for transfers between devices, exchange(): pairs = lax.all_to_all(pairs, BOTH, split_axis=0, concat_axis=0, tiled=True)  97.6 us
    all_to_all x3, starting transfers between devices, exchange(): pairs = lax.all_to_all(pairs, BOTH, split_axis=0, concat_axis=0, tiled=True)  46 us
    all_gather x1, blocking collectives, shards(): cands = lax.all_gather(picked, 'ent', axis=0, tiled=True)  23.6 us
    ppermute x4, starting transfers between devices, scatter_sum(): got = lax.ppermute(sent.astype(BF16), axis, pairs)  19 us
    ppermute x4, waiting for transfers between devices, scatter_sum(): got = lax.ppermute(sent.astype(BF16), axis, pairs)  17.9 us
    pallas_call x1, Pallas kernels, shards(): call(middle_kernel, [((slots, width), BF16), ((negatives, queries), BF16)...  10.1 us
    pallas_call x1, Pallas kernels, shards(): call(slope_kernel, [((slots, hidden), BF16), ((width, slots), BF16)], 2 *...  7.55 us
    pallas_call x1, Pallas kernels, shards(): call(backward_kernel, [((width, hidden), BF16)], 4 * slots * width * hidd...  7.28 us
  transfers between devices with their start and end apart: 7, of which 6 were waited for; matrix products, arithmetic and copies ran while one was open for 1% of the time, Pallas kernels for 4%

profile of v3, /device:TPU:1, one launch (start us, length us, event | category | flops | bytes accessed | tf_op | source)
XLA Modules:
  0.0 259.1 jit_solution(1077202637752354114)
XLA Ops:
  0.6 0.0 copy-start
  0.6 0.9 copy.15.rel_col
  1.5 0.0 copy-start.1
  1.5 0.0 copy-start.3
  1.5 0.7 copy-done.3
  2.2 1.0 copy-done.4
  3.2 1.0 shard_map.112
  4.2 0.0 copy-start.2
  4.2 1.0 copy-done.2
  5.2 1.3 reshape.44
  6.4 0.0 copy-done.1
  6.4 24.3 %all-to-all-start = ((bf16[512,2,400]{2,1,0:T(2,128)(2,1)}), bf16[512,2,400]{2,1,0:T(2,128)(2,1)S(1)}, u32[]{:S(2)}, u32[]{:S(2)}) async-start(bf16[512,2,400]{2,1,0:T(2,128)(2,1)} %reshape.44), calls=%async_computation | async-start | bytes 2097152 | tf_op jit(solution)/shard_map/all_to_all | solution.py:220
  30.8 0.0 copy-done.8
  30.8 0.0 copy-done
  30.8 0.2 convolution_convert_fusion
  31.0 23.6 %all_gather.3.far_cands = bf16[1024,400]{1,0:T(8,128)(2,1)} all-gather(bf16[64,400]{1,0:T(8,128)(2,1)S(1)} %convolution_convert_fusion), channel_id=1, replica_groups=mesh['rel'=32,'ent'=16] {'ent'}, dimensions={0}, use_global_device_ids=true | all-gather | bytes 870400 | tf_op jit(solution)/shard_map/all_gather | solution.py:237
  54.6 33.9 %all-to-all-done = bf16[512,2,400]{2,1,0:T(2,128)(2,1)S(1)} async-done(((bf16[512,2,400]{2,1,0:T(2,128)(2,1)}), bf16[512,2,400]{2,1,0:T(2,128)(2,1)S(1)}, u32[]{:S(2)}, u32[]{:S(2)}) %all-to-all-start) | async-done | bytes 819232 | tf_op jit(solution)/shard_map/all_to_all | solution.py:220
  88.5 1.7 reshape.45.inputs
  90.2 6.8 %shard_map.113 = bf16[1024,400]{1,0:T(8,128)(2,1)} custom-call(bf16[1024,400]{1,0:T(8,128)(2,1)} %reshape.45.inputs, bf16[400,1600]{1,0:T(8,128)(2,1)} %bitcast.22, bf16[400,1600]{1,0:T(8,128)(2,1)} %bitcast.24), custom_call_target="tpu_custom_call" | custom-call | flops 2621440000 | bytes 4198400 | tf_op jit(solution)/shard_map/pallas_call | solution.py:258
  97.0 2.3 reshape.46
  99.3 9.5 %all-to-all-start.1 = ((bf16[512,2,400]{2,1,0:T(2,128)(2,1)}), bf16[512,2,400]{2,1,0:T(2,128)(2,1)S(1)}, u32[]{:S(2)}, u32[]{:S(2)}) async-start(bf16[512,2,400]{2,1,0:T(2,128)(2,1)} %reshape.46), calls=%async_computation.1 | async-start | bytes 2097152 | tf_op jit(solution)/shard_map/all_to_all | solution.py:220
  108.9 0.0 copy-done.7
  108.9 0.8 copy.17.query_col
  109.7 2.8 %shard_map.114 = (bf16[512,1024]{1,0:T(8,128)(2,1)}, bf16[512,512]{1,0:T(8,128)(2,1)}, bf16[256,512]{1,0:T(8,128)(2,1)}, bf16[512,256]{1,0:T(8,128)(2,1)}) custom-call(s32[1,512]{1,0:T(1,128)} %bitcast.17, s32[512,1]{1,0:T(8,128)} %copy-done.1, s32[1,512]{1,0:T(1,128)} %query_row.1, s32[512,1]{1,0:T(8,128)} %copy.17.query_col), custom_call_target="tpu_custom_call" | custom-call | flops 5242880 | bytes 2097152 | tf_op jit(solution)/shard_map/pallas_call | solution.py:241
  112.6 54.2 %all-to-all-done.1 = bf16[512,2,400]{2,1,0:T(2,128)(2,1)S(1)} async-done(((bf16[512,2,400]{2,1,0:T(2,128)(2,1)}), bf16[512,2,400]{2,1,0:T(2,128)(2,1)S(1)}, u32[]{:S(2)}, u32[]{:S(2)}) %all-to-all-start.1) | async-done | bytes 819232 | tf_op jit(solution)/shard_map/all_to_all | solution.py:220
  166.8 1.7 reshape.47.returned
  168.4 10.1 %shard_map.115 = (bf16[1024,400]{1,0:T(8,128)(2,1)}, bf16[1024,256]{1,0:T(8,128)(2,1)}, bf16[256,400]{1,0:T(8,128)(2,1)}, f32[1,256]{1,0:T(1,128)}) custom-call(bf16[1024,400]{1,0:T(8,128)(2,1)} %reshape.47.returned, s32[1,256]{1,0:T(1,128)} %bitcast.21, bf16[512,1024]{1,0:T(8,128)(2,1)} %get-tuple-element.19.far_place_t, bf16[400,400]{1,0:T(8,128)(2,1)} %far_weight.1, ...), custom_call_target="tpu_custom_call" | custom-call | flops 838860800 | bytes 3276800 | tf_op jit(solution)/shard_map/pallas_call | solution.py:284
  178.6 2.4 reshape.51
  181.0 12.2 %all-to-all-start.2 = ((bf16[512,2,400]{2,1,0:T(2,128)(2,1)}), bf16[512,2,400]{2,1,0:T(2,128)(2,1)}, u32[]{:S(2)}, u32[]{:S(2)}) async-start(bf16[512,2,400]{2,1,0:T(2,128)(2,1)} %reshape.51), calls=%async_computation.2 | async-start | bytes 2097152 | tf_op jit(solution)/shard_map/all_to_all | solution.py:220
  193.2 0.4 convolution_multiply_fusion
  193.6 0.1 select_convert_fusion
  193.7 4.8 %collective-permute-start = (bf16[512,400]{0,1:T(8,128)(2,1)S(1)}, bf16[512,400]{0,1:T(8,128)(2,1)S(1)}, u32[]{:S(2)}, u32[]{:S(2)}) collective-permute-start(bf16[512,400]{0,1:T(8,128)(2,1)S(1)} %select_convert_fusion), channel_id=1, source_target_pairs={{0,8},{1,9},{2,10},{3,11},{4,12},{5,13},{6,14},{7,15},{8,0},{9,1},... | collective-permute-start | bytes 1228808 | tf_op jit(solution)/shard_map/ppermute | solution.py:203
  198.5 9.7 %collective-permute-done = bf16[512,400]{0,1:T(8,128)(2,1)S(1)} collective-permute-done((bf16[512,400]{0,1:T(8,128)(2,1)S(1)}, bf16[512,400]{0,1:T(8,128)(2,1)S(1)}, u32[]{:S(2)}, u32[]{:S(2)}) %collective-permute-start) | collective-permute-done | bytes 409632 | tf_op jit(solution)/shard_map/ppermute | solution.py:203
  208.3 0.2 convert_add_fusion
  208.5 5.6 %collective-permute-start.1 = (bf16[256,400]{0,1:T(8,128)(2,1)S(1)}, bf16[256,400]{0,1:T(8,128)(2,1)S(1)}, u32[]{:S(2)}, u32[]{:S(2)}) collective-permute-start(bf16[256,400]{0,1:T(8,128)(2,1)S(1)} %select_convert_fusion.1), channel_id=1, source_target_pairs={{0,4},{1,5},{2,6},{3,7},{4,0},{5,1},{6,2},{7,3},{8,12},{9,13},{10,... | collective-permute-start | bytes 614408 | tf_op jit(solution)/shard_map/ppermute | solution.py:203
  214.2 5.4 %collective-permute-done.1 = bf16[256,400]{0,1:T(8,128)(2,1)S(1)} collective-permute-done((bf16[256,400]{0,1:T(8,128)(2,1)S(1)}, bf16[256,400]{0,1:T(8,128)(2,1)S(1)}, u32[]{:S(2)}, u32[]{:S(2)}) %collective-permute-start.1) | collective-permute-done | bytes 204832 | tf_op jit(solution)/shard_map/ppermute | solution.py:203
  219.6 0.1 convert_add_fusion.1
  219.7 4.8 %collective-permute-start.2 = (bf16[128,400]{0,1:T(8,128)(2,1)S(1)}, bf16[128,400]{0,1:T(8,128)(2,1)S(1)}, u32[]{:S(2)}, u32[]{:S(2)}) collective-permute-start(bf16[128,400]{0,1:T(8,128)(2,1)S(1)} %select_convert_fusion.3), channel_id=1, source_target_pairs={{0,2},{1,3},{2,0},{3,1},{4,6},{5,7},{6,4},{7,5},{8,10},{9,11},{10,... | collective-permute-start | bytes 307208 | tf_op jit(solution)/shard_map/ppermute | solution.py:203
  224.5 2.8 %collective-permute-done.2 = bf16[128,400]{0,1:T(8,128)(2,1)S(1)} collective-permute-done((bf16[128,400]{0,1:T(8,128)(2,1)S(1)}, bf16[128,400]{0,1:T(8,128)(2,1)S(1)}, u32[]{:S(2)}, u32[]{:S(2)}) %collective-permute-start.2) | collective-permute-done | bytes 102432 | tf_op jit(solution)/shard_map/ppermute | solution.py:203
  227.3 0.1 select_convert_fusion.2
  227.4 3.7 %collective-permute-start.3 = (bf16[64,400]{0,1:T(8,128)(2,1)S(1)}, bf16[64,400]{0,1:T(8,128)(2,1)S(1)}, u32[]{:S(2)}, u32[]{:S(2)}) collective-permute-start(bf16[64,400]{0,1:T(8,128)(2,1)S(1)} %select_convert_fusion.2), channel_id=1, source_target_pairs={{0,1},{1,0},{2,3},{3,2},{4,5},{5,4},{6,7},{7,6},{8,9},{9,8},{10,11... | collective-permute-start | bytes 153608 | tf_op jit(solution)/shard_map/ppermute | solution.py:203
  231.2 7.6 %shard_map.116 = (bf16[1024,1600]{1,0:T(8,128)(2,1)}, bf16[400,1024]{1,0:T(8,128)(2,1)}) custom-call(bf16[1024,400]{1,0:T(8,128)(2,1)} %reshape.45.inputs, bf16[400,1600]{1,0:T(8,128)(2,1)} %bitcast.23), custom_call_target="tpu_custom_call" | custom-call | flops 1310720000 | bytes 3276800 | tf_op jit(solution)/shard_map/pallas_call | solution.py:273
  238.7 0.0 collective-permute-done.3
  238.7 0.1 add_bitcast_fusion
  238.8 0.8 copy.18
  239.6 9.5 %all-to-all-done.2 = bf16[512,2,400]{2,1,0:T(2,128)(2,1)} async-done(((bf16[512,2,400]{2,1,0:T(2,128)(2,1)}), bf16[512,2,400]{2,1,0:T(2,128)(2,1)}, u32[]{:S(2)}, u32[]{:S(2)}) %all-to-all-start.2) | async-done | bytes 819232 | tf_op jit(solution)/shard_map/all_to_all | solution.py:220
  249.1 2.7 %reshape.52.incoming = bf16[1024,400]{1,0:T(8,128)(2,1)} reshape(bf16[512,2,400]{2,1,0:T(2,128)(2,1)} %all-to-all-done.2) | data formatting | bytes 1638400 | tf_op jit(solution)/shard_map/reshape | solution.py:221
  251.8 7.3 %shard_map.117 = bf16[400,1600]{1,0:T(8,128)(2,1)} custom-call(bf16[1024,400]{1,0:T(8,128)(2,1)} %reshape.52.incoming, bf16[400,1600]{1,0:T(8,128)(2,1)} %bitcast.25, bf16[1024,1600]{1,0:T(8,128)(2,1)} %get-tuple-element.29.slope, bf16[400,1024]{1,0:T(8,128)(2,1)} %get-tuple-element.30.inputs_t), custom_call_target="tpu_custom_call" | custom-call | flops 2621440000 | bytes 6553600 | tf_op jit(solution)/shard_map/pallas_call | solution.py:303
  (11 shorter events, 0.1 us)
Async XLA Ops:
  0.6 30.1 %copy-start = (bf16[256,400]{0,1:T(8,128)(2,1)S(1)}, bf16[256,400]{0,1:T(8,128)(2,1)}, u32[]{:S(2)}) copy-start(bf16[256,400]{0,1:T(8,128)(2,1)} %param.14) | copy-start | bytes 614404
  1.5 4.9 %copy-start.1 = (s32[512,1]{1,0:T(8,128)}, s32[512,1]{1,0:T(8,128)S(1)}, u32[]{:S(2)}) copy-start(s32[512,1]{1,0:T(8,128)S(1)} %copy.15.rel_col) | copy-start | bytes 6148
  1.5 0.7 copy-start.3
  2.2 1.0 copy-start.4
  4.2 1.0 copy-start.2
  5.2 25.6 %copy-start.8 = (s32[1,64]{1,0:T(1,128)S(1)}, s32[1,64]{1,0:T(1,128)}, u32[]{:S(2)}) copy-start(s32[1,64]{1,0:T(1,128)} %param.13) | copy-start | bytes 772
  6.4 82.1 %all-to-all-start = ((bf16[512,2,400]{2,1,0:T(2,128)(2,1)}), bf16[512,2,400]{2,1,0:T(2,128)(2,1)S(1)}, u32[]{:S(2)}, u32[]{:S(2)}) async-start(bf16[512,2,400]{2,1,0:T(2,128)(2,1)} %reshape.44), calls=%async_computation | async-start | bytes 2097152 | tf_op jit(solution)/shard_map/all_to_all | solution.py:220
  97.0 11.9 %copy-start.7 = (s32[1,512]{1,0:T(1,128)S(1)}, s32[1,512]{1,0:T(1,128)}, u32[]{:S(2)}) copy-start(s32[1,512]{1,0:T(1,128)} %query_row.1) | copy-start | bytes 6148
  99.3 67.4 %all-to-all-start.1 = ((bf16[512,2,400]{2,1,0:T(2,128)(2,1)}), bf16[512,2,400]{2,1,0:T(2,128)(2,1)S(1)}, u32[]{:S(2)}, u32[]{:S(2)}) async-start(bf16[512,2,400]{2,1,0:T(2,128)(2,1)} %reshape.46), calls=%async_computation.1 | async-start | bytes 2097152 | tf_op jit(solution)/shard_map/all_to_all | solution.py:220
  178.6 14.6 %copy-start.5 = (bf16[1024,256]{1,0:T(8,128)(2,1)S(1)}, bf16[1024,256]{1,0:T(8,128)(2,1)}, u32[]{:S(2)}) copy-start(bf16[1024,256]{1,0:T(8,128)(2,1)} %get-tuple-element.26) | copy-start | bytes 1572868
  178.6 14.6 %copy-start.6 = (bf16[256,400]{1,0:T(8,128)(2,1)S(1)}, bf16[256,400]{1,0:T(8,128)(2,1)}, u32[]{:S(2)}) copy-start(bf16[256,400]{1,0:T(8,128)(2,1)} %get-tuple-element.27) | copy-start | bytes 614404
  181.0 68.1 %all-to-all-start.2 = ((bf16[512,2,400]{2,1,0:T(2,128)(2,1)}), bf16[512,2,400]{2,1,0:T(2,128)(2,1)}, u32[]{:S(2)}, u32[]{:S(2)}) async-start(bf16[512,2,400]{2,1,0:T(2,128)(2,1)} %reshape.51), calls=%async_computation.2 | async-start | bytes 2097152 | tf_op jit(solution)/shard_map/all_to_all | solution.py:220
  193.7 14.6 %collective-permute-start = (bf16[512,400]{0,1:T(8,128)(2,1)S(1)}, bf16[512,400]{0,1:T(8,128)(2,1)S(1)}, u32[]{:S(2)}, u32[]{:S(2)}) collective-permute-start(bf16[512,400]{0,1:T(8,128)(2,1)S(1)} %select_convert_fusion), channel_id=1, source_target_pairs={{0,8},{1,9},{2,10},{3,11},{4,12},{5,13},{6,14},{7,15},{8,0},{9,1},... | collective-permute-start | bytes 1228808 | tf_op jit(solution)/shard_map/ppermute | solution.py:203
  208.5 11.0 %collective-permute-start.1 = (bf16[256,400]{0,1:T(8,128)(2,1)S(1)}, bf16[256,400]{0,1:T(8,128)(2,1)S(1)}, u32[]{:S(2)}, u32[]{:S(2)}) collective-permute-start(bf16[256,400]{0,1:T(8,128)(2,1)S(1)} %select_convert_fusion.1), channel_id=1, source_target_pairs={{0,4},{1,5},{2,6},{3,7},{4,0},{5,1},{6,2},{7,3},{8,12},{9,13},{10,... | collective-permute-start | bytes 614408 | tf_op jit(solution)/shard_map/ppermute | solution.py:203
  219.7 7.6 %collective-permute-start.2 = (bf16[128,400]{0,1:T(8,128)(2,1)S(1)}, bf16[128,400]{0,1:T(8,128)(2,1)S(1)}, u32[]{:S(2)}, u32[]{:S(2)}) collective-permute-start(bf16[128,400]{0,1:T(8,128)(2,1)S(1)} %select_convert_fusion.3), channel_id=1, source_target_pairs={{0,2},{1,3},{2,0},{3,1},{4,6},{5,7},{6,4},{7,5},{8,10},{9,11},{10,... | collective-permute-start | bytes 307208 | tf_op jit(solution)/shard_map/ppermute | solution.py:203
  227.4 11.3 %collective-permute-start.3 = (bf16[64,400]{0,1:T(8,128)(2,1)S(1)}, bf16[64,400]{0,1:T(8,128)(2,1)S(1)}, u32[]{:S(2)}, u32[]{:S(2)}) collective-permute-start(bf16[64,400]{0,1:T(8,128)(2,1)S(1)} %select_convert_fusion.2), channel_id=1, source_target_pairs={{0,1},{1,0},{2,3},{3,2},{4,5},{5,4},{6,7},{7,6},{8,9},{9,8},{10,11... | collective-permute-start | bytes 153608 | tf_op jit(solution)/shard_map/ppermute | solution.py:203

commit v4 on v3

--- a/solution.py
+++ b/solution.py
@@ -59,7 +59,7 @@
     ]
 
 
-def pack_kernel(rel_row, rel_col, anchors_t, packed, place):
+def pack_kernel(rel_row, rel_col, anchors_t, packed):
     count = rel_row.shape[1]
     row = rel_row[...]
     same = (rel_col[...] == row) & (iota((count, count), 0) < iota((count, count), 1))
@@ -69,24 +69,30 @@
     step = 256
     for start in range(0, rows, step):
         hot = jnp.where(iota((step, count), 0) + start == slot, 1.0, 0.0).astype(BF16)
-        place[start : start + step, :] = hot
         packed[start : start + step, :] = mm(hot, anchors_t[...], 1, 1).astype(BF16)
 
 
-def maps_kernel(rel_row, rel_col, query_row, query_col, place_t, same_query, first, expand):
+def maps_kernel(
+    rel_row, rel_col, query_row, query_col, place, place_t, same_query, first, expand
+):
     count = rel_row.shape[1]
     queries = first.shape[0]
     col = rel_col[...]
-    same = (col == rel_row[...]) & (iota((count, count), 1) < iota((count, count), 0))
-    rank = jnp.sum(jnp.where(same, 1.0, 0.0), axis=1, keepdims=True).astype(jnp.int32)
-    slot = col * 2 + rank
+    row = rel_row[...]
+    below = iota((count, count), 0) < iota((count, count), 1)
+    above = iota((count, count), 0) > iota((count, count), 1)
+    equal = col == row
+    rank = jnp.sum(jnp.where(equal & below, 1.0, 0.0), axis=0, keepdims=True)
+    slot = row * 2 + rank.astype(jnp.int32)
+    place[...] = jnp.where(iota(place.shape, 0) == slot, 1.0, 0.0).astype(BF16)
+    rank = jnp.sum(jnp.where(equal & above, 1.0, 0.0), axis=1, keepdims=True)
+    slot = col * 2 + rank.astype(jnp.int32)
     place_t[...] = jnp.where(iota(place_t.shape, 1) == slot, 1.0, 0.0).astype(BF16)
     q_row = query_row[...]
     q_col = query_col[...]
     together = q_row == q_col
     same_query[...] = jnp.where(together, 1.0, 0.0).astype(BF16)
-    earlier = together & (iota((count, count), 0) < iota((count, count), 1))
-    before = jnp.sum(jnp.where(earlier, 1.0, 0.0), axis=0, keepdims=True)
+    before = jnp.sum(jnp.where(together & below, 1.0, 0.0), axis=0, keepdims=True)
     leading = jnp.where(before == 0.0, q_row, -1)
     first[...] = jnp.where(iota((queries, count), 0) == leading, 1.0, 0.0).astype(BF16)
     expand[...] = jnp.where(iota((count, queries), 1) == q_col, 1.0, 0.0).astype(BF16)
@@ -117,9 +123,17 @@
     inputs_t[...] = rows.T
 
 
+def sigmoid_parts(scores, is_answer, negatives):
+    signed = jnp.where(is_answer, -scores, scores)
+    small = jnp.exp(-jnp.abs(signed))
+    weight = jnp.where(is_answer, -1.0, 1.0 / (negatives - 1))
+    sigmoid = jnp.where(signed >= 0.0, 1.0, small) / (1.0 + small)
+    return signed, small, (sigmoid * weight).astype(BF16)
+
+
 def middle_kernel(
-    returned,
     answer,
+    far_returned,
     far_place_t,
     far_weight,
     far_same,
@@ -128,9 +142,8 @@
     far_expand,
     far_place,
     outgoing,
-    coef_t,
     query_b,
-    loss,
+    returned,
     place_t,
     att_weight,
     same_query,
@@ -141,47 +154,61 @@
     sems,
 ):
     copies = fetch(
-        (far_place_t, far_weight, far_same, far_first, far_cands, far_expand, far_place),
-        (place_t, att_weight, same_query, first, cands, expand, place),
+        (
+            far_returned,
+            far_place_t,
+            far_weight,
+            far_same,
+            far_first,
+            far_cands,
+            far_expand,
+            far_place,
+        ),
+        (returned, place_t, att_weight, same_query, first, cands, expand, place),
         sems,
     )
-    width = returned.shape[1]
-    scale = width ** (-0.5)
+    scale = returned.shape[1] ** (-0.5)
     copies[0].wait()
+    copies[1].wait()
     projected = mm(place_t[...], returned[...])
-    copies[1].wait()
+    copies[2].wait()
     att_tanh = jnp.tanh(mm(projected.astype(BF16), att_weight[...]))
     att_exp = jnp.exp(ATT_GAIN * att_tanh)
     exp_hi, exp_lo = split(att_exp)
     both_hi, both_lo = split(att_exp * projected)
-    copies[2].wait()
+    copies[3].wait()
     group = same_query[...]
     inverse = 1.0 / (mm(group, exp_hi) + mm(group, exp_lo))
     query_each = (mm(group, both_hi) + mm(group, both_lo)) * inverse
     share = att_exp * inverse
-    copies[3].wait()
+    copies[4].wait()
     queries = mm(first[...], query_each.astype(BF16)).astype(BF16)
     query_b[...] = queries
-    copies[4].wait()
-    candidates = cands[...]
-    scores = mm(candidates, queries, 1, 1) * scale
-    is_answer = iota(scores.shape, 0) == answer[...]
-    signed = jnp.where(is_answer, -scores, scores)
-    weight = jnp.where(is_answer, 1.0, 1.0 / (scores.shape[0] - 1))
-    small = jnp.exp(-jnp.abs(signed))
-    softplus = jnp.maximum(signed, 0.0) + jnp.log1p(small)
-    loss[...] = jnp.sum(softplus * weight, axis=0, keepdims=True)
-    sigmoid = jnp.where(signed >= 0.0, 1.0, small) / (1.0 + small) * weight
-    coefficient = jnp.where(is_answer, -sigmoid, sigmoid).astype(BF16)
-    coef_t[...] = coefficient
-    grad_hi, grad_lo = split(mm(coefficient, candidates, 0, 0) * scale)
     copies[5].wait()
+    scores = mm(queries, cands[...], 1, 1) * scale
+    is_answer = iota(scores.shape, 1) == answer[...]
+    _, _, coefficient = sigmoid_parts(scores, is_answer, scores.shape[1])
+    grad_hi, grad_lo = split(mm(coefficient, cands[...]) * scale)
+    copies[6].wait()
     spread = expand[...]
     grad_each = (mm(spread, grad_hi) + mm(spread, grad_lo)) * share
     pre_grad = grad_each * (projected - query_each) * ATT_GAIN * (1.0 - att_tanh * att_tanh)
     proj_grad = grad_each + mm(pre_grad.astype(BF16), att_weight[...], 1, 1)
-    copies[6].wait()
+    copies[7].wait()
     outgoing[...] = mm(place[...], proj_grad.astype(BF16)).astype(BF16)
+
+
+def loss_kernel(cands, query_b, answer, loss, cand_part):
+    negatives, width = cands.shape
+    scale = width ** (-0.5)
+    queries = query_b[...]
+    scores = mm(cands[...], queries, 1, 1) * scale
+    is_answer = iota(scores.shape, 0) == answer[...]
+    signed, small, coefficient = sigmoid_parts(scores, is_answer, negatives)
+    softplus = jnp.maximum(signed, 0.0) + jnp.log1p(small)
+    weight = jnp.where(is_answer, 1.0, 1.0 / (negatives - 1))
+    loss[...] = jnp.sum(softplus * weight, axis=0, keepdims=True)
+    cand_part[...] = mm(coefficient, queries) * scale
 
 
 def backward_kernel(incoming, w_out_t, slope, inputs_t, w_in_grad):
@@ -222,9 +249,9 @@
 
     rel_row = rel_ids.reshape(1, branches)
     query_col = query_of.reshape(branches, 1)
-    packed, place = call(
+    (packed,) = call(
         pack_kernel,
-        [((slots, width), BF16), ((slots, branches), BF16)],
+        [((slots, width), BF16)],
         2 * slots * branches * width,
         4 * slots * branches,
         limit=16,
@@ -238,9 +265,10 @@
     negatives = cands.shape[0]
     inputs, cands = lax.optimization_barrier((inputs, cands))
 
-    place_t, same_query, first, expand = call(
+    place, place_t, same_query, first, expand = call(
         maps_kernel,
         [
+            ((slots, branches), BF16),
             ((branches, slots), BF16),
             ((branches, branches), BF16),
             ((queries, branches), BF16),
@@ -260,6 +288,7 @@
         [((slots, width), BF16)],
         4 * slots * width * hidden,
         4 * slots * width + 4 * width * hidden,
+        limit=51,
         grid=(slots // half,),
         in_specs=[
             pl.BlockSpec((half, width), lambda i: (i, 0)),
@@ -280,24 +309,25 @@
         out_specs=[rows_of(hidden), pl.BlockSpec((width, block), lambda i: (0, i))],
     )(inputs, weight_in)
 
-    far = (place_t, att_weight, same_query, first, cands, expand, place)
-    outgoing, coef_t, query_b, loss = call(
+    returned, slope, inputs_t = lax.optimization_barrier((returned, slope, inputs_t))
+    far = (returned, place_t, att_weight, same_query, first, cands, expand, place)
+    outgoing, query_b = call(
         middle_kernel,
-        [
-            ((slots, width), BF16),
-            ((negatives, queries), BF16),
-            ((queries, width), BF16),
-            ((1, queries), F32),
-        ],
+        [((slots, width), BF16), ((queries, width), BF16)],
         4 * branches * slots * width,
         8 * slots * width,
-        in_specs=[NEAR, NEAR] + [FAR] * len(far),
-        out_specs=[NEAR] * 4,
+        in_specs=[NEAR] + [FAR] * len(far),
+        out_specs=[NEAR] * 2,
         scratch_shapes=room(far),
-    )(returned, answer.reshape(1, queries), *far)
+    )(answer.reshape(queries, 1), *far)
     incoming = exchange(outgoing)
 
-    cand_part = jnp.dot(coef_t, query_b, preferred_element_type=F32) * width ** (-0.5)
+    loss, cand_part = call(
+        loss_kernel,
+        [((1, queries), F32), ((negatives, width), F32)],
+        4 * queries * negatives * width,
+        8 * negatives * width,
+    )(cands, query_b, answer.reshape(1, queries))
     cand_grad = scatter_sum(cand_part, "ent")
 
     (w_in_grad,) = call(

time: 260 us -> 254 us (0.977)
  waiting for transfers between devices: 116 us -> 109 us
  Pallas kernels: 35.6 us -> 39.4 us
  other arithmetic: 0.66 us -> 4.39 us
  local copies, waits for them, and re-layouts: 17.1 us -> 13.4 us
  starting transfers between devices: 65 us -> 61.9 us
    all_to_all x3, waiting for transfers between devices: 97.6 us -> 84.3 us  [exchange(): pairs = lax.all_to_all(pairs, BOTH, split_axis=0, concat_axis=0, tiled=True)]
    ppermute x4, waiting for transfers between devices: 17.9 us -> 24.9 us  [scatter_sum(): got = lax.ppermute(sent.astype(BF16), axis, pairs)]
    pallas_call x3 -> x4, Pallas kernels: 13.9 us -> 18.3 us  [the longest x1 9.14 us: shards(): call(middle_kernel, [((slots, width), BF16), ((queries, width), BF16)], 4...]
    all_to_all x3, starting transfers between devices: 46 us -> 43.4 us  [exchange(): pairs = lax.all_to_all(pairs, BOTH, split_axis=0, concat_axis=0, tiled=True)]
  transfers between devices with their start and end apart: 7 -> 7, of which waited for: 6 -> 7; matrix products, arithmetic and copies ran while one was open for 1% -> 2% of each run, Pallas kernels for 4% -> 6%
where the time goes in v4:
time: 254 us; the launch traced here: 253 us
  waiting for transfers between devices  109 us (43%)
  starting transfers between devices  61.9 us (24%)
  Pallas kernels  39.4 us (16%)
  blocking collectives  23.6 us (9%)
  local copies, waits for them, and re-layouts  13.4 us (5%)
  other arithmetic  4.39 us (2%)
    all_to_all x3, waiting for transfers between devices, exchange(): pairs = lax.all_to_all(pairs, BOTH, split_axis=0, concat_axis=0, tiled=True)  84.3 us
    all_to_all x3, starting transfers between devices, exchange(): pairs = lax.all_to_all(pairs, BOTH, split_axis=0, concat_axis=0, tiled=True)  43.4 us
    ppermute x4, waiting for transfers between devices, scatter_sum(): got = lax.ppermute(sent.astype(BF16), axis, pairs)  24.9 us
    all_gather x1, blocking collectives, shards(): cands = lax.all_gather(picked, 'ent', axis=0, tiled=True)  23.6 us
    ppermute x4, starting transfers between devices, scatter_sum(): got = lax.ppermute(sent.astype(BF16), axis, pairs)  18.5 us
    pallas_call x1, Pallas kernels, shards(): call(middle_kernel, [((slots, width), BF16), ((queries, width), BF16)], 4...  9.14 us
    pallas_call x1, Pallas kernels, shards(): call(slope_kernel, [((slots, hidden), BF16), ((width, slots), BF16)], 2 *...  7.55 us
    pallas_call x1, Pallas kernels, shards(): call(backward_kernel, [((width, hidden), BF16)], 4 * slots * width * hidd...  7.28 us
  transfers between devices with their start and end apart: 7, of which 7 were waited for; matrix products, arithmetic and copies ran while one was open for 2% of the time, Pallas kernels for 6%

profile of v4, /device:TPU:1, one launch (start us, length us, event | category | flops | bytes accessed | tf_op | source)
XLA Modules:
  0.0 253.0 jit_solution(188143042348578711)
XLA Ops:
  0.6 0.0 copy-start
  0.6 0.9 copy.14.rel_col
  1.5 0.0 copy-start.1
  1.5 0.0 copy-start.3
  1.5 1.1 copy-done.3
  2.6 0.7 copy-done.4
  3.3 0.9 shard_map.112
  4.2 0.0 copy-start.7
  4.2 1.3 reshape.47
  5.5 0.0 copy-done.1
  5.5 24.3 %all-to-all-start = ((bf16[512,2,400]{2,1,0:T(2,128)(2,1)}), bf16[512,2,400]{2,1,0:T(2,128)(2,1)S(1)}, u32[]{:S(2)}, u32[]{:S(2)}) async-start(bf16[512,2,400]{2,1,0:T(2,128)(2,1)} %reshape.47), calls=%async_computation | async-start | bytes 2097152 | tf_op jit(solution)/shard_map/all_to_all | solution.py:247
  29.8 0.0 copy-done.7
  29.8 0.0 copy-done
  29.8 0.2 convolution_convert_fusion
  30.0 23.6 %all_gather.3.far_cands.cands = bf16[1024,400]{1,0:T(8,128)(2,1)} all-gather(bf16[64,400]{1,0:T(8,128)(2,1)S(1)} %convolution_convert_fusion), channel_id=1, replica_groups=mesh['rel'=32,'ent'=16] {'ent'}, dimensions={0}, use_global_device_ids=true | all-gather | bytes 870400 | tf_op jit(solution)/shard_map/all_gather | solution.py:264
  53.6 33.9 %all-to-all-done = bf16[512,2,400]{2,1,0:T(2,128)(2,1)S(1)} async-done(((bf16[512,2,400]{2,1,0:T(2,128)(2,1)}), bf16[512,2,400]{2,1,0:T(2,128)(2,1)S(1)}, u32[]{:S(2)}, u32[]{:S(2)}) %all-to-all-start) | async-done | bytes 819232 | tf_op jit(solution)/shard_map/all_to_all | solution.py:247
  87.6 0.9 reshape.48.inputs
  88.4 6.3 %shard_map.113 = bf16[1024,400]{1,0:T(8,128)(2,1)S(1)} custom-call(bf16[1024,400]{1,0:T(8,128)(2,1)S(1)} %reshape.48.inputs, bf16[400,1600]{1,0:T(8,128)(2,1)} %bitcast.22, bf16[400,1600]{1,0:T(8,128)(2,1)} %bitcast.24), custom_call_target="tpu_custom_call" | custom-call | flops 2621440000 | bytes 4198400 | tf_op jit(solution)/shard_map/pallas_call | solution.py:286
  94.7 0.0 copy-start.5
  94.7 0.0 copy-start.6
  94.8 1.3 reshape.50
  96.0 9.5 %all-to-all-start.1 = ((bf16[512,2,400]{2,1,0:T(2,128)(2,1)}), bf16[512,2,400]{2,1,0:T(2,128)(2,1)S(1)}, u32[]{:S(2)}, u32[]{:S(2)}) async-start(bf16[512,2,400]{2,1,0:T(2,128)(2,1)} %reshape.50), calls=%async_computation.1 | async-start | bytes 2097152 | tf_op jit(solution)/shard_map/all_to_all | solution.py:247
  105.6 0.9 copy.16.query_col
  106.5 0.8 copy.17.answer
  107.3 3.6 %shard_map.115 = (bf16[1024,512]{1,0:T(8,128)(2,1)}, bf16[512,1024]{1,0:T(8,128)(2,1)}, bf16[512,512]{1,0:T(8,128)(2,1)}, bf16[256,512]{1,0:T(8,128)(2,1)}, bf16[512,256]{1,0:T(8,128)(2,1)}) custom-call(s32[1,512]{1,0:T(1,128)} %bitcast.17, s32[512,1]{1,0:T(8,128)} %copy-done.1, s32[1,512]{1,0:T(1,128)} %query_row.1, s32[512,1]{1,0:T(8,128)} %copy.16.query_col), custom_call_target="tpu_custom_call" | custom-call | flops 5242880 | bytes 2097152 | tf_op jit(solution)/shard_map/pallas_call | solution.py:268
  111.0 7.5 %shard_map.114 = (bf16[1024,1600]{1,0:T(8,128)(2,1)}, bf16[400,1024]{1,0:T(8,128)(2,1)}) custom-call(bf16[1024,400]{1,0:T(8,128)(2,1)} %copy-done.2, bf16[400,1600]{1,0:T(8,128)(2,1)} %bitcast.23), custom_call_target="tpu_custom_call" | custom-call | flops 1310720000 | bytes 3276800 | tf_op jit(solution)/shard_map/pallas_call | solution.py:302
  118.5 45.0 %all-to-all-done.1 = bf16[512,2,400]{2,1,0:T(2,128)(2,1)S(1)} async-done(((bf16[512,2,400]{2,1,0:T(2,128)(2,1)}), bf16[512,2,400]{2,1,0:T(2,128)(2,1)S(1)}, u32[]{:S(2)}, u32[]{:S(2)}) %all-to-all-start.1) | async-done | bytes 819232 | tf_op jit(solution)/shard_map/all_to_all | solution.py:247
  163.5 1.7 reshape.51.far_returned
  165.1 9.1 %shard_map.116 = (bf16[1024,400]{1,0:T(8,128)(2,1)}, bf16[256,400]{1,0:T(8,128)(2,1)}) custom-call(s32[256,1]{1,0:T(8,128)} %copy.17.answer, bf16[1024,400]{1,0:T(8,128)(2,1)} %reshape.51.far_returned, bf16[512,1024]{1,0:T(8,128)(2,1)} %get-tuple-element.24.far_place_t, bf16[400,400]{1,0:T(8,128)(2,1)} %far_weight.1, ...), custom_call_target="tpu_custom_call" | custom-call | flops 838860800 | bytes 3276800 | tf_op jit(solution)/shard_map/pallas_call | solution.py:314
  174.3 2.3 reshape.55
  176.6 9.5 %all-to-all-start.2 = ((bf16[512,2,400]{2,1,0:T(2,128)(2,1)}), bf16[512,2,400]{2,1,0:T(2,128)(2,1)S(1)}, u32[]{:S(2)}, u32[]{:S(2)}) async-start(bf16[512,2,400]{2,1,0:T(2,128)(2,1)} %reshape.55), calls=%async_computation.2 | async-start | bytes 2097152 | tf_op jit(solution)/shard_map/all_to_all | solution.py:247
  186.1 4.6 %shard_map.117 = (f32[1,256]{1,0:T(1,128)}, f32[1024,400]{1,0:T(8,128)}) custom-call(bf16[1024,400]{1,0:T(8,128)(2,1)} %all_gather.3.far_cands.cands, bf16[256,400]{1,0:T(8,128)(2,1)} %get-tuple-element.29.query_b, s32[1,256]{1,0:T(1,128)} %bitcast.20), custom_call_target="tpu_custom_call" | custom-call | flops 419430400 | bytes 3276800 | tf_op jit(solution)/shard_map/pallas_call | solution.py:325
  190.8 1.6 select_convert_fusion
  192.4 4.8 %collective-permute-start = (bf16[512,400]{1,0:T(8,128)(2,1)S(1)}, bf16[512,400]{1,0:T(8,128)(2,1)S(1)}, u32[]{:S(2)}, u32[]{:S(2)}) collective-permute-start(bf16[512,400]{1,0:T(8,128)(2,1)S(1)} %select_convert_fusion), channel_id=1, source_target_pairs={{0,8},{1,9},{2,10},{3,11},{4,12},{5,13},{6,14},{7,15},{8,0},{9,1},... | collective-permute-start | bytes 1228808 | tf_op jit(solution)/shard_map/ppermute | solution.py:230
  197.2 13.0 %collective-permute-done = bf16[512,400]{1,0:T(8,128)(2,1)S(1)} collective-permute-done((bf16[512,400]{1,0:T(8,128)(2,1)S(1)}, bf16[512,400]{1,0:T(8,128)(2,1)S(1)}, u32[]{:S(2)}, u32[]{:S(2)}) %collective-permute-start) | collective-permute-done | bytes 409632 | tf_op jit(solution)/shard_map/ppermute | solution.py:230
  210.2 1.8 convert_add_fusion
  212.1 0.1 select_convert_fusion.1
  212.1 5.3 %collective-permute-start.1 = (bf16[256,400]{1,0:T(8,128)(2,1)S(1)}, bf16[256,400]{1,0:T(8,128)(2,1)S(1)}, u32[]{:S(2)}, u32[]{:S(2)}) collective-permute-start(bf16[256,400]{1,0:T(8,128)(2,1)S(1)} %select_convert_fusion.1), channel_id=1, source_target_pairs={{0,4},{1,5},{2,6},{3,7},{4,0},{5,1},{6,2},{7,3},{8,12},{9,13},{10,... | collective-permute-start | bytes 614408 | tf_op jit(solution)/shard_map/ppermute | solution.py:230
  217.5 6.9 %collective-permute-done.1 = bf16[256,400]{1,0:T(8,128)(2,1)S(1)} collective-permute-done((bf16[256,400]{1,0:T(8,128)(2,1)S(1)}, bf16[256,400]{1,0:T(8,128)(2,1)S(1)}, u32[]{:S(2)}, u32[]{:S(2)}) %collective-permute-start.1) | collective-permute-done | bytes 204832 | tf_op jit(solution)/shard_map/ppermute | solution.py:230
  224.4 0.1 convert_add_fusion.1
  224.5 4.8 %collective-permute-start.2 = (bf16[128,400]{1,0:T(8,128)(2,1)S(1)}, bf16[128,400]{1,0:T(8,128)(2,1)S(1)}, u32[]{:S(2)}, u32[]{:S(2)}) collective-permute-start(bf16[128,400]{1,0:T(8,128)(2,1)S(1)} %select_convert_fusion.2), channel_id=1, source_target_pairs={{0,2},{1,3},{2,0},{3,1},{4,6},{5,7},{6,4},{7,5},{8,10},{9,11},{10,... | collective-permute-start | bytes 307208 | tf_op jit(solution)/shard_map/ppermute | solution.py:230
  229.3 3.0 %collective-permute-done.2 = bf16[128,400]{1,0:T(8,128)(2,1)S(1)} collective-permute-done((bf16[128,400]{1,0:T(8,128)(2,1)S(1)}, bf16[128,400]{1,0:T(8,128)(2,1)S(1)}, u32[]{:S(2)}, u32[]{:S(2)}) %collective-permute-start.2) | collective-permute-done | bytes 102432 | tf_op jit(solution)/shard_map/ppermute | solution.py:230
  232.4 3.6 %collective-permute-start.3 = (bf16[64,400]{1,0:T(8,128)(2,1)S(1)}, bf16[64,400]{1,0:T(8,128)(2,1)S(1)}, u32[]{:S(2)}, u32[]{:S(2)}) collective-permute-start(bf16[64,400]{1,0:T(8,128)(2,1)S(1)} %select_convert_fusion.3), channel_id=1, source_target_pairs={{0,1},{1,0},{2,3},{3,2},{4,5},{5,4},{6,7},{7,6},{8,9},{9,8},{10,11... | collective-permute-start | bytes 153608 | tf_op jit(solution)/shard_map/ppermute | solution.py:230
  236.0 2.0 collective-permute-done.3
  238.0 0.7 add_bitcast_fusion
  238.7 5.4 %all-to-all-done.2 = bf16[512,2,400]{2,1,0:T(2,128)(2,1)S(1)} async-done(((bf16[512,2,400]{2,1,0:T(2,128)(2,1)}), bf16[512,2,400]{2,1,0:T(2,128)(2,1)S(1)}, u32[]{:S(2)}, u32[]{:S(2)}) %all-to-all-start.2) | async-done | bytes 819232 | tf_op jit(solution)/shard_map/all_to_all | solution.py:247
  244.0 1.7 reshape.56.incoming
  245.7 7.3 %shard_map.118 = bf16[400,1600]{1,0:T(8,128)(2,1)} custom-call(bf16[1024,400]{1,0:T(8,128)(2,1)} %reshape.56.incoming, bf16[400,1600]{1,0:T(8,128)(2,1)} %bitcast.25, bf16[1024,1600]{1,0:T(8,128)(2,1)} %get-tuple-element.33.slope, bf16[400,1024]{1,0:T(8,128)(2,1)} %get-tuple-element.34.inputs_t), custom_call_target="tpu_custom_call" | custom-call | flops 2621440000 | bytes 6553600 | tf_op jit(solution)/shard_map/pallas_call | solution.py:333
  (9 shorter events, 0.1 us)
Async XLA Ops:
  0.6 29.2 %copy-start = (bf16[256,400]{0,1:T(8,128)(2,1)S(1)}, bf16[256,400]{0,1:T(8,128)(2,1)}, u32[]{:S(2)}) copy-start(bf16[256,400]{0,1:T(8,128)(2,1)} %param.14) | copy-start | bytes 614404
  1.5 4.0 %copy-start.1 = (s32[512,1]{1,0:T(8,128)}, s32[512,1]{1,0:T(8,128)S(1)}, u32[]{:S(2)}) copy-start(s32[512,1]{1,0:T(8,128)S(1)} %copy.14.rel_col) | copy-start | bytes 6148
  1.5 1.1 copy-start.3
  2.6 0.7 copy-start.4
  4.2 25.6 %copy-start.7 = (s32[1,64]{1,0:T(1,128)S(1)}, s32[1,64]{1,0:T(1,128)}, u32[]{:S(2)}) copy-start(s32[1,64]{1,0:T(1,128)} %param.13) | copy-start | bytes 772
  5.5 82.1 %all-to-all-start = ((bf16[512,2,400]{2,1,0:T(2,128)(2,1)}), bf16[512,2,400]{2,1,0:T(2,128)(2,1)S(1)}, u32[]{:S(2)}, u32[]{:S(2)}) async-start(bf16[512,2,400]{2,1,0:T(2,128)(2,1)} %reshape.47), calls=%async_computation | async-start | bytes 2097152 | tf_op jit(solution)/shard_map/all_to_all | solution.py:247
  88.4 6.3 %copy-start.2 = (bf16[1024,400]{1,0:T(8,128)(2,1)}, bf16[1024,400]{1,0:T(8,128)(2,1)S(1)}, u32[]{:S(2)}) copy-start(bf16[1024,400]{1,0:T(8,128)(2,1)S(1)} %reshape.48.inputs) | copy-start | bytes 2457604
  94.7 10.9 %copy-start.5 = (s32[1,512]{1,0:T(1,128)S(1)}, s32[1,512]{1,0:T(1,128)}, u32[]{:S(2)}) copy-start(s32[1,512]{1,0:T(1,128)} %query_row.1) | copy-start | bytes 6148
  94.7 11.8 %copy-start.6 = (s32[256]{0:T(256)S(1)}, s32[256]{0:T(256)}, u32[]{:S(2)}) copy-start(s32[256]{0:T(256)} %param.12) | copy-start | bytes 3076
  96.0 67.5 %all-to-all-start.1 = ((bf16[512,2,400]{2,1,0:T(2,128)(2,1)}), bf16[512,2,400]{2,1,0:T(2,128)(2,1)S(1)}, u32[]{:S(2)}, u32[]{:S(2)}) async-start(bf16[512,2,400]{2,1,0:T(2,128)(2,1)} %reshape.50), calls=%async_computation.1 | async-start | bytes 2097152 | tf_op jit(solution)/shard_map/all_to_all | solution.py:247
  176.6 67.5 %all-to-all-start.2 = ((bf16[512,2,400]{2,1,0:T(2,128)(2,1)}), bf16[512,2,400]{2,1,0:T(2,128)(2,1)S(1)}, u32[]{:S(2)}, u32[]{:S(2)}) async-start(bf16[512,2,400]{2,1,0:T(2,128)(2,1)} %reshape.55), calls=%async_computation.2 | async-start | bytes 2097152 | tf_op jit(solution)/shard_map/all_to_all | solution.py:247
  192.4 17.9 %collective-permute-start = (bf16[512,400]{1,0:T(8,128)(2,1)S(1)}, bf16[512,400]{1,0:T(8,128)(2,1)S(1)}, u32[]{:S(2)}, u32[]{:S(2)}) collective-permute-start(bf16[512,400]{1,0:T(8,128)(2,1)S(1)} %select_convert_fusion), channel_id=1, source_target_pairs={{0,8},{1,9},{2,10},{3,11},{4,12},{5,13},{6,14},{7,15},{8,0},{9,1},... | collective-permute-start | bytes 1228808 | tf_op jit(solution)/shard_map/ppermute | solution.py:230
  212.1 12.2 %collective-permute-start.1 = (bf16[256,400]{1,0:T(8,128)(2,1)S(1)}, bf16[256,400]{1,0:T(8,128)(2,1)S(1)}, u32[]{:S(2)}, u32[]{:S(2)}) collective-permute-start(bf16[256,400]{1,0:T(8,128)(2,1)S(1)} %select_convert_fusion.1), channel_id=1, source_target_pairs={{0,4},{1,5},{2,6},{3,7},{4,0},{5,1},{6,2},{7,3},{8,12},{9,13},{10,... | collective-permute-start | bytes 614408 | tf_op jit(solution)/shard_map/ppermute | solution.py:230
  224.5 7.8 %collective-permute-start.2 = (bf16[128,400]{1,0:T(8,128)(2,1)S(1)}, bf16[128,400]{1,0:T(8,128)(2,1)S(1)}, u32[]{:S(2)}, u32[]{:S(2)}) collective-permute-start(bf16[128,400]{1,0:T(8,128)(2,1)S(1)} %select_convert_fusion.2), channel_id=1, source_target_pairs={{0,2},{1,3},{2,0},{3,1},{4,6},{5,7},{6,4},{7,5},{8,10},{9,11},{10,... | collective-permute-start | bytes 307208 | tf_op jit(solution)/shard_map/ppermute | solution.py:230
  232.4 5.6 %collective-permute-start.3 = (bf16[64,400]{1,0:T(8,128)(2,1)S(1)}, bf16[64,400]{1,0:T(8,128)(2,1)S(1)}, u32[]{:S(2)}, u32[]{:S(2)}) collective-permute-start(bf16[64,400]{1,0:T(8,128)(2,1)S(1)} %select_convert_fusion.3), channel_id=1, source_target_pairs={{0,1},{1,0},{2,3},{3,2},{4,5},{5,4},{6,7},{7,6},{8,9},{9,8},{10,11... | collective-permute-start | bytes 153608 | tf_op jit(solution)/shard_map/ppermute | solution.py:230

commit v5 on v4

--- a/solution.py
+++ b/solution.py
@@ -59,17 +59,27 @@
     ]
 
 
-def pack_kernel(rel_row, rel_col, anchors_t, packed):
+def paired(rows):
+    return rows.reshape(rows.shape[0] // 2, 2, rows.shape[1])
+
+
+def unpaired(pairs):
+    return pairs.reshape(pairs.shape[0] * 2, pairs.shape[2])
+
+
+def pack_kernel(rel_row, anchors_t, packed):
     count = rel_row.shape[1]
     row = rel_row[...]
-    same = (rel_col[...] == row) & (iota((count, count), 0) < iota((count, count), 1))
+    col = jnp.broadcast_to(row, (128, count)).T[:, :1]
+    same = (col == row) & (iota((count, count), 0) < iota((count, count), 1))
     rank = jnp.sum(jnp.where(same, 1.0, 0.0), axis=0, keepdims=True).astype(jnp.int32)
     slot = row * 2 + rank
-    rows = packed.shape[0]
+    rows = packed.shape[0] * 2
     step = 256
     for start in range(0, rows, step):
         hot = jnp.where(iota((step, count), 0) + start == slot, 1.0, 0.0).astype(BF16)
-        packed[start : start + step, :] = mm(hot, anchors_t[...], 1, 1).astype(BF16)
+        part = mm(hot, anchors_t[...], 1, 1).astype(BF16)
+        packed[start // 2 : (start + step) // 2] = paired(part)
 
 
 def maps_kernel(
@@ -112,13 +122,13 @@
 
 
 def forward_kernel(inputs, w_in, w_out_t, moved):
-    rows = inputs[...]
+    rows = unpaired(inputs[...])
     hidden = gelu(mm(rows, w_in[...])).astype(BF16)
-    moved[...] = (rows.astype(F32) + mm(hidden, w_out_t[...], 1, 1)).astype(BF16)
+    moved[...] = paired((rows.astype(F32) + mm(hidden, w_out_t[...], 1, 1)).astype(BF16))
 
 
 def slope_kernel(inputs, w_in, slope, inputs_t):
-    rows = inputs[...]
+    rows = unpaired(inputs[...])
     slope[...] = gelu_slope(mm(rows, w_in[...])).astype(BF16)
     inputs_t[...] = rows.T
 
@@ -167,10 +177,10 @@
         (returned, place_t, att_weight, same_query, first, cands, expand, place),
         sems,
     )
-    scale = returned.shape[1] ** (-0.5)
+    scale = returned.shape[2] ** (-0.5)
     copies[0].wait()
     copies[1].wait()
-    projected = mm(place_t[...], returned[...])
+    projected = mm(place_t[...], unpaired(returned[...]))
     copies[2].wait()
     att_tanh = jnp.tanh(mm(projected.astype(BF16), att_weight[...]))
     att_exp = jnp.exp(ATT_GAIN * att_tanh)
@@ -195,7 +205,7 @@
     pre_grad = grad_each * (projected - query_each) * ATT_GAIN * (1.0 - att_tanh * att_tanh)
     proj_grad = grad_each + mm(pre_grad.astype(BF16), att_weight[...], 1, 1)
     copies[7].wait()
-    outgoing[...] = mm(place[...], proj_grad.astype(BF16)).astype(BF16)
+    outgoing[...] = paired(mm(place[...], proj_grad.astype(BF16)).astype(BF16))
 
 
 def loss_kernel(cands, query_b, answer, loss, cand_part):
@@ -212,7 +222,7 @@
 
 
 def backward_kernel(incoming, w_out_t, slope, inputs_t, w_in_grad):
-    part = (mm(incoming[...], w_out_t[...]) * slope[...].astype(F32)).astype(BF16)
+    part = (mm(unpaired(incoming[...]), w_out_t[...]) * slope[...].astype(F32)).astype(BF16)
     w_in_grad[...] = mm(inputs_t[...], part).astype(BF16)
 
 
@@ -242,20 +252,18 @@
     weight_in = w_in[0]
     weight_out_t = w_out[0].T
 
-    def exchange(rows):
-        pairs = rows.reshape(owners, 2, width)
-        pairs = lax.all_to_all(pairs, BOTH, split_axis=0, concat_axis=0, tiled=True)
-        return pairs.reshape(slots, width)
+    def exchange(pairs):
+        return lax.all_to_all(pairs, BOTH, split_axis=0, concat_axis=0, tiled=True)
 
     rel_row = rel_ids.reshape(1, branches)
     query_col = query_of.reshape(branches, 1)
     (packed,) = call(
         pack_kernel,
-        [((slots, width), BF16)],
+        [((owners, 2, width), BF16)],
         2 * slots * branches * width,
         4 * slots * branches,
         limit=16,
-    )(rel_row, rel_ids, anchors.T)
+    )(rel_row, anchors.T)
     inputs = exchange(packed)
 
     local_ids = cand_ids[0] - lax.axis_index("ent") * ent_table.shape[0]
@@ -282,20 +290,21 @@
     half = slots // 2
     columns = 896
     whole = lambda shape: pl.BlockSpec(shape, lambda i: (0, 0))
+    pairs_of = lambda rows: pl.BlockSpec((rows // 2, 2, width), lambda i: (i, 0, 0))
     rows_of = lambda cols: pl.BlockSpec((block, cols), lambda i: (i, 0))
     (moved,) = call(
         forward_kernel,
-        [((slots, width), BF16)],
+        [((owners, 2, width), BF16)],
         4 * slots * width * hidden,
         4 * slots * width + 4 * width * hidden,
         limit=51,
         grid=(slots // half,),
         in_specs=[
-            pl.BlockSpec((half, width), lambda i: (i, 0)),
+            pairs_of(half),
             whole((width, hidden)),
             whole((width, hidden)),
         ],
-        out_specs=[pl.BlockSpec((half, width), lambda i: (i, 0))],
+        out_specs=[pairs_of(half)],
     )(inputs, weight_in, weight_out_t)
     returned = exchange(moved)
 
@@ -305,7 +314,7 @@
         2 * slots * width * hidden,
         2 * slots * hidden,
         grid=(slots // block,),
-        in_specs=[rows_of(width), whole((width, hidden))],
+        in_specs=[pairs_of(block), whole((width, hidden))],
         out_specs=[rows_of(hidden), pl.BlockSpec((width, block), lambda i: (0, i))],
     )(inputs, weight_in)
 
@@ -313,7 +322,7 @@
     far = (returned, place_t, att_weight, same_query, first, cands, expand, place)
     outgoing, query_b = call(
         middle_kernel,
-        [((slots, width), BF16), ((queries, width), BF16)],
+        [((owners, 2, width), BF16), ((queries, width), BF16)],
         4 * branches * slots * width,
         8 * slots * width,
         in_specs=[NEAR] + [FAR] * len(far),
@@ -335,9 +344,10 @@
         [((width, hidden), BF16)],
         4 * slots * width * hidden,
         4 * slots * hidden,
+        limit=52,
         grid=(pl.cdiv(hidden, columns),),
         in_specs=[
-            whole((slots, width)),
+            pl.BlockSpec((owners, 2, width), lambda i: (0, 0, 0)),
             pl.BlockSpec((width, columns), lambda i: (0, i)),
             pl.BlockSpec((slots, columns), lambda i: (0, i)),
             whole((width, slots)),

time: 254 us -> 247 us (0.972)
  local copies, waits for them, and re-layouts: 13.4 us -> 6.09 us
  waiting for transfers between devices: 109 us -> 106 us
    reshape x6 -> x0, local copies, waits for them, and re-layouts: 9.03 us -> none  [the longest x3 4.84 us: exchange(): pairs = rows.reshape(owners, 2, width)]
    all_to_all x3, waiting for transfers between devices: 84.3 us -> 80.7 us  [exchange(): return lax.all_to_all(pairs, BOTH, split_axis=0, concat_axis=0, tiled=True)]
  transfers between devices with their start and end apart: 7 -> 7, of which waited for: 7 -> 7; matrix products, arithmetic and copies ran while one was open for 2% -> 4% of each run, Pallas kernels for 6% -> 6%
where the time goes in v5:
time: 247 us; the launch traced here: 246 us
  waiting for transfers between devices  106 us (43%)
  starting transfers between devices  61.6 us (25%)
  Pallas kernels  41.4 us (17%)
  blocking collectives  23.6 us (10%)
  other arithmetic  6.29 us (3%)
  local copies, waits for them, and re-layouts  6.09 us (2%)
    all_to_all x3, waiting for transfers between devices, exchange(): return lax.all_to_all(pairs, BOTH, split_axis=0, concat_axis=0, tiled=True)  80.7 us
    all_to_all x3, starting transfers between devices, exchange(): return lax.all_to_all(pairs, BOTH, split_axis=0, concat_axis=0, tiled=True)  43.6 us
    ppermute x4, waiting for transfers between devices, scatter_sum(): got = lax.ppermute(sent.astype(BF16), axis, pairs)  25.5 us
    all_gather x1, blocking collectives, shards(): cands = lax.all_gather(picked, 'ent', axis=0, tiled=True)  23.6 us
    ppermute x4, starting transfers between devices, scatter_sum(): got = lax.ppermute(sent.astype(BF16), axis, pairs)  18.1 us
    pallas_call x1, Pallas kernels, shards(): call(middle_kernel, [((owners, 2, width), BF16), ((queries, width), BF16)...  9.2 us
    pallas_call x1, Pallas kernels, shards(): call(slope_kernel, [((slots, hidden), BF16), ((width, slots), BF16)], 2 *...  7.57 us
    pallas_call x1, Pallas kernels, shards(): call(forward_kernel, [((owners, 2, width), BF16)], 4 * slots * width * hi...  7.5 us
  transfers between devices with their start and end apart: 7, of which 7 were waited for; matrix products, arithmetic and copies ran while one was open for 4% of the time, Pallas kernels for 6%

profile of v5, /device:TPU:1, one launch (start us, length us, event | category | flops | bytes accessed | tf_op | source)
XLA Modules:
  0.0 246.1 jit_solution(13153502997132915263)
XLA Ops:
  0.6 0.0 copy-start
  0.6 0.0 copy-start.10
  0.7 0.0 copy-start.2
  0.7 0.7 copy-done.2
  1.4 1.0 copy-done.4
  2.4 2.0 shard_map.112
  4.4 24.3 %all-to-all-start = ((bf16[512,2,400]{2,1,0:T(2,128)(2,1)}), bf16[512,2,400]{2,1,0:T(2,128)(2,1)S(1)}, u32[]{:S(2)}, u32[]{:S(2)}) async-start(bf16[512,2,400]{2,1,0:T(2,128)(2,1)} %shard_map.112), calls=%async_computation | async-start | bytes 2097152 | tf_op jit(solution)/shard_map/all_to_all | solution.py:256
  28.7 0.0 copy-done.10
  28.8 0.0 copy-done
  28.8 0.2 convolution_convert_fusion
  29.0 23.6 %all_gather.3.far_cands.cands = bf16[1024,400]{1,0:T(8,128)(2,1)} all-gather(bf16[64,400]{1,0:T(8,128)(2,1)S(1)} %convolution_convert_fusion), channel_id=1, replica_groups=mesh['rel'=32,'ent'=16] {'ent'}, dimensions={0}, use_global_device_ids=true | all-gather | bytes 870400 | tf_op jit(solution)/shard_map/all_gather | solution.py:272
  52.6 33.9 %all-to-all-done.inputs = bf16[512,2,400]{2,1,0:T(2,128)(2,1)S(1)} async-done(((bf16[512,2,400]{2,1,0:T(2,128)(2,1)}), bf16[512,2,400]{2,1,0:T(2,128)(2,1)S(1)}, u32[]{:S(2)}, u32[]{:S(2)}) %all-to-all-start) | async-done | bytes 819232 | tf_op jit(solution)/shard_map/all_to_all | solution.py:256
  86.5 7.5 %shard_map.113 = bf16[512,2,400]{2,1,0:T(2,128)(2,1)} custom-call(bf16[512,2,400]{2,1,0:T(2,128)(2,1)S(1)} %all-to-all-done.inputs, bf16[400,1600]{1,0:T(8,128)(2,1)} %bitcast.22, bf16[400,1600]{1,0:T(8,128)(2,1)} %bitcast.24), custom_call_target="tpu_custom_call" | custom-call | flops 2621440000 | bytes 4198400 | tf_op jit(solution)/shard_map/pallas_call | solution.py:295
  94.0 0.0 copy-done.1
  94.0 0.0 copy-start.9
  94.0 9.7 %all-to-all-start.1 = ((bf16[512,2,400]{2,1,0:T(2,128)(2,1)}), bf16[512,2,400]{2,1,0:T(2,128)(2,1)S(1)}, u32[]{:S(2)}, u32[]{:S(2)}) async-start(bf16[512,2,400]{2,1,0:T(2,128)(2,1)} %shard_map.113), calls=%async_computation.1 | async-start | bytes 2097152 | tf_op jit(solution)/shard_map/all_to_all | solution.py:256
  103.7 0.0 copy-done.3
  103.7 0.9 copy.13.rel_col
  104.6 0.0 copy-done.8
  104.6 0.9 copy.14.query_col
  105.5 0.0 copy-done.9
  105.5 0.8 copy.15.answer
  106.3 3.6 %shard_map.115 = (bf16[1024,512]{1,0:T(8,128)(2,1)}, bf16[512,1024]{1,0:T(8,128)(2,1)}, bf16[512,512]{1,0:T(8,128)(2,1)}, bf16[256,512]{1,0:T(8,128)(2,1)}, bf16[512,256]{1,0:T(8,128)(2,1)}) custom-call(s32[1,512]{1,0:T(1,128)} %bitcast.16, s32[512,1]{1,0:T(8,128)} %copy.13.rel_col, s32[1,512]{1,0:T(1,128)} %query_row.1, s32[512,1]{1,0:T(8,128)} %copy.14.query_col), custom_call_target="tpu_custom_call" | custom-call | flops 5242880 | bytes 2097152 | tf_op jit(solution)/shard_map/pallas_call | solution.py:276
  109.9 7.6 %shard_map.114 = (bf16[1024,1600]{1,0:T(8,128)(2,1)}, bf16[400,1024]{1,0:T(8,128)(2,1)}) custom-call(bf16[512,2,400]{2,1,0:T(2,128)(2,1)} %copy-done.1, bf16[400,1600]{1,0:T(8,128)(2,1)} %bitcast.23), custom_call_target="tpu_custom_call" | custom-call | flops 1310720000 | bytes 3276800 | tf_op jit(solution)/shard_map/pallas_call | solution.py:311
  117.5 44.1 %all-to-all-done.1.far_returned = bf16[512,2,400]{2,1,0:T(2,128)(2,1)S(1)} async-done(((bf16[512,2,400]{2,1,0:T(2,128)(2,1)}), bf16[512,2,400]{2,1,0:T(2,128)(2,1)S(1)}, u32[]{:S(2)}, u32[]{:S(2)}) %all-to-all-start.1) | async-done | bytes 819232 | tf_op jit(solution)/shard_map/all_to_all | solution.py:256
  161.6 1.0 copy-done.6
  162.6 9.2 %shard_map.116 = (bf16[512,2,400]{2,1,0:T(2,128)(2,1)}, bf16[256,400]{1,0:T(8,128)(2,1)}) custom-call(s32[256,1]{1,0:T(8,128)} %copy.15.answer, bf16[512,2,400]{2,1,0:T(2,128)(2,1)} %copy-done.6, bf16[512,1024]{1,0:T(8,128)(2,1)} %get-tuple-element.24.far_place_t, bf16[400,400]{1,0:T(8,128)(2,1)} %far_weight.1, bf16[512,512]{1,0:T(8,128)(2,1)} %get-tuple-element.25.far_same, ...), custom_call_target="tpu_custom_call" | custom-call | flops 838860800 | bytes 3276800 | tf_op jit(solution)/shard_map/pallas_call | solution.py:323
  171.8 9.5 %all-to-all-start.2 = ((bf16[512,2,400]{2,1,0:T(2,128)(2,1)}), bf16[512,2,400]{2,1,0:T(2,128)(2,1)S(1)}, u32[]{:S(2)}, u32[]{:S(2)}) async-start(bf16[512,2,400]{2,1,0:T(2,128)(2,1)} %get-tuple-element.32), calls=%async_computation.2 | async-start | bytes 2097152 | tf_op jit(solution)/shard_map/all_to_all | solution.py:256
  181.4 4.6 %shard_map.117 = (f32[1,256]{1,0:T(1,128)}, f32[1024,400]{1,0:T(8,128)}) custom-call(bf16[1024,400]{1,0:T(8,128)(2,1)} %all_gather.3.far_cands.cands, bf16[256,400]{1,0:T(8,128)(2,1)} %get-tuple-element.29.query_b, s32[1,256]{1,0:T(1,128)} %bitcast.20), custom_call_target="tpu_custom_call" | custom-call | flops 419430400 | bytes 3276800 | tf_op jit(solution)/shard_map/pallas_call | solution.py:334
  186.0 1.6 select_convert_fusion
  187.6 4.8 %collective-permute-start = (bf16[512,400]{1,0:T(8,128)(2,1)S(1)}, bf16[512,400]{1,0:T(8,128)(2,1)}, u32[]{:S(2)}, u32[]{:S(2)}) collective-permute-start(bf16[512,400]{1,0:T(8,128)(2,1)S(1)} %select_convert_fusion), channel_id=1, source_target_pairs={{0,8},{1,9},{2,10},{3,11},{4,12},{5,13},{6,14},{7,15},{8,0},{9,1},... | collective-permute-start | bytes 1228808 | tf_op jit(solution)/shard_map/ppermute | solution.py:240
  192.5 13.0 %collective-permute-done = bf16[512,400]{1,0:T(8,128)(2,1)} collective-permute-done((bf16[512,400]{1,0:T(8,128)(2,1)S(1)}, bf16[512,400]{1,0:T(8,128)(2,1)}, u32[]{:S(2)}, u32[]{:S(2)}) %collective-permute-start) | collective-permute-done | bytes 409632 | tf_op jit(solution)/shard_map/ppermute | solution.py:240
  205.5 2.0 convert_add_fusion
  207.5 0.8 select_convert_fusion.1
  208.2 5.6 %collective-permute-start.1 = (bf16[256,400]{1,0:T(8,128)(2,1)}, bf16[256,400]{1,0:T(8,128)(2,1)S(1)}, u32[]{:S(2)}, u32[]{:S(2)}) collective-permute-start(bf16[256,400]{1,0:T(8,128)(2,1)} %select_convert_fusion.1), channel_id=1, source_target_pairs={{0,4},{1,5},{2,6},{3,7},{4,0},{5,1},{6,2},{7,3},{8,12},{9,13},{10,... | collective-permute-start | bytes 614408 | tf_op jit(solution)/shard_map/ppermute | solution.py:240
  213.8 7.0 %collective-permute-done.1 = bf16[256,400]{1,0:T(8,128)(2,1)S(1)} collective-permute-done((bf16[256,400]{1,0:T(8,128)(2,1)}, bf16[256,400]{1,0:T(8,128)(2,1)S(1)}, u32[]{:S(2)}, u32[]{:S(2)}) %collective-permute-start.1) | collective-permute-done | bytes 204832 | tf_op jit(solution)/shard_map/ppermute | solution.py:240
  220.8 0.1 convert_add_fusion.1
  220.9 0.0 copy-start.7
  220.9 0.8 copy-done.7
  221.7 4.6 %collective-permute-start.2 = (bf16[128,400]{1,0:T(8,128)(2,1)S(1)}, bf16[128,400]{1,0:T(8,128)(2,1)S(1)}, u32[]{:S(2)}, u32[]{:S(2)}) collective-permute-start(bf16[128,400]{1,0:T(8,128)(2,1)S(1)} %select_convert_fusion.2), channel_id=1, source_target_pairs={{0,2},{1,3},{2,0},{3,1},{4,6},{5,7},{6,4},{7,5},{8,10},{9,11},{10,... | collective-permute-start | bytes 307208 | tf_op jit(solution)/shard_map/ppermute | solution.py:240
  226.3 3.2 %collective-permute-done.2 = bf16[128,400]{1,0:T(8,128)(2,1)S(1)} collective-permute-done((bf16[128,400]{1,0:T(8,128)(2,1)S(1)}, bf16[128,400]{1,0:T(8,128)(2,1)S(1)}, u32[]{:S(2)}, u32[]{:S(2)}) %collective-permute-start.2) | collective-permute-done | bytes 102432 | tf_op jit(solution)/shard_map/ppermute | solution.py:240
  229.6 1.1 convert_add_fusion.2
  230.7 3.1 %collective-permute-start.3 = (bf16[64,400]{1,0:T(8,128)(2,1)S(1)}, bf16[64,400]{1,0:T(8,128)(2,1)S(1)}, u32[]{:S(2)}, u32[]{:S(2)}) collective-permute-start(bf16[64,400]{1,0:T(8,128)(2,1)S(1)} %select_convert_fusion.3), channel_id=1, source_target_pairs={{0,1},{1,0},{2,3},{3,2},{4,5},{5,4},{6,7},{7,6},{8,9},{9,8},{10,11... | collective-permute-start | bytes 153608 | tf_op jit(solution)/shard_map/ppermute | solution.py:240
  233.8 2.2 collective-permute-done.3
  236.0 0.7 add_bitcast_fusion
  236.7 2.6 %all-to-all-done.2.incoming = bf16[512,2,400]{2,1,0:T(2,128)(2,1)S(1)} async-done(((bf16[512,2,400]{2,1,0:T(2,128)(2,1)}), bf16[512,2,400]{2,1,0:T(2,128)(2,1)S(1)}, u32[]{:S(2)}, u32[]{:S(2)}) %all-to-all-start.2) | async-done | bytes 819232 | tf_op jit(solution)/shard_map/all_to_all | solution.py:256
  239.3 0.0 copy-done.5
  239.3 6.8 %shard_map.118 = bf16[400,1600]{1,0:T(8,128)(2,1)} custom-call(bf16[512,2,400]{2,1,0:T(2,128)(2,1)S(1)} %all-to-all-done.2.incoming, bf16[400,1600]{1,0:T(8,128)(2,1)} %bitcast.25, bf16[1024,1600]{1,0:T(8,128)(2,1)} %get-tuple-element.33.slope, bf16[400,1024]{1,0:T(8,128)(2,1)S(1)} %copy-done.5), custom_call_target="tpu_custom_call" | custom-call | flops 2621440000 | bytes 6553600 | tf_op jit(solution)/shard_map/pallas_call | solution.py:342
  (9 shorter events, 0.1 us)
Async XLA Ops:
  0.6 28.1 %copy-start = (bf16[256,400]{0,1:T(8,128)(2,1)S(1)}, bf16[256,400]{0,1:T(8,128)(2,1)}, u32[]{:S(2)}) copy-start(bf16[256,400]{0,1:T(8,128)(2,1)} %param.14) | copy-start | bytes 614404
  0.6 28.1 %copy-start.10 = (s32[1,64]{1,0:T(1,128)S(1)}, s32[1,64]{1,0:T(1,128)}, u32[]{:S(2)}) copy-start(s32[1,64]{1,0:T(1,128)} %param.13) | copy-start | bytes 772
  0.7 0.7 copy-start.2
  1.4 1.0 copy-start.4
  4.4 82.1 %all-to-all-start = ((bf16[512,2,400]{2,1,0:T(2,128)(2,1)}), bf16[512,2,400]{2,1,0:T(2,128)(2,1)S(1)}, u32[]{:S(2)}, u32[]{:S(2)}) async-start(bf16[512,2,400]{2,1,0:T(2,128)(2,1)} %shard_map.112), calls=%async_computation | async-start | bytes 2097152 | tf_op jit(solution)/shard_map/all_to_all | solution.py:256
  86.5 7.5 %copy-start.1 = (bf16[512,2,400]{2,1,0:T(2,128)(2,1)}, bf16[512,2,400]{2,1,0:T(2,128)(2,1)S(1)}, u32[]{:S(2)}) copy-start(bf16[512,2,400]{2,1,0:T(2,128)(2,1)S(1)} %all-to-all-done.inputs) | copy-start | bytes 2457604
  94.0 9.7 %copy-start.3 = (s32[512,1]{0,1:T(1,128)S(1)}, s32[512,1]{0,1:T(1,128)}, u32[]{:S(2)}) copy-start(s32[512,1]{0,1:T(1,128)} %param.10) | copy-start | bytes 6148
  94.0 10.6 %copy-start.8 = (s32[1,512]{1,0:T(1,128)S(1)}, s32[1,512]{1,0:T(1,128)}, u32[]{:S(2)}) copy-start(s32[1,512]{1,0:T(1,128)} %query_row.1) | copy-start | bytes 6148
  94.0 11.5 %copy-start.9 = (s32[256]{0:T(256)S(1)}, s32[256]{0:T(256)}, u32[]{:S(2)}) copy-start(s32[256]{0:T(256)} %param.12) | copy-start | bytes 3076
  94.0 67.6 %all-to-all-start.1 = ((bf16[512,2,400]{2,1,0:T(2,128)(2,1)}), bf16[512,2,400]{2,1,0:T(2,128)(2,1)S(1)}, u32[]{:S(2)}, u32[]{:S(2)}) async-start(bf16[512,2,400]{2,1,0:T(2,128)(2,1)} %shard_map.113), calls=%async_computation.1 | async-start | bytes 2097152 | tf_op jit(solution)/shard_map/all_to_all | solution.py:256
  161.6 1.0 copy-start.6
  171.8 67.5 %all-to-all-start.2 = ((bf16[512,2,400]{2,1,0:T(2,128)(2,1)}), bf16[512,2,400]{2,1,0:T(2,128)(2,1)S(1)}, u32[]{:S(2)}, u32[]{:S(2)}) async-start(bf16[512,2,400]{2,1,0:T(2,128)(2,1)} %get-tuple-element.32), calls=%async_computation.2 | async-start | bytes 2097152 | tf_op jit(solution)/shard_map/all_to_all | solution.py:256
  187.6 17.9 %collective-permute-start = (bf16[512,400]{1,0:T(8,128)(2,1)S(1)}, bf16[512,400]{1,0:T(8,128)(2,1)}, u32[]{:S(2)}, u32[]{:S(2)}) collective-permute-start(bf16[512,400]{1,0:T(8,128)(2,1)S(1)} %select_convert_fusion), channel_id=1, source_target_pairs={{0,8},{1,9},{2,10},{3,11},{4,12},{5,13},{6,14},{7,15},{8,0},{9,1},... | collective-permute-start | bytes 1228808 | tf_op jit(solution)/shard_map/ppermute | solution.py:240
  208.2 31.1 %copy-start.5 = (bf16[400,1024]{1,0:T(8,128)(2,1)S(1)}, bf16[400,1024]{1,0:T(8,128)(2,1)}, u32[]{:S(2)}) copy-start(bf16[400,1024]{1,0:T(8,128)(2,1)} %get-tuple-element.34.inputs_t) | copy-start | bytes 2457604
  208.2 12.6 %collective-permute-start.1 = (bf16[256,400]{1,0:T(8,128)(2,1)}, bf16[256,400]{1,0:T(8,128)(2,1)S(1)}, u32[]{:S(2)}, u32[]{:S(2)}) collective-permute-start(bf16[256,400]{1,0:T(8,128)(2,1)} %select_convert_fusion.1), channel_id=1, source_target_pairs={{0,4},{1,5},{2,6},{3,7},{4,0},{5,1},{6,2},{7,3},{8,12},{9,13},{10,... | collective-permute-start | bytes 614408 | tf_op jit(solution)/shard_map/ppermute | solution.py:240
  220.9 0.8 copy-start.7
  221.7 7.8 %collective-permute-start.2 = (bf16[128,400]{1,0:T(8,128)(2,1)S(1)}, bf16[128,400]{1,0:T(8,128)(2,1)S(1)}, u32[]{:S(2)}, u32[]{:S(2)}) collective-permute-start(bf16[128,400]{1,0:T(8,128)(2,1)S(1)} %select_convert_fusion.2), channel_id=1, source_target_pairs={{0,2},{1,3},{2,0},{3,1},{4,6},{5,7},{6,4},{7,5},{8,10},{9,11},{10,... | collective-permute-start | bytes 307208 | tf_op jit(solution)/shard_map/ppermute | solution.py:240
  230.7 5.3 %collective-permute-start.3 = (bf16[64,400]{1,0:T(8,128)(2,1)S(1)}, bf16[64,400]{1,0:T(8,128)(2,1)S(1)}, u32[]{:S(2)}, u32[]{:S(2)}) collective-permute-start(bf16[64,400]{1,0:T(8,128)(2,1)S(1)} %select_convert_fusion.3), channel_id=1, source_target_pairs={{0,1},{1,0},{2,3},{3,2},{4,5},{5,4},{6,7},{7,6},{8,9},{9,8},{10,11... | collective-permute-start | bytes 153608 | tf_op jit(solution)/shard_map/ppermute | solution.py:240

commit v6 on v5

--- a/solution.py
+++ b/solution.py
@@ -162,6 +162,8 @@
     expand,
     place,
     sems,
+    ready,
+    out_sems,
 ):
     copies = fetch(
         (
@@ -205,7 +207,18 @@
     pre_grad = grad_each * (projected - query_each) * ATT_GAIN * (1.0 - att_tanh * att_tanh)
     proj_grad = grad_each + mm(pre_grad.astype(BF16), att_weight[...], 1, 1)
     copies[7].wait()
-    outgoing[...] = paired(mm(place[...], proj_grad.astype(BF16)).astype(BF16))
+    grads = proj_grad.astype(BF16)
+    pairs = ready.shape[0]
+    leaving = []
+    for number in range(4):
+        part = slice(number * pairs // 4, (number + 1) * pairs // 4)
+        rows = slice(number * pairs // 2, (number + 1) * pairs // 2)
+        ready[part] = paired(mm(place[rows, :], grads).astype(BF16))
+        copy = pltpu.make_async_copy(ready.at[part], outgoing.at[part], out_sems.at[number])
+        copy.start()
+        leaving.append(copy)
+    for copy in leaving:
+        copy.wait()
 
 
 def loss_kernel(cands, query_b, answer, loss, cand_part):
@@ -262,7 +275,6 @@
         [((owners, 2, width), BF16)],
         2 * slots * branches * width,
         4 * slots * branches,
-        limit=16,
     )(rel_row, anchors.T)
     inputs = exchange(packed)
 
@@ -297,7 +309,7 @@
         [((owners, 2, width), BF16)],
         4 * slots * width * hidden,
         4 * slots * width + 4 * width * hidden,
-        limit=51,
+        limit=50,
         grid=(slots // half,),
         in_specs=[
             pairs_of(half),
@@ -326,8 +338,9 @@
         4 * branches * slots * width,
         8 * slots * width,
         in_specs=[NEAR] + [FAR] * len(far),
-        out_specs=[NEAR] * 2,
-        scratch_shapes=room(far),
+        out_specs=[FAR, NEAR],
+        scratch_shapes=room(far)
+        + [pltpu.VMEM((owners, 2, width), BF16), pltpu.SemaphoreType.DMA((4,))],
     )(answer.reshape(queries, 1), *far)
     incoming = exchange(outgoing)
 

time: 247 us -> 246 us (level)
  no operation moved by 1% of the time
where the time goes in v6:
time: 246 us
  waiting for transfers between devices  106 us (43%)
  starting transfers between devices  61.7 us (25%)
  Pallas kernels  42.5 us (17%)
  blocking collectives  23.6 us (10%)
  other arithmetic  6.29 us (3%)
  local copies, waits for them, and re-layouts  4.35 us (2%)
    all_to_all x3, waiting for transfers between devices, exchange(): return lax.all_to_all(pairs, BOTH, split_axis=0, concat_axis=0, tiled=True)  80.7 us
    all_to_all x3, starting transfers between devices, exchange(): return lax.all_to_all(pairs, BOTH, split_axis=0, concat_axis=0, tiled=True)  43.5 us
    ppermute x4, waiting for transfers between devices, scatter_sum(): got = lax.ppermute(sent.astype(BF16), axis, pairs)  25.4 us
    all_gather x1, blocking collectives, shards(): cands = lax.all_gather(picked, 'ent', axis=0, tiled=True)  23.6 us
    ppermute x4, starting transfers between devices, scatter_sum(): got = lax.ppermute(sent.astype(BF16), axis, pairs)  18.1 us
    pallas_call x1, Pallas kernels, shards(): call(middle_kernel, [((owners, 2, width), BF16), ((queries, width), BF16)...  9.64 us
    pallas_call x1, Pallas kernels, shards(): call(slope_kernel, [((slots, hidden), BF16), ((width, slots), BF16)], 2 *...  7.57 us
    pallas_call x1, Pallas kernels, shards(): call(forward_kernel, [((owners, 2, width), BF16)], 4 * slots * width * hi...  7.11 us
  transfers between devices with their start and end apart: 7, of which 7 were waited for; matrix products, arithmetic and copies ran while one was open for 4% of the time, Pallas kernels for 6%

profile of v6, /device:TPU:1, one launch (start us, length us, event | category | flops | bytes accessed | tf_op | source)
XLA Modules:
  0.0 245.5 jit_solution(4242526507420134930)
XLA Ops:
  0.6 0.0 copy-start
  0.6 0.0 copy-start.9
  0.7 3.1 %shard_map.112 = bf16[512,2,400]{2,1,0:T(2,128)(2,1)} custom-call(s32[1,512]{1,0:T(1,128)} %bitcast.18, bf16[400,512]{1,0:T(8,128)(2,1)} %bitcast.25), custom_call_target="tpu_custom_call" | custom-call | flops 419430400 | bytes 2097152 | tf_op jit(solution)/shard_map/pallas_call | solution.py:273
  3.8 0.0 copy-start.2
  3.8 24.3 %all-to-all-start = ((bf16[512,2,400]{2,1,0:T(2,128)(2,1)}), bf16[512,2,400]{2,1,0:T(2,128)(2,1)S(1)}, u32[]{:S(2)}, u32[]{:S(2)}) async-start(bf16[512,2,400]{2,1,0:T(2,128)(2,1)} %shard_map.112), calls=%async_computation | async-start | bytes 2097152 | tf_op jit(solution)/shard_map/all_to_all | solution.py:269
  28.1 0.0 copy-done.9
  28.1 0.0 copy-done
  28.1 0.2 convolution_convert_fusion
  28.3 23.6 %all_gather.3.far_cands.cands = bf16[1024,400]{1,0:T(8,128)(2,1)} all-gather(bf16[64,400]{1,0:T(8,128)(2,1)S(1)} %convolution_convert_fusion), channel_id=1, replica_groups=mesh['rel'=32,'ent'=16] {'ent'}, dimensions={0}, use_global_device_ids=true | all-gather | bytes 870400 | tf_op jit(solution)/shard_map/all_gather | solution.py:284
  51.9 33.9 %all-to-all-done.inputs = bf16[512,2,400]{2,1,0:T(2,128)(2,1)S(1)} async-done(((bf16[512,2,400]{2,1,0:T(2,128)(2,1)}), bf16[512,2,400]{2,1,0:T(2,128)(2,1)S(1)}, u32[]{:S(2)}, u32[]{:S(2)}) %all-to-all-start) | async-done | bytes 819232 | tf_op jit(solution)/shard_map/all_to_all | solution.py:269
  85.8 0.0 copy-start.1
  85.9 0.0 copy-done.2
  85.9 7.1 %shard_map.113 = bf16[512,2,400]{2,1,0:T(2,128)(2,1)} custom-call(bf16[512,2,400]{2,1,0:T(2,128)(2,1)S(1)} %all-to-all-done.inputs, bf16[400,1600]{1,0:T(8,128)(2,1)S(1)} %bitcast.17, bf16[400,1600]{1,0:T(8,128)(2,1)} %bitcast.23), custom_call_target="tpu_custom_call" | custom-call | flops 2621440000 | bytes 4198400 | tf_op jit(solution)/shard_map/pallas_call | solution.py:307
  93.0 0.0 copy-done.1
  93.0 0.0 copy-start.6
  93.0 9.7 %all-to-all-start.1 = ((bf16[512,2,400]{2,1,0:T(2,128)(2,1)}), bf16[512,2,400]{2,1,0:T(2,128)(2,1)S(1)}, u32[]{:S(2)}, u32[]{:S(2)}) async-start(bf16[512,2,400]{2,1,0:T(2,128)(2,1)} %shard_map.113), calls=%async_computation.1 | async-start | bytes 2097152 | tf_op jit(solution)/shard_map/all_to_all | solution.py:269
  102.7 0.0 copy-done.6
  102.7 0.9 copy.13.rel_col
  103.5 0.0 copy-done.7
  103.6 0.9 copy.14.query_col
  104.5 0.0 copy-done.8
  104.5 0.8 copy.15.answer
  105.3 3.6 %shard_map.115 = (bf16[1024,512]{1,0:T(8,128)(2,1)}, bf16[512,1024]{1,0:T(8,128)(2,1)}, bf16[512,512]{1,0:T(8,128)(2,1)}, bf16[256,512]{1,0:T(8,128)(2,1)}, bf16[512,256]{1,0:T(8,128)(2,1)}) custom-call(s32[1,512]{1,0:T(1,128)} %bitcast.19, s32[512,1]{1,0:T(8,128)} %copy.13.rel_col, s32[1,512]{1,0:T(1,128)} %query_row.1, s32[512,1]{1,0:T(8,128)} %copy.14.query_col), custom_call_target="tpu_custom_call" | custom-call | flops 5242880 | bytes 2097152 | tf_op jit(solution)/shard_map/pallas_call | solution.py:288
  108.9 7.6 %shard_map.114 = (bf16[1024,1600]{1,0:T(8,128)(2,1)}, bf16[400,1024]{1,0:T(8,128)(2,1)}) custom-call(bf16[512,2,400]{2,1,0:T(2,128)(2,1)} %copy-done.1, bf16[400,1600]{1,0:T(8,128)(2,1)} %bitcast.16), custom_call_target="tpu_custom_call" | custom-call | flops 1310720000 | bytes 3276800 | tf_op jit(solution)/shard_map/pallas_call | solution.py:323
  116.5 44.1 %all-to-all-done.1.far_returned = bf16[512,2,400]{2,1,0:T(2,128)(2,1)S(1)} async-done(((bf16[512,2,400]{2,1,0:T(2,128)(2,1)}), bf16[512,2,400]{2,1,0:T(2,128)(2,1)S(1)}, u32[]{:S(2)}, u32[]{:S(2)}) %all-to-all-start.1) | async-done | bytes 819232 | tf_op jit(solution)/shard_map/all_to_all | solution.py:269
  160.6 1.0 copy-done.4
  161.6 9.6 %shard_map.116 = (bf16[512,2,400]{2,1,0:T(2,128)(2,1)}, bf16[256,400]{1,0:T(8,128)(2,1)}) custom-call(s32[256,1]{1,0:T(8,128)} %copy.15.answer, bf16[512,2,400]{2,1,0:T(2,128)(2,1)} %copy-done.4, bf16[512,1024]{1,0:T(8,128)(2,1)} %get-tuple-element.24.far_place_t, bf16[400,400]{1,0:T(8,128)(2,1)} %far_weight.1, bf16[512,512]{1,0:T(8,128)(2,1)} %get-tuple-element.25.far_same, ...), custom_call_target="tpu_custom_call" | custom-call | flops 838860800 | bytes 3276800 | tf_op jit(solution)/shard_map/pallas_call | solution.py:335
  171.2 9.5 %all-to-all-start.2 = ((bf16[512,2,400]{2,1,0:T(2,128)(2,1)}), bf16[512,2,400]{2,1,0:T(2,128)(2,1)S(1)}, u32[]{:S(2)}, u32[]{:S(2)}) async-start(bf16[512,2,400]{2,1,0:T(2,128)(2,1)} %get-tuple-element.32), calls=%async_computation.2 | async-start | bytes 2097152 | tf_op jit(solution)/shard_map/all_to_all | solution.py:269
  180.8 4.6 %shard_map.117 = (f32[1,256]{1,0:T(1,128)}, f32[1024,400]{1,0:T(8,128)}) custom-call(bf16[1024,400]{1,0:T(8,128)(2,1)} %all_gather.3.far_cands.cands, bf16[256,400]{1,0:T(8,128)(2,1)} %get-tuple-element.29.query_b, s32[1,256]{1,0:T(1,128)} %bitcast.21), custom_call_target="tpu_custom_call" | custom-call | flops 419430400 | bytes 3276800 | tf_op jit(solution)/shard_map/pallas_call | solution.py:347
  185.4 1.6 select_convert_fusion
  187.0 4.8 %collective-permute-start = (bf16[512,400]{1,0:T(8,128)(2,1)S(1)}, bf16[512,400]{1,0:T(8,128)(2,1)}, u32[]{:S(2)}, u32[]{:S(2)}) collective-permute-start(bf16[512,400]{1,0:T(8,128)(2,1)S(1)} %select_convert_fusion), channel_id=1, source_target_pairs={{0,8},{1,9},{2,10},{3,11},{4,12},{5,13},{6,14},{7,15},{8,0},{9,1},... | collective-permute-start | bytes 1228808 | tf_op jit(solution)/shard_map/ppermute | solution.py:253
  191.8 13.0 %collective-permute-done = bf16[512,400]{1,0:T(8,128)(2,1)} collective-permute-done((bf16[512,400]{1,0:T(8,128)(2,1)S(1)}, bf16[512,400]{1,0:T(8,128)(2,1)}, u32[]{:S(2)}, u32[]{:S(2)}) %collective-permute-start) | collective-permute-done | bytes 409632 | tf_op jit(solution)/shard_map/ppermute | solution.py:253
  204.9 2.0 convert_add_fusion
  206.8 0.8 select_convert_fusion.1
  207.6 5.6 %collective-permute-start.1 = (bf16[256,400]{1,0:T(8,128)(2,1)}, bf16[256,400]{1,0:T(8,128)(2,1)S(1)}, u32[]{:S(2)}, u32[]{:S(2)}) collective-permute-start(bf16[256,400]{1,0:T(8,128)(2,1)} %select_convert_fusion.1), channel_id=1, source_target_pairs={{0,4},{1,5},{2,6},{3,7},{4,0},{5,1},{6,2},{7,3},{8,12},{9,13},{10,... | collective-permute-start | bytes 614408 | tf_op jit(solution)/shard_map/ppermute | solution.py:253
  213.2 7.0 %collective-permute-done.1 = bf16[256,400]{1,0:T(8,128)(2,1)S(1)} collective-permute-done((bf16[256,400]{1,0:T(8,128)(2,1)}, bf16[256,400]{1,0:T(8,128)(2,1)S(1)}, u32[]{:S(2)}, u32[]{:S(2)}) %collective-permute-start.1) | collective-permute-done | bytes 204832 | tf_op jit(solution)/shard_map/ppermute | solution.py:253
  220.2 0.1 convert_add_fusion.1
  220.3 0.0 copy-start.5
  220.3 0.8 copy-done.5
  221.1 4.6 %collective-permute-start.2 = (bf16[128,400]{1,0:T(8,128)(2,1)S(1)}, bf16[128,400]{1,0:T(8,128)(2,1)S(1)}, u32[]{:S(2)}, u32[]{:S(2)}) collective-permute-start(bf16[128,400]{1,0:T(8,128)(2,1)S(1)} %select_convert_fusion.2), channel_id=1, source_target_pairs={{0,2},{1,3},{2,0},{3,1},{4,6},{5,7},{6,4},{7,5},{8,10},{9,11},{10,... | collective-permute-start | bytes 307208 | tf_op jit(solution)/shard_map/ppermute | solution.py:253
  225.7 3.2 %collective-permute-done.2 = bf16[128,400]{1,0:T(8,128)(2,1)S(1)} collective-permute-done((bf16[128,400]{1,0:T(8,128)(2,1)S(1)}, bf16[128,400]{1,0:T(8,128)(2,1)S(1)}, u32[]{:S(2)}, u32[]{:S(2)}) %collective-permute-start.2) | collective-permute-done | bytes 102432 | tf_op jit(solution)/shard_map/ppermute | solution.py:253
  228.9 1.1 convert_add_fusion.2
  230.0 3.1 %collective-permute-start.3 = (bf16[64,400]{1,0:T(8,128)(2,1)S(1)}, bf16[64,400]{1,0:T(8,128)(2,1)S(1)}, u32[]{:S(2)}, u32[]{:S(2)}) collective-permute-start(bf16[64,400]{1,0:T(8,128)(2,1)S(1)} %select_convert_fusion.3), channel_id=1, source_target_pairs={{0,1},{1,0},{2,3},{3,2},{4,5},{5,4},{6,7},{7,6},{8,9},{9,8},{10,11... | collective-permute-start | bytes 153608 | tf_op jit(solution)/shard_map/ppermute | solution.py:253
  233.2 2.2 collective-permute-done.3
  235.4 0.7 add_bitcast_fusion
  236.1 2.6 %all-to-all-done.2.incoming = bf16[512,2,400]{2,1,0:T(2,128)(2,1)S(1)} async-done(((bf16[512,2,400]{2,1,0:T(2,128)(2,1)}), bf16[512,2,400]{2,1,0:T(2,128)(2,1)S(1)}, u32[]{:S(2)}, u32[]{:S(2)}) %all-to-all-start.2) | async-done | bytes 819232 | tf_op jit(solution)/shard_map/all_to_all | solution.py:269
  238.7 0.0 copy-done.3
  238.7 6.9 %shard_map.118 = bf16[400,1600]{1,0:T(8,128)(2,1)} custom-call(bf16[512,2,400]{2,1,0:T(2,128)(2,1)S(1)} %all-to-all-done.2.incoming, bf16[400,1600]{1,0:T(8,128)(2,1)} %bitcast.24, bf16[1024,1600]{1,0:T(8,128)(2,1)} %get-tuple-element.33.slope, bf16[400,1024]{1,0:T(8,128)(2,1)S(1)} %copy-done.3), custom_call_target="tpu_custom_call" | custom-call | flops 2621440000 | bytes 6553600 | tf_op jit(solution)/shard_map/pallas_call | solution.py:355
  (7 shorter events, 0.1 us)
Async XLA Ops:
  0.6 27.5 %copy-start = (bf16[256,400]{0,1:T(8,128)(2,1)S(1)}, bf16[256,400]{0,1:T(8,128)(2,1)}, u32[]{:S(2)}) copy-start(bf16[256,400]{0,1:T(8,128)(2,1)} %param.14) | copy-start | bytes 614404
  0.6 27.4 %copy-start.9 = (s32[1,64]{1,0:T(1,128)S(1)}, s32[1,64]{1,0:T(1,128)}, u32[]{:S(2)}) copy-start(s32[1,64]{1,0:T(1,128)} %param.13) | copy-start | bytes 772
  3.8 82.1 %copy-start.2 = (bf16[1,400,1600]{2,1,0:T(8,128)(2,1)S(1)}, bf16[1,400,1600]{2,1,0:T(8,128)(2,1)}, u32[]{:S(2)}) copy-start(bf16[1,400,1600]{2,1,0:T(8,128)(2,1)} %param.15) | copy-start | bytes 3840004
  3.8 82.1 %all-to-all-start = ((bf16[512,2,400]{2,1,0:T(2,128)(2,1)}), bf16[512,2,400]{2,1,0:T(2,128)(2,1)S(1)}, u32[]{:S(2)}, u32[]{:S(2)}) async-start(bf16[512,2,400]{2,1,0:T(2,128)(2,1)} %shard_map.112), calls=%async_computation | async-start | bytes 2097152 | tf_op jit(solution)/shard_map/all_to_all | solution.py:269
  85.8 7.1 %copy-start.1 = (bf16[512,2,400]{2,1,0:T(2,128)(2,1)}, bf16[512,2,400]{2,1,0:T(2,128)(2,1)S(1)}, u32[]{:S(2)}) copy-start(bf16[512,2,400]{2,1,0:T(2,128)(2,1)S(1)} %all-to-all-done.inputs) | copy-start | bytes 2457604
  93.0 9.7 %copy-start.6 = (s32[512,1]{0,1:T(1,128)S(1)}, s32[512,1]{0,1:T(1,128)}, u32[]{:S(2)}) copy-start(s32[512,1]{0,1:T(1,128)} %param.10) | copy-start | bytes 6148
  93.0 10.6 %copy-start.7 = (s32[1,512]{1,0:T(1,128)S(1)}, s32[1,512]{1,0:T(1,128)}, u32[]{:S(2)}) copy-start(s32[1,512]{1,0:T(1,128)} %query_row.1) | copy-start | bytes 6148
  93.0 11.5 %copy-start.8 = (s32[256]{0:T(256)S(1)}, s32[256]{0:T(256)}, u32[]{:S(2)}) copy-start(s32[256]{0:T(256)} %param.12) | copy-start | bytes 3076
  93.0 67.6 %all-to-all-start.1 = ((bf16[512,2,400]{2,1,0:T(2,128)(2,1)}), bf16[512,2,400]{2,1,0:T(2,128)(2,1)S(1)}, u32[]{:S(2)}, u32[]{:S(2)}) async-start(bf16[512,2,400]{2,1,0:T(2,128)(2,1)} %shard_map.113), calls=%async_computation.1 | async-start | bytes 2097152 | tf_op jit(solution)/shard_map/all_to_all | solution.py:269
  160.6 1.0 copy-start.4
  171.2 67.5 %all-to-all-start.2 = ((bf16[512,2,400]{2,1,0:T(2,128)(2,1)}), bf16[512,2,400]{2,1,0:T(2,128)(2,1)S(1)}, u32[]{:S(2)}, u32[]{:S(2)}) async-start(bf16[512,2,400]{2,1,0:T(2,128)(2,1)} %get-tuple-element.32), calls=%async_computation.2 | async-start | bytes 2097152 | tf_op jit(solution)/shard_map/all_to_all | solution.py:269
  187.0 17.9 %collective-permute-start = (bf16[512,400]{1,0:T(8,128)(2,1)S(1)}, bf16[512,400]{1,0:T(8,128)(2,1)}, u32[]{:S(2)}, u32[]{:S(2)}) collective-permute-start(bf16[512,400]{1,0:T(8,128)(2,1)S(1)} %select_convert_fusion), channel_id=1, source_target_pairs={{0,8},{1,9},{2,10},{3,11},{4,12},{5,13},{6,14},{7,15},{8,0},{9,1},... | collective-permute-start | bytes 1228808 | tf_op jit(solution)/shard_map/ppermute | solution.py:253
  207.6 31.1 %copy-start.3 = (bf16[400,1024]{1,0:T(8,128)(2,1)S(1)}, bf16[400,1024]{1,0:T(8,128)(2,1)}, u32[]{:S(2)}) copy-start(bf16[400,1024]{1,0:T(8,128)(2,1)} %get-tuple-element.34.inputs_t) | copy-start | bytes 2457604
  207.6 12.6 %collective-permute-start.1 = (bf16[256,400]{1,0:T(8,128)(2,1)}, bf16[256,400]{1,0:T(8,128)(2,1)S(1)}, u32[]{:S(2)}, u32[]{:S(2)}) collective-permute-start(bf16[256,400]{1,0:T(8,128)(2,1)} %select_convert_fusion.1), channel_id=1, source_target_pairs={{0,4},{1,5},{2,6},{3,7},{4,0},{5,1},{6,2},{7,3},{8,12},{9,13},{10,... | collective-permute-start | bytes 614408 | tf_op jit(solution)/shard_map/ppermute | solution.py:253
  220.3 0.8 copy-start.5
  221.1 7.8 %collective-permute-start.2 = (bf16[128,400]{1,0:T(8,128)(2,1)S(1)}, bf16[128,400]{1,0:T(8,128)(2,1)S(1)}, u32[]{:S(2)}, u32[]{:S(2)}) collective-permute-start(bf16[128,400]{1,0:T(8,128)(2,1)S(1)} %select_convert_fusion.2), channel_id=1, source_target_pairs={{0,2},{1,3},{2,0},{3,1},{4,6},{5,7},{6,4},{7,5},{8,10},{9,11},{10,... | collective-permute-start | bytes 307208 | tf_op jit(solution)/shard_map/ppermute | solution.py:253
  230.0 5.3 %collective-permute-start.3 = (bf16[64,400]{1,0:T(8,128)(2,1)S(1)}, bf16[64,400]{1,0:T(8,128)(2,1)S(1)}, u32[]{:S(2)}, u32[]{:S(2)}) collective-permute-start(bf16[64,400]{1,0:T(8,128)(2,1)S(1)} %select_convert_fusion.3), channel_id=1, source_target_pairs={{0,1},{1,0},{2,3},{3,2},{4,5},{5,4},{6,7},{7,6},{8,9},{9,8},{10,11... | collective-permute-start | bytes 153608 | tf_op jit(solution)/shard_map/ppermute | solution.py:253

commit v7 on v6

--- a/solution.py
+++ b/solution.py
@@ -221,17 +221,24 @@
         copy.wait()
 
 
-def loss_kernel(cands, query_b, answer, loss, cand_part):
-    negatives, width = cands.shape
-    scale = width ** (-0.5)
+def scores_by_candidate(cands, queries, answer):
+    scores = mm(cands[...], queries, 1, 1) * cands.shape[1] ** (-0.5)
+    return scores, iota(scores.shape, 0) == answer[...]
+
+
+def cand_kernel(cands, query_b, answer, cand_part):
     queries = query_b[...]
-    scores = mm(cands[...], queries, 1, 1) * scale
-    is_answer = iota(scores.shape, 0) == answer[...]
-    signed, small, coefficient = sigmoid_parts(scores, is_answer, negatives)
-    softplus = jnp.maximum(signed, 0.0) + jnp.log1p(small)
-    weight = jnp.where(is_answer, 1.0, 1.0 / (negatives - 1))
+    scores, is_answer = scores_by_candidate(cands, queries, answer)
+    _, _, coefficient = sigmoid_parts(scores, is_answer, cands.shape[0])
+    cand_part[...] = mm(coefficient, queries) * cands.shape[1] ** (-0.5)
+
+
+def loss_kernel(cands, query_b, answer, loss):
+    scores, is_answer = scores_by_candidate(cands, query_b[...], answer)
+    signed = jnp.where(is_answer, -scores, scores)
+    softplus = jnp.maximum(signed, 0.0) + jnp.log1p(jnp.exp(-jnp.abs(signed)))
+    weight = jnp.where(is_answer, 1.0, 1.0 / (cands.shape[0] - 1))
     loss[...] = jnp.sum(softplus * weight, axis=0, keepdims=True)
-    cand_part[...] = mm(coefficient, queries) * scale
 
 
 def backward_kernel(incoming, w_out_t, slope, inputs_t, w_in_grad):
@@ -242,17 +249,19 @@
 def scatter_sum(part, axis):
     count = lax.axis_size(axis)
     me = lax.axis_index(axis)
-    gap = count // 2
-    while gap:
-        half = part.shape[0] // 2
-        low, high = part[:half], part[half:]
+    gaps = [1 << bit for bit in range(count.bit_length() - 1)][::-1]
+    part = part.reshape((2,) * len(gaps) + (part.shape[0] // count, part.shape[1]))
+    for gap in sorted(gaps, key=lambda gap: (gap in gaps[::2], gap)):
+        place = gaps.index(gap)
+        low = lax.index_in_dim(part, 0, place, keepdims=False)
+        high = lax.index_in_dim(part, 1, place, keepdims=False)
         upper = (me & gap) != 0
         sent = jnp.where(upper, low, high)
         kept = jnp.where(upper, high, low)
         pairs = [(i, i ^ gap) for i in range(count)]
         got = lax.ppermute(sent.astype(BF16), axis, pairs)
         part = kept + got.astype(F32)
-        gap //= 2
+        gaps.remove(gap)
     return part
 
 
@@ -344,12 +353,19 @@
     )(answer.reshape(queries, 1), *far)
     incoming = exchange(outgoing)
 
-    loss, cand_part = call(
-        loss_kernel,
-        [((1, queries), F32), ((negatives, width), F32)],
+    scored = (cands, query_b, answer.reshape(1, queries))
+    (cand_part,) = call(
+        cand_kernel,
+        [((negatives, width), F32)],
         4 * queries * negatives * width,
         8 * negatives * width,
-    )(cands, query_b, answer.reshape(1, queries))
+    )(*scored)
+    (loss,) = call(
+        loss_kernel,
+        [((1, queries), F32)],
+        2 * queries * negatives * width,
+        2 * negatives * width,
+    )(*scored)
     cand_grad = scatter_sum(cand_part, "ent")
 
     (w_in_grad,) = call(

time: 246 us -> 246 us (level)
  waiting for transfers between devices: 106 us -> 101 us
    ppermute x4, waiting for transfers between devices: 25.4 us -> 21.8 us  [scatter_sum(): got = lax.ppermute(sent.astype(BF16), axis, pairs)]
    pallas_call x1 -> x2, Pallas kernels: 4.61 us -> 7 us  [the longest x1 4.12 us: shards(): call(cand_kernel, [((negatives, width), F32)], 4 * queries * negatives *...]
  transfers between devices with their start and end apart: 7 -> 7, of which waited for: 7 -> 6; matrix products, arithmetic and copies ran while one was open for 4% -> 4% of each run, Pallas kernels for 6% -> 7%
where the time goes in v7:
time: 246 us
  waiting for transfers between devices  101 us (41%)
  starting transfers between devices  64.1 us (26%)
  Pallas kernels  44.9 us (18%)
  blocking collectives  23.6 us (10%)
  local copies, waits for them, and re-layouts  6.33 us (3%)
  other arithmetic  4.36 us (2%)
    all_to_all x3, waiting for transfers between devices, exchange(): return lax.all_to_all(pairs, BOTH, split_axis=0, concat_axis=0, tiled=True)  79.3 us
    all_to_all x3, starting transfers between devices, exchange(): return lax.all_to_all(pairs, BOTH, split_axis=0, concat_axis=0, tiled=True)  43.6 us
    all_gather x1, blocking collectives, shards(): cands = lax.all_gather(picked, 'ent', axis=0, tiled=True)  23.6 us
    ppermute x4, waiting for transfers between devices, scatter_sum(): got = lax.ppermute(sent.astype(BF16), axis, pairs)  21.8 us
    ppermute x4, starting transfers between devices, scatter_sum(): got = lax.ppermute(sent.astype(BF16), axis, pairs)  20.6 us
    pallas_call x1, Pallas kernels, shards(): call(middle_kernel, [((owners, 2, width), BF16), ((queries, width), BF16)...  9.64 us
    pallas_call x1, Pallas kernels, shards(): call(slope_kernel, [((slots, hidden), BF16), ((width, slots), BF16)], 2 *...  7.57 us
    pallas_call x1, Pallas kernels, shards(): call(forward_kernel, [((owners, 2, width), BF16)], 4 * slots * width * hi...  7.11 us
  transfers between devices with their start and end apart: 7, of which 6 were waited for; matrix products, arithmetic and copies ran while one was open for 4% of the time, Pallas kernels for 7%

profile of v7, /device:TPU:1, one launch (start us, length us, event | category | flops | bytes accessed | tf_op | source)
XLA Modules:
  0.0 245.5 jit_solution(17995883182906729046)
XLA Ops:
  0.6 0.0 copy-start
  0.6 0.0 copy-start.9
  0.7 3.1 %shard_map.112 = bf16[512,2,400]{2,1,0:T(2,128)(2,1)} custom-call(s32[1,512]{1,0:T(1,128)} %bitcast.41, bf16[400,512]{1,0:T(8,128)(2,1)} %bitcast.47), custom_call_target="tpu_custom_call" | custom-call | flops 419430400 | bytes 2097152 | tf_op jit(solution)/shard_map/pallas_call | solution.py:282
  3.8 0.0 copy-start.2
  3.8 24.3 %all-to-all-start = ((bf16[512,2,400]{2,1,0:T(2,128)(2,1)}), bf16[512,2,400]{2,1,0:T(2,128)(2,1)S(1)}, u32[]{:S(2)}, u32[]{:S(2)}) async-start(bf16[512,2,400]{2,1,0:T(2,128)(2,1)} %shard_map.112), calls=%async_computation | async-start | bytes 2097152 | tf_op jit(solution)/shard_map/all_to_all | solution.py:278
  28.1 0.0 copy-done.9
  28.1 0.0 copy-done
  28.1 0.2 convolution_convert_fusion
  28.3 23.6 %all_gather.3.far_cands.cands = bf16[1024,400]{1,0:T(8,128)(2,1)} all-gather(bf16[64,400]{1,0:T(8,128)(2,1)S(1)} %convolution_convert_fusion), channel_id=1, replica_groups=mesh['rel'=32,'ent'=16] {'ent'}, dimensions={0}, use_global_device_ids=true | all-gather | bytes 870400 | tf_op jit(solution)/shard_map/all_gather | solution.py:293
  51.9 33.9 %all-to-all-done.inputs = bf16[512,2,400]{2,1,0:T(2,128)(2,1)S(1)} async-done(((bf16[512,2,400]{2,1,0:T(2,128)(2,1)}), bf16[512,2,400]{2,1,0:T(2,128)(2,1)S(1)}, u32[]{:S(2)}, u32[]{:S(2)}) %all-to-all-start) | async-done | bytes 819232 | tf_op jit(solution)/shard_map/all_to_all | solution.py:278
  85.8 0.0 copy-start.1
  85.9 0.0 copy-done.2
  85.9 7.1 %shard_map.113 = bf16[512,2,400]{2,1,0:T(2,128)(2,1)} custom-call(bf16[512,2,400]{2,1,0:T(2,128)(2,1)S(1)} %all-to-all-done.inputs, bf16[400,1600]{1,0:T(8,128)(2,1)S(1)} %bitcast.36, bf16[400,1600]{1,0:T(8,128)(2,1)} %bitcast.45), custom_call_target="tpu_custom_call" | custom-call | flops 2621440000 | bytes 4198400 | tf_op jit(solution)/shard_map/pallas_call | solution.py:316
  93.0 0.0 copy-done.1
  93.0 9.7 %all-to-all-start.1 = ((bf16[512,2,400]{2,1,0:T(2,128)(2,1)}), bf16[512,2,400]{2,1,0:T(2,128)(2,1)S(1)}, u32[]{:S(2)}, u32[]{:S(2)}) async-start(bf16[512,2,400]{2,1,0:T(2,128)(2,1)} %shard_map.113), calls=%async_computation.1 | async-start | bytes 2097152 | tf_op jit(solution)/shard_map/all_to_all | solution.py:278
  102.7 0.0 copy-done.7
  102.7 0.9 copy.15.rel_col
  103.6 0.0 copy-done.8
  103.6 0.9 copy.16.query_col
  104.5 0.0 copy-done.6
  104.5 0.8 copy.17.answer
  105.3 3.6 %shard_map.115 = (bf16[1024,512]{1,0:T(8,128)(2,1)}, bf16[512,1024]{1,0:T(8,128)(2,1)}, bf16[512,512]{1,0:T(8,128)(2,1)}, bf16[256,512]{1,0:T(8,128)(2,1)}, bf16[512,256]{1,0:T(8,128)(2,1)}) custom-call(s32[1,512]{1,0:T(1,128)} %bitcast.42, s32[512,1]{1,0:T(8,128)} %copy.15.rel_col, s32[1,512]{1,0:T(1,128)} %query_row.1, s32[512,1]{1,0:T(8,128)} %copy.16.query_col), custom_call_target="tpu_custom_call" | custom-call | flops 5242880 | bytes 2097152 | tf_op jit(solution)/shard_map/pallas_call | solution.py:297
  108.9 7.6 %shard_map.114 = (bf16[1024,1600]{1,0:T(8,128)(2,1)}, bf16[400,1024]{1,0:T(8,128)(2,1)}) custom-call(bf16[512,2,400]{2,1,0:T(2,128)(2,1)} %copy-done.1, bf16[400,1600]{1,0:T(8,128)(2,1)} %bitcast.35), custom_call_target="tpu_custom_call" | custom-call | flops 1310720000 | bytes 3276800 | tf_op jit(solution)/shard_map/pallas_call | solution.py:332
  116.5 44.1 %all-to-all-done.1.far_returned = bf16[512,2,400]{2,1,0:T(2,128)(2,1)S(1)} async-done(((bf16[512,2,400]{2,1,0:T(2,128)(2,1)}), bf16[512,2,400]{2,1,0:T(2,128)(2,1)S(1)}, u32[]{:S(2)}, u32[]{:S(2)}) %all-to-all-start.1) | async-done | bytes 819232 | tf_op jit(solution)/shard_map/all_to_all | solution.py:278
  160.6 1.0 copy-done.5
  161.6 9.6 %shard_map.116 = (bf16[512,2,400]{2,1,0:T(2,128)(2,1)}, bf16[256,400]{1,0:T(8,128)(2,1)}) custom-call(s32[256,1]{1,0:T(8,128)} %copy.17.answer, bf16[512,2,400]{2,1,0:T(2,128)(2,1)} %copy-done.5, bf16[512,1024]{1,0:T(8,128)(2,1)} %get-tuple-element.22.far_place_t, bf16[400,400]{1,0:T(8,128)(2,1)} %far_weight.1, bf16[512,512]{1,0:T(8,128)(2,1)} %get-tuple-element.23.far_same, ...), custom_call_target="tpu_custom_call" | custom-call | flops 838860800 | bytes 3276800 | tf_op jit(solution)/shard_map/pallas_call | solution.py:344
  171.2 9.5 %all-to-all-start.2 = ((bf16[512,2,400]{2,1,0:T(2,128)(2,1)}), bf16[512,2,400]{2,1,0:T(2,128)(2,1)S(1)}, u32[]{:S(2)}, u32[]{:S(2)}) async-start(bf16[512,2,400]{2,1,0:T(2,128)(2,1)} %get-tuple-element.28), calls=%async_computation.2 | async-start | bytes 2097152 | tf_op jit(solution)/shard_map/all_to_all | solution.py:278
  180.8 4.1 %shard_map.118 = f32[1024,400]{1,0:T(8,128)} custom-call(bf16[1024,400]{1,0:T(8,128)(2,1)} %all_gather.3.far_cands.cands, bf16[256,400]{1,0:T(8,128)(2,1)} %get-tuple-element.27.query_b, s32[1,256]{1,0:T(1,128)} %bitcast.38), custom_call_target="tpu_custom_call" | custom-call | flops 419430400 | bytes 3276800 | tf_op jit(solution)/shard_map/pallas_call | solution.py:357
  184.9 1.8 fusion.6
  186.7 0.9 fusion
  187.6 3.3 %collective-permute-start = (bf16[2,2,2,64,400]{4,3,0,2,1:T(8,128)(2,1)}, bf16[2,2,2,64,400]{4,3,0,2,1:T(8,128)(2,1)}, u32[]{:S(2)}, u32[]{:S(2)}) collective-permute-start(bf16[2,2,2,64,400]{4,3,0,2,1:T(8,128)(2,1)} %fusion), channel_id=1, source_target_pairs={{0,1},{1,0},{2,3},{3,2},{4,5},{5,4},{6,7},{7,6},{8,9},{9,8},{10,11... | collective-permute-start | bytes 1228808 | tf_op jit(solution)/shard_map/ppermute | solution.py:262
  190.9 12.1 %collective-permute-done = bf16[2,2,2,64,400]{4,3,0,2,1:T(8,128)(2,1)} collective-permute-done((bf16[2,2,2,64,400]{4,3,0,2,1:T(8,128)(2,1)}, bf16[2,2,2,64,400]{4,3,0,2,1:T(8,128)(2,1)}, u32[]{:S(2)}, u32[]{:S(2)}) %collective-permute-start) | collective-permute-done | bytes 409632 | tf_op jit(solution)/shard_map/ppermute | solution.py:262
  203.1 1.3 bitcast_add_fusion
  204.4 0.0 copy-start.4
  204.4 1.0 copy-done.4
  205.4 6.6 %collective-permute-start.1 = (bf16[2,2,64,400]{3,2,0,1:T(8,128)(2,1)S(1)}, bf16[2,2,64,400]{3,2,0,1:T(8,128)(2,1)S(1)}, u32[]{:S(2)}, u32[]{:S(2)}) collective-permute-start(bf16[2,2,64,400]{3,2,0,1:T(8,128)(2,1)S(1)} %fusion.1), channel_id=1, source_target_pairs={{0,4},{1,5},{2,6},{3,7},{4,0},{5,1},{6,2},{7,3},{8,12},{9,13},{10,... | collective-permute-start | bytes 614408 | tf_op jit(solution)/shard_map/ppermute | solution.py:262
  212.1 6.8 %collective-permute-done.1 = bf16[2,2,64,400]{3,2,0,1:T(8,128)(2,1)S(1)} collective-permute-done((bf16[2,2,64,400]{3,2,0,1:T(8,128)(2,1)S(1)}, bf16[2,2,64,400]{3,2,0,1:T(8,128)(2,1)S(1)}, u32[]{:S(2)}, u32[]{:S(2)}) %collective-permute-start.1) | collective-permute-done | bytes 204832 | tf_op jit(solution)/shard_map/ppermute | solution.py:262
  218.9 1.3 bitcast_add_fusion.1
  220.3 0.0 copy-start.3
  220.3 5.3 %collective-permute-start.2 = (bf16[2,64,400]{2,1,0:T(8,128)(2,1)S(1)}, bf16[2,64,400]{2,1,0:T(8,128)(2,1)S(1)}, u32[]{:S(2)}, u32[]{:S(2)}) collective-permute-start(bf16[2,64,400]{2,1,0:T(8,128)(2,1)S(1)} %fusion.2), channel_id=1, source_target_pairs={{0,2},{1,3},{2,0},{3,1},{4,6},{5,7},{6,4},{7,5},{8,10},{9,11},{10,... | collective-permute-start | bytes 307208 | tf_op jit(solution)/shard_map/ppermute | solution.py:262
  225.6 2.8 %collective-permute-done.2 = bf16[2,64,400]{2,1,0:T(8,128)(2,1)S(1)} collective-permute-done((bf16[2,64,400]{2,1,0:T(8,128)(2,1)S(1)}, bf16[2,64,400]{2,1,0:T(8,128)(2,1)S(1)}, u32[]{:S(2)}, u32[]{:S(2)}) %collective-permute-start.2) | collective-permute-done | bytes 102432 | tf_op jit(solution)/shard_map/ppermute | solution.py:262
  228.5 5.3 %collective-permute-start.3 = (bf16[64,400]{1,0:T(8,128)(2,1)S(1)}, bf16[64,400]{1,0:T(8,128)(2,1)S(1)}, u32[]{:S(2)}, u32[]{:S(2)}) collective-permute-start(bf16[64,400]{1,0:T(8,128)(2,1)S(1)} %fusion.4), channel_id=1, source_target_pairs={{0,8},{1,9},{2,10},{3,11},{4,12},{5,13},{6,14},{7,15},{8,0},{9,1},... | collective-permute-start | bytes 153608 | tf_op jit(solution)/shard_map/ppermute | solution.py:262
  233.9 2.9 %shard_map.117 = f32[1,256]{1,0:T(1,128)} custom-call(bf16[1024,400]{1,0:T(8,128)(2,1)} %all_gather.3.far_cands.cands, bf16[256,400]{1,0:T(8,128)(2,1)} %get-tuple-element.27.query_b, s32[1,256]{1,0:T(1,128)} %bitcast.39), custom_call_target="tpu_custom_call" | custom-call | flops 209715200 | bytes 819200 | tf_op jit(solution)/shard_map/pallas_call | solution.py:363
  236.7 0.0 collective-permute-done.3
  236.7 0.7 fusion.3
  237.4 1.3 all-to-all-done.2.incoming
  238.7 0.0 copy-done.3
  238.7 6.8 %shard_map.119 = bf16[400,1600]{1,0:T(8,128)(2,1)} custom-call(bf16[512,2,400]{2,1,0:T(2,128)(2,1)S(1)} %all-to-all-done.2.incoming, bf16[400,1600]{1,0:T(8,128)(2,1)} %bitcast.46, bf16[1024,1600]{1,0:T(8,128)(2,1)} %get-tuple-element.29.slope, bf16[400,1024]{1,0:T(8,128)(2,1)S(1)} %copy-done.3), custom_call_target="tpu_custom_call" | custom-call | flops 2621440000 | bytes 6553600 | tf_op jit(solution)/shard_map/pallas_call | solution.py:371
  (9 shorter events, 0.2 us)
Async XLA Ops:
  0.6 27.5 %copy-start = (bf16[256,400]{0,1:T(8,128)(2,1)S(1)}, bf16[256,400]{0,1:T(8,128)(2,1)}, u32[]{:S(2)}) copy-start(bf16[256,400]{0,1:T(8,128)(2,1)} %param.14) | copy-start | bytes 614404
  0.6 27.4 %copy-start.9 = (s32[1,64]{1,0:T(1,128)S(1)}, s32[1,64]{1,0:T(1,128)}, u32[]{:S(2)}) copy-start(s32[1,64]{1,0:T(1,128)} %param.13) | copy-start | bytes 772
  3.8 82.1 %copy-start.2 = (bf16[1,400,1600]{2,1,0:T(8,128)(2,1)S(1)}, bf16[1,400,1600]{2,1,0:T(8,128)(2,1)}, u32[]{:S(2)}) copy-start(bf16[1,400,1600]{2,1,0:T(8,128)(2,1)} %param.15) | copy-start | bytes 3840004
  3.8 82.1 %all-to-all-start = ((bf16[512,2,400]{2,1,0:T(2,128)(2,1)}), bf16[512,2,400]{2,1,0:T(2,128)(2,1)S(1)}, u32[]{:S(2)}, u32[]{:S(2)}) async-start(bf16[512,2,400]{2,1,0:T(2,128)(2,1)} %shard_map.112), calls=%async_computation | async-start | bytes 2097152 | tf_op jit(solution)/shard_map/all_to_all | solution.py:278
  85.8 7.1 %copy-start.1 = (bf16[512,2,400]{2,1,0:T(2,128)(2,1)}, bf16[512,2,400]{2,1,0:T(2,128)(2,1)S(1)}, u32[]{:S(2)}) copy-start(bf16[512,2,400]{2,1,0:T(2,128)(2,1)S(1)} %all-to-all-done.inputs) | copy-start | bytes 2457604
  93.0 9.7 %copy-start.7 = (s32[512,1]{0,1:T(1,128)S(1)}, s32[512,1]{0,1:T(1,128)}, u32[]{:S(2)}) copy-start(s32[512,1]{0,1:T(1,128)} %param.10) | copy-start | bytes 6148
  93.0 10.6 %copy-start.8 = (s32[1,512]{1,0:T(1,128)S(1)}, s32[1,512]{1,0:T(1,128)}, u32[]{:S(2)}) copy-start(s32[1,512]{1,0:T(1,128)} %query_row.1) | copy-start | bytes 6148
  93.0 11.5 %copy-start.6 = (s32[256]{0:T(256)S(1)}, s32[256]{0:T(256)}, u32[]{:S(2)}) copy-start(s32[256]{0:T(256)} %param.12) | copy-start | bytes 3076
  93.0 67.6 %all-to-all-start.1 = ((bf16[512,2,400]{2,1,0:T(2,128)(2,1)}), bf16[512,2,400]{2,1,0:T(2,128)(2,1)S(1)}, u32[]{:S(2)}, u32[]{:S(2)}) async-start(bf16[512,2,400]{2,1,0:T(2,128)(2,1)} %shard_map.113), calls=%async_computation.1 | async-start | bytes 2097152 | tf_op jit(solution)/shard_map/all_to_all | solution.py:278
  160.6 1.0 copy-start.5
  171.2 67.5 %all-to-all-start.2 = ((bf16[512,2,400]{2,1,0:T(2,128)(2,1)}), bf16[512,2,400]{2,1,0:T(2,128)(2,1)S(1)}, u32[]{:S(2)}, u32[]{:S(2)}) async-start(bf16[512,2,400]{2,1,0:T(2,128)(2,1)} %get-tuple-element.28), calls=%async_computation.2 | async-start | bytes 2097152 | tf_op jit(solution)/shard_map/all_to_all | solution.py:278
  187.6 15.5 %collective-permute-start = (bf16[2,2,2,64,400]{4,3,0,2,1:T(8,128)(2,1)}, bf16[2,2,2,64,400]{4,3,0,2,1:T(8,128)(2,1)}, u32[]{:S(2)}, u32[]{:S(2)}) collective-permute-start(bf16[2,2,2,64,400]{4,3,0,2,1:T(8,128)(2,1)} %fusion), channel_id=1, source_target_pairs={{0,1},{1,0},{2,3},{3,2},{4,5},{5,4},{6,7},{7,6},{8,9},{9,8},{10,11... | collective-permute-start | bytes 1228808 | tf_op jit(solution)/shard_map/ppermute | solution.py:262
  204.4 1.0 copy-start.4
  205.4 13.5 %collective-permute-start.1 = (bf16[2,2,64,400]{3,2,0,1:T(8,128)(2,1)S(1)}, bf16[2,2,64,400]{3,2,0,1:T(8,128)(2,1)S(1)}, u32[]{:S(2)}, u32[]{:S(2)}) collective-permute-start(bf16[2,2,64,400]{3,2,0,1:T(8,128)(2,1)S(1)} %fusion.1), channel_id=1, source_target_pairs={{0,4},{1,5},{2,6},{3,7},{4,0},{5,1},{6,2},{7,3},{8,12},{9,13},{10,... | collective-permute-start | bytes 614408 | tf_op jit(solution)/shard_map/ppermute | solution.py:262
  220.3 18.4 %copy-start.3 = (bf16[400,1024]{1,0:T(8,128)(2,1)S(1)}, bf16[400,1024]{1,0:T(8,128)(2,1)}, u32[]{:S(2)}) copy-start(bf16[400,1024]{1,0:T(8,128)(2,1)} %get-tuple-element.30.inputs_t) | copy-start | bytes 2457604
  220.3 8.1 %collective-permute-start.2 = (bf16[2,64,400]{2,1,0:T(8,128)(2,1)S(1)}, bf16[2,64,400]{2,1,0:T(8,128)(2,1)S(1)}, u32[]{:S(2)}, u32[]{:S(2)}) collective-permute-start(bf16[2,64,400]{2,1,0:T(8,128)(2,1)S(1)} %fusion.2), channel_id=1, source_target_pairs={{0,2},{1,3},{2,0},{3,1},{4,6},{5,7},{6,4},{7,5},{8,10},{9,11},{10,... | collective-permute-start | bytes 307208 | tf_op jit(solution)/shard_map/ppermute | solution.py:262
  228.5 8.2 %collective-permute-start.3 = (bf16[64,400]{1,0:T(8,128)(2,1)S(1)}, bf16[64,400]{1,0:T(8,128)(2,1)S(1)}, u32[]{:S(2)}, u32[]{:S(2)}) collective-permute-start(bf16[64,400]{1,0:T(8,128)(2,1)S(1)} %fusion.4), channel_id=1, source_target_pairs={{0,8},{1,9},{2,10},{3,11},{4,12},{5,13},{6,14},{7,15},{8,0},{9,1},... | collective-permute-start | bytes 153608 | tf_op jit(solution)/shard_map/ppermute | solution.py:262
